TPU v7x, 512 devices: a whole 4x4x16 slice. The times are simulated.
512 devices in a mesh: batch: 8 (over x, y_lo), ctx: 64 (over y_hi, z, core).
Axes of the slice: x: 4, y: 4 (y_hi: 2, y_lo: 2; y = y_hi * 2 + y_lo), z: 16, core: 2. Of those that a mesh axis runs over, the one named last changes fastest.
Arguments:
- queries: bfloat16 [8, 16384, 768], P('batch', 'ctx'), may hold values from -8 to 8
- keys: bfloat16 [8, 16384, 768], P('batch', 'ctx'), may hold values from -8 to 8
- values: bfloat16 [8, 16384, 768], P('batch', 'ctx'), may hold values from -6 to 6
- cotangent: bfloat16 [8, 16384, 768], P('batch', 'ctx'), may hold values from -6 to 6
- out_weight: bfloat16 [768, 768], replicated, may hold values from -0.21875 to 0.21875
- offsets: int32 [16], replicated, may hold values from 0 to 15, each once
Outputs:
- grad_queries: bfloat16 [8, 16384, 768], P('batch', 'ctx')
- grad_keys: bfloat16 [8, 16384, 768], P('batch', 'ctx')
- grad_values: bfloat16 [8, 16384, 768], P('batch', 'ctx')
- grad_out_weight: float32 [768, 768], P('ctx', 'batch')
All inputs are finite; a program needn't handle non-finite values.
Results may differ from a plain program's by a relative error of at most 0.035.
Values may be sent and summed in bfloat16 or wider, within the bound.
No kernel may reach another device: no remote copies, remote signals or barrier semaphores. Data moves between devices by JAX's collectives and lax.ppermute only.
A program may use at most 64 MiB of HBM per device.

v0:
```python
import math

import jax
import jax.numpy as jnp
from jax import lax
from jax.sharding import PartitionSpec as P

LEVELS = 4


def partner_2(block, axis, bit):
    count = lax.axis_size(axis)
    route = []
    for low in range(count):
        high = low | 1 << bit
        if high != low and high < count:
            route += [(low, high), (high, low)]
    return lax.ppermute(block, axis, route)


def gather_class(own_rows, low_bit, high_bit, position, sender):
    gathered = own_rows
    for bit_index in range(low_bit, high_bit):
        partner = sender(gathered, bit_index)
        upper_half = position // (1 << bit_index) % 2 == 1
        gathered = jnp.where(
            upper_half,
            jnp.concatenate([partner, gathered], 0),
            jnp.concatenate([gathered, partner], 0),
        )
    return gathered


def return_class(partials, low_bit, high_bit, position, sender):
    summed = partials
    for bit_index in reversed(range(low_bit, high_bit)):
        half_rows = summed.shape[0] // 2
        upper_half = position // (1 << bit_index) % 2 == 1
        kept_half = jnp.where(upper_half, summed[half_rows:], summed[:half_rows])
        given_half = jnp.where(upper_half, summed[:half_rows], summed[half_rows:])
        summed = kept_half + sender(given_half, bit_index)
    return summed


def first_pass(query_slots, grad_slots, all_keys, all_values, softmax_scale):
    scores = (
        jnp.einsum("qhd,khd->hqk", query_slots, all_keys, preferred_element_type=jnp.float32)
        * softmax_scale
    )
    top_score = jnp.max(scores, axis=-1, keepdims=True)
    log_total = top_score + jnp.log(jnp.sum(jnp.exp(scores - top_score), axis=-1, keepdims=True))
    weights = jnp.exp(scores - log_total)
    weights_low = weights.astype(jnp.bfloat16)
    attended = jnp.einsum(
        "hqk,khd->qhd", weights_low, all_values, preferred_element_type=jnp.float32
    ).astype(jnp.bfloat16)
    row_dots = jnp.sum(grad_slots.astype(jnp.float32) * attended.astype(jnp.float32), axis=-1)
    grad_weights = jnp.einsum(
        "qhd,khd->hqk", grad_slots, all_values, preferred_element_type=jnp.float32
    )
    grad_scores = (weights * (grad_weights - jnp.transpose(row_dots)[:, :, None])).astype(
        jnp.bfloat16
    )
    grad_query = (
        jnp.einsum("hqk,khd->qhd", grad_scores, all_keys, preferred_element_type=jnp.float32)
        * softmax_scale
    )
    return (attended, log_total[:, :, 0], row_dots, grad_query, grad_scores, weights_low)


def local(queries, keys, values, cotangent, out_weight, offsets):
    query_rows = queries[0]
    key_rows = keys[0]
    value_rows = values[0]
    grad_rows = cotangent[0]
    row_count, model_width = query_rows.shape
    head_count = offsets.shape[0]
    head_width = model_width // head_count
    group_heads = head_count // LEVELS
    group_width = group_heads * head_width
    position = lax.axis_index("ctx")
    softmax_scale = 1.0 / math.sqrt(head_width)
    grad_attended = lax.dot_general(
        grad_rows, out_weight, (((1,), (1,)), ((), ())), preferred_element_type=jnp.float32
    ).astype(jnp.bfloat16)

    def send_pairs(message, bit_index):
        return partner_2(message, "ctx", bit_index)

    attended_parts = []
    query_parts = []
    key_parts = []
    value_parts = []
    for level_index in range(LEVELS):
        dilation = 2**level_index
        slot_rows = row_count // dilation
        high_bit = dilation.bit_length() - 1
        first_head = level_index * group_heads
        head_offsets = offsets[first_head : first_head + group_heads] % dilation
        chosen = jnp.arange(dilation)[:, None] == head_offsets[None, :]
        mask_shape = chosen[None, :, :, None]
        column_start = first_head * head_width

        def select(matrix):
            window_part = matrix[:, column_start : column_start + group_width].reshape(
                slot_rows, dilation, group_heads, head_width
            )
            return jnp.sum(
                jnp.where(mask_shape, window_part, jnp.zeros((), window_part.dtype)), axis=1
            )

        def spread(slot_values):
            rows_form = slot_values.reshape(slot_rows, 1, group_heads, head_width)
            placed = jnp.where(mask_shape, rows_form, jnp.zeros((), slot_values.dtype))
            return placed.reshape(row_count, group_width)

        query_slots = select(query_rows)
        key_slots = select(key_rows)
        value_slots = select(value_rows)
        grad_slots = select(grad_attended)
        own_pairs = jnp.concatenate(
            [
                key_slots.reshape(slot_rows, group_width),
                value_slots.reshape(slot_rows, group_width),
            ],
            1,
        )
        all_pairs = gather_class(own_pairs, 0, high_bit, position, send_pairs)
        key_total = all_pairs.shape[0]
        all_keys = all_pairs[:, :group_width].reshape(key_total, group_heads, head_width)
        all_values = all_pairs[:, group_width:].reshape(key_total, group_heads, head_width)
        attended, log_total, row_dots, grad_query, grad_scores, weights_low = first_pass(
            query_slots, grad_slots, all_keys, all_values, softmax_scale
        )

        def send_partials(message, bit_index):
            return partner_2(message, "ctx", bit_index)

        key_part = (
            jnp.einsum("hqk,qhd->khd", grad_scores, query_slots, preferred_element_type=jnp.float32)
            * softmax_scale
        )
        value_part = jnp.einsum(
            "hqk,qhd->khd", weights_low, grad_slots, preferred_element_type=jnp.float32
        )
        partials = jnp.concatenate(
            [key_part.reshape(key_total, group_width), value_part.reshape(key_total, group_width)],
            1,
        )
        own_sums = return_class(partials, 0, high_bit, position, send_partials)
        key_grad = own_sums[:, :group_width]
        value_grad = own_sums[:, group_width:]
        attended_parts.append(spread(attended))
        query_parts.append(spread(grad_query))
        key_parts.append(spread(key_grad.reshape(slot_rows, group_heads, head_width)))
        value_parts.append(spread(value_grad.reshape(slot_rows, group_heads, head_width)))
    attended_rows = jnp.concatenate(attended_parts, 1)
    grad_q = jnp.concatenate(query_parts, 1).astype(jnp.bfloat16)[None]
    grad_k = jnp.concatenate(key_parts, 1).astype(jnp.bfloat16)[None]
    grad_v = jnp.concatenate(value_parts, 1).astype(jnp.bfloat16)[None]
    partial_rows = lax.psum_scatter(
        lax.dot_general(
            attended_rows, grad_rows, (((0,), (0,)), ((), ())), preferred_element_type=jnp.float32
        ),
        "ctx",
        scatter_dimension=0,
        tiled=True,
    )
    weight_grad = lax.psum_scatter(partial_rows, "batch", scatter_dimension=1, tiled=True)
    return (grad_q, grad_k, grad_v, weight_grad)


def solution(mesh):
    return jax.shard_map(
        local,
        mesh=mesh,
        in_specs=(
            P("batch", "ctx", None),
            P("batch", "ctx", None),
            P("batch", "ctx", None),
            P("batch", "ctx", None),
            P(),
            P(),
        ),
        out_specs=(
            P("batch", "ctx", None),
            P("batch", "ctx", None),
            P("batch", "ctx", None),
            P("ctx", "batch"),
        ),
        check_vma=False,
    )
```

profile of v0, /device:TPU:1, one launch (start us, length us, event | category | flops | bytes accessed | tf_op | source)
XLA Modules:
  0.0 412.6 jit_solution(14297808512280493899)
XLA Ops:
  8.5 1.5 convolution_convert_fusion
  12.7 1.1 reshape.599
  14.6 1.1 reshape.601
  15.7 1.5 select_reduce_fusion
  18.2 8.8 %collective-permute-start.3 = (bf16[32,384]{0,1:T(8,128)(2,1)}, bf16[32,384]{0,1:T(8,128)(2,1)}, u32[]{:S(2)}, u32[]{:S(2)}) collective-permute-start(bf16[32,384]{0,1:T(8,128)(2,1)} %copy.129), channel_id=1, source_target_pairs={{0,1},{1,0},{2,3},{3,2},{4,5},{5,4},{6,7},{7,6},{8,9},{9,8},{10,11... | collective-permute-start | bytes 73736 | tf_op jit(solution)/shard_map/ppermute | solution.py:18
  27.7 1.5 select_reduce_fusion.5
  30.1 1.9 collective-permute-start.1
  32.7 1.0 select_reduce_fusion.9
  34.7 2.4 collective-permute-start
  41.4 1.7 copy.156
  43.1 1.2 maximum_select_fusion.4
  44.2 1.9 collective-permute-start.4
  46.2 1.7 maximum_select_fusion.3
  47.9 3.3 collective-permute-start.2
  52.1 1.9 collective-permute-start.5
  54.0 1.0 maximum_select_fusion
  59.2 2.5 collective-permute-start.6
  66.4 1.5 copy.128
  67.9 1.5 copy.154
  70.2 1.9 collective-permute-start.7
  72.1 1.1 maximum_select_fusion.2
  75.4 1.1 multiply_reduce_fusion.3
  79.0 4.7 %collective-permute-start.9 = (f32[128,384]{0,1:T(8,128)}, f32[128,384]{0,1:T(8,128)}, u32[]{:S(2)}, u32[]{:S(2)}) collective-permute-start(f32[128,384]{0,1:T(8,128)} %broadcast_select_fusion.3), channel_id=1, source_target_pairs={{0,4},{4,0},{1,5},{5,1},{2,6},{6,2},{3,7},{7,3},{8,12},{12,8},{9,1... | collective-permute-start | bytes 589832 | tf_op jit(solution)/shard_map/ppermute | solution.py:18
  87.1 2.5 broadcast_select_fusion.2
  89.6 1.8 select_n.416
  92.5 2.2 collective-permute-start.8
  94.7 1.1 select_add_fusion.2
  96.6 3.6 collective-permute-start.10
  101.8 3.8 collective-permute-done.10
  105.7 1.0 select_add_fusion.1
  107.5 2.6 collective-permute-start.11
  110.2 2.2 broadcast_select_fusion.1
  112.4 1.8 select_n.418
  114.2 1.0 select_add_fusion
  116.7 2.0 broadcast_select_fusion
  119.6 3.2 fusion.19
  122.7 148.2 %fusion = f32[16,768]{1,0:T(8,128)} fusion(f32[768,768]{1,0:T(8,128)} %fusion.19), kind=kCustom, calls=%all-reduce-scatter | all-reduce-scatter fusion | flops 786433 | bytes 2410496
  271.8 1.4 collective-permute-start.27
  274.2 18.8 %collective-permute-start.26 = (f32[16,768]{1,0:T(8,128)}, f32[16,768]{1,0:T(8,128)S(1)}, u32[]{:S(2)}, u32[]{:S(2)}) collective-permute-start(f32[16,768]{1,0:T(8,128)} %fusion), channel_id=1, source_target_pairs={{0,15},{1,16},{2,17},{3,18},{4,19},{5,20},{6,21},{7,22},{8,23},{9,... | collective-permute-start | bytes 147464
  293.0 1.3 collective-permute-start.25
  294.3 1.3 collective-permute-start.24
  295.6 1.3 collective-permute-start.23
  296.9 1.3 collective-permute-start.22
  298.2 1.2 fusion.7
  299.4 4.5 %collective-permute-done.26 = f32[16,768]{1,0:T(8,128)S(1)} collective-permute-done((f32[16,768]{1,0:T(8,128)}, f32[16,768]{1,0:T(8,128)S(1)}, u32[]{:S(2)}, u32[]{:S(2)}) %collective-permute-start.26) | collective-permute-done | bytes 49184
  303.9 7.6 %collective-permute-start.21 = (f32[16,768]{1,0:T(8,128)}, f32[16,768]{1,0:T(8,128)}, u32[]{:S(2)}, u32[]{:S(2)}) collective-permute-start(f32[16,768]{1,0:T(8,128)} %fusion), channel_id=1, source_target_pairs={{0,10},{1,11},{2,12},{3,13},{4,14},{5,15},{6,16},{7,17},{8,18},{9,... | collective-permute-start | bytes 147464
  311.5 2.2 collective-permute-start.20
  313.7 5.4 %collective-permute-start.19 = (f32[16,768]{1,0:T(8,128)}, f32[16,768]{1,0:T(8,128)}, u32[]{:S(2)}, u32[]{:S(2)}) collective-permute-start(f32[16,768]{1,0:T(8,128)} %fusion), channel_id=1, source_target_pairs={{0,8},{1,9},{2,10},{3,11},{4,12},{5,13},{6,14},{7,15},{8,16},{9,17... | collective-permute-start | bytes 147464
  319.1 10.5 %collective-permute-start.18 = (f32[16,768]{1,0:T(8,128)}, f32[16,768]{1,0:T(8,128)}, u32[]{:S(2)}, u32[]{:S(2)}) collective-permute-start(f32[16,768]{1,0:T(8,128)} %fusion), channel_id=1, source_target_pairs={{0,7},{1,8},{2,9},{3,10},{4,11},{5,12},{6,13},{7,14},{8,15},{9,16}... | collective-permute-start | bytes 147464
  329.7 1.9 collective-permute-start.17
  331.8 1.6 copy.152
  333.7 1.3 dynamic-slice.4
  335.6 1.2 concatenate.118
  336.8 1.2 concatenate.136
  338.0 1.8 concatenate.143
  340.8 1.4 collective-permute-start.16
  342.2 4.4 %collective-permute-start.15 = (f32[16,768]{1,0:T(8,128)}, f32[16,768]{1,0:T(8,128)S(1)}, u32[]{:S(2)}, u32[]{:S(2)}) collective-permute-start(f32[16,768]{1,0:T(8,128)} %fusion), channel_id=1, source_target_pairs={{0,4},{1,5},{2,6},{3,7},{4,8},{5,9},{6,10},{7,11},{8,12},{9,13},{1... | collective-permute-start | bytes 147464
  346.6 3.9 collective-permute-start.14
  350.6 1.9 collective-permute-start.13
  352.5 2.8 collective-permute-start.12
  355.2 1.2 pad_maximum_fusion
  356.7 10.3 %concatenate.148 = f32[268,768]{1,0:T(8,128)S(1)} concatenate(f32[12,768]{1,0:T(8,128)} %copy-done.36, f32[16,768]{1,0:T(8,128)} %copy-done.37, f32[16,768]{1,0:T(8,128)} %copy-done.38, f32[16,768]{1,0:T(8,128)} %copy-done.39, f32[16,768]{1,0:T(8,128)} %copy-done.40, f32[16,768]{1,0:T(8,128)S(1)} %copy-done.42, f32[16,768]{1,0:T(8,128)} %collective-permute-done.21, ...), dimensions={0} | concatenate | bytes 1646592
  368.9 35.4 %reduce-scatter.6.cloned.1.call-done = f32[96,12]{1,0:T(8,128)} async-done(((f32[768,12]{1,0:T(8,128)}), f32[96,12]{1,0:T(8,128)}) %reduce-scatter.6.cloned.1.call-update) | async-done | bytes 4624
  404.3 1.5 copy.163
  (220 shorter events, 43.0 us)
Async XLA Ops:
  7.2 3.8 copy-start.16
  7.2 397.1 %reduce-scatter.6.cloned.1.call-start = ((), (), s32[]{:S(2)}) async-start(), calls=%async_computation.1 | async-start | bytes 442368
  8.5 3.4 copy-start.17
  10.0 3.7 copy-start.18
  14.6 12.9 %copy-start.22 = (bf16[256,192]{1,0:T(8,128)(2,1)S(1)}, bf16[256,192]{1,0:T(8,128)(2,1)}, u32[]{:S(2)}) copy-start(bf16[256,192]{1,0:T(8,128)(2,1)} %get-tuple-element.22) | copy-start | bytes 294916
  18.2 24.9 %collective-permute-start.3 = (bf16[32,384]{0,1:T(8,128)(2,1)}, bf16[32,384]{0,1:T(8,128)(2,1)}, u32[]{:S(2)}, u32[]{:S(2)}) collective-permute-start(bf16[32,384]{0,1:T(8,128)(2,1)} %copy.129), channel_id=1, source_target_pairs={{0,1},{1,0},{2,3},{3,2},{4,5},{5,4},{6,7},{7,6},{8,9},{9,8},{10,11... | collective-permute-start | bytes 73736 | tf_op jit(solution)/shard_map/ppermute | solution.py:18
  29.2 7.8 %copy-start.24 = (bf16[256,192]{1,0:T(8,128)(2,1)S(1)}, bf16[256,192]{1,0:T(8,128)(2,1)}, u32[]{:S(2)}) copy-start(bf16[256,192]{1,0:T(8,128)(2,1)} %get-tuple-element.24) | copy-start | bytes 294916
  29.2 8.0 %copy-start.25 = (bf16[256,192]{1,0:T(8,128)(2,1)S(1)}, bf16[256,192]{1,0:T(8,128)(2,1)}, u32[]{:S(2)}) copy-start(bf16[256,192]{1,0:T(8,128)(2,1)} %get-tuple-element.16) | copy-start | bytes 294916
  29.2 8.1 %copy-start.26 = (bf16[256,192]{1,0:T(8,128)(2,1)S(1)}, bf16[256,192]{1,0:T(8,128)(2,1)}, u32[]{:S(2)}) copy-start(bf16[256,192]{1,0:T(8,128)(2,1)} %get-tuple-element.28) | copy-start | bytes 294916
  29.3 8.1 %copy-start.27 = (bf16[256,192]{1,0:T(8,128)(2,1)S(1)}, bf16[256,192]{1,0:T(8,128)(2,1)}, u32[]{:S(2)}) copy-start(bf16[256,192]{1,0:T(8,128)(2,1)} %get-tuple-element.20) | copy-start | bytes 294916
  30.1 16.1 %collective-permute-start.1 = (bf16[64,384]{0,1:T(8,128)(2,1)}, bf16[64,384]{0,1:T(8,128)(2,1)}, u32[]{:S(2)}, u32[]{:S(2)}) collective-permute-start(bf16[64,384]{0,1:T(8,128)(2,1)} %pad_maximum_fusion.7), channel_id=1, source_target_pairs={{0,1},{1,0},{2,3},{3,2},{4,5},{5,4},{6,7},{7,6},{8,9},{9,8},{10,11... | collective-permute-start | bytes 147464 | tf_op jit(solution)/shard_map/ppermute | solution.py:18
  34.0 3.4 copy-start.28
  34.7 19.3 %collective-permute-start = (bf16[128,384]{0,1:T(8,128)(2,1)}, bf16[128,384]{0,1:T(8,128)(2,1)}, u32[]{:S(2)}, u32[]{:S(2)}) collective-permute-start(bf16[128,384]{0,1:T(8,128)(2,1)} %pad_maximum_fusion.6), channel_id=1, source_target_pairs={{0,1},{1,0},{2,3},{3,2},{4,5},{5,4},{6,7},{7,6},{8,9},{9,8},{10,11... | collective-permute-start | bytes 294920 | tf_op jit(solution)/shard_map/ppermute | solution.py:18
  38.1 15.9 %copy-start.29 = (bf16[128,4,48]{0,2,1:T(8,128)(2,1)S(1)}, bf16[128,4,48]{0,2,1:T(8,128)(2,1)}, u32[]{:S(2)}) copy-start(bf16[128,4,48]{0,2,1:T(8,128)(2,1)} %copy-done.28) | copy-start | bytes 147460
  41.3 14.4 %copy-start.31 = (bf16[128,4,48]{0,2,1:T(8,128)(2,1)}, bf16[128,4,48]{0,2,1:T(8,128)(2,1)S(1)}, u32[]{:S(2)}) copy-start(bf16[128,4,48]{0,2,1:T(8,128)(2,1)S(1)} %copy.119) | copy-start | bytes 147460
  44.2 7.0 %collective-permute-start.4 = (bf16[64,384]{0,1:T(8,128)(2,1)S(1)}, bf16[64,384]{0,1:T(8,128)(2,1)S(1)}, u32[]{:S(2)}, u32[]{:S(2)}) collective-permute-start(bf16[64,384]{0,1:T(8,128)(2,1)S(1)} %maximum_select_fusion.4), channel_id=1, source_target_pairs={{0,2},{2,0},{1,3},{3,1},{4,6},{6,4},{5,7},{7,5},{8,10},{10,8},{9,1... | collective-permute-start | bytes 147464 | tf_op jit(solution)/shard_map/ppermute | solution.py:18
  47.9 13.8 %collective-permute-start.2 = (bf16[128,384]{0,1:T(8,128)(2,1)}, bf16[128,384]{0,1:T(8,128)(2,1)S(1)}, u32[]{:S(2)}, u32[]{:S(2)}) collective-permute-start(bf16[128,384]{0,1:T(8,128)(2,1)} %maximum_select_fusion.3), channel_id=1, source_target_pairs={{0,2},{2,0},{1,3},{3,1},{4,6},{6,4},{5,7},{7,5},{8,10},{10,8},{9,1... | collective-permute-start | bytes 294920 | tf_op jit(solution)/shard_map/ppermute | solution.py:18
  52.1 20.0 %collective-permute-start.5 = (bf16[128,384]{0,1:T(8,128)(2,1)}, bf16[128,384]{0,1:T(8,128)(2,1)}, u32[]{:S(2)}, u32[]{:S(2)}) collective-permute-start(bf16[128,384]{0,1:T(8,128)(2,1)} %maximum_select_fusion.5), channel_id=1, source_target_pairs={{0,4},{4,0},{1,5},{5,1},{2,6},{6,2},{3,7},{7,3},{8,12},{12,8},{9,1... | collective-permute-start | bytes 294920 | tf_op jit(solution)/shard_map/ppermute | solution.py:18
  56.0 6.8 %copy-start.30 = (bf16[64,4,48]{0,2,1:T(8,128)(2,1)S(1)}, bf16[64,4,48]{0,2,1:T(8,128)(2,1)}, u32[]{:S(2)}) copy-start(bf16[64,4,48]{0,2,1:T(8,128)(2,1)} %copy.125) | copy-start | bytes 73732
  59.2 24.5 %collective-permute-start.6 = (f32[128,384]{0,1:T(8,128)}, f32[128,384]{0,1:T(8,128)}, u32[]{:S(2)}, u32[]{:S(2)}) collective-permute-start(f32[128,384]{0,1:T(8,128)} %broadcast_select_fusion.5), channel_id=1, source_target_pairs={{0,1},{1,0},{2,3},{3,2},{4,5},{5,4},{6,7},{7,6},{8,9},{9,8},{10,11... | collective-permute-start | bytes 589832 | tf_op jit(solution)/shard_map/ppermute | solution.py:18
  69.5 7.0 %copy-start.23 = (bf16[32,4,48]{2,1,0:T(4,128)(2,1)S(1)}, bf16[32,4,48]{2,1,0:T(4,128)(2,1)}, u32[]{:S(2)}) copy-start(bf16[32,4,48]{2,1,0:T(4,128)(2,1)} %get-tuple-element.4) | copy-start | bytes 36868
  69.5 7.2 %copy-start.33 = (bf16[32,4,48]{2,1,0:T(4,128)(2,1)S(1)}, bf16[32,4,48]{2,1,0:T(4,128)(2,1)}, u32[]{:S(2)}) copy-start(bf16[32,4,48]{2,1,0:T(4,128)(2,1)} %get-tuple-element.6) | copy-start | bytes 36868
  70.2 21.2 %collective-permute-start.7 = (f32[128,384]{0,1:T(8,128)}, f32[128,384]{0,1:T(8,128)}, u32[]{:S(2)}, u32[]{:S(2)}) collective-permute-start(f32[128,384]{0,1:T(8,128)} %broadcast_select_fusion.4), channel_id=1, source_target_pairs={{0,2},{2,0},{1,3},{3,1},{4,6},{6,4},{5,7},{7,5},{8,10},{10,8},{9,1... | collective-permute-start | bytes 589832 | tf_op jit(solution)/shard_map/ppermute | solution.py:18
  79.0 15.7 %collective-permute-start.9 = (f32[128,384]{0,1:T(8,128)}, f32[128,384]{0,1:T(8,128)}, u32[]{:S(2)}, u32[]{:S(2)}) collective-permute-start(f32[128,384]{0,1:T(8,128)} %broadcast_select_fusion.3), channel_id=1, source_target_pairs={{0,4},{4,0},{1,5},{5,1},{2,6},{6,2},{3,7},{7,3},{8,12},{12,8},{9,1... | collective-permute-start | bytes 589832 | tf_op jit(solution)/shard_map/ppermute | solution.py:18
  84.7 10.0 %copy-start.2 = (f32[4,48,256]{2,1,0:T(8,128)S(1)}, f32[4,48,256]{2,1,0:T(8,128)}, u32[]{:S(2)}) copy-start(f32[4,48,256]{2,1,0:T(8,128)} %copy-done.1) | copy-start | bytes 589828
  92.3 17.8 %copy-start.35 = (bf16[64,4,48]{2,1,0:T(4,128)(2,1)S(1)}, bf16[64,4,48]{2,1,0:T(4,128)(2,1)}, u32[]{:S(2)}) copy-start(bf16[64,4,48]{2,1,0:T(4,128)(2,1)} %copy.128) | copy-start | bytes 73732
  92.5 7.7 %collective-permute-start.8 = (f32[64,384]{0,1:T(8,128)S(1)}, f32[64,384]{0,1:T(8,128)S(1)}, u32[]{:S(2)}, u32[]{:S(2)}) collective-permute-start(f32[64,384]{0,1:T(8,128)S(1)} %slice_select_fusion.2), channel_id=1, source_target_pairs={{0,1},{1,0},{2,3},{3,2},{4,5},{5,4},{6,7},{7,6},{8,9},{9,8},{10,11... | collective-permute-start | bytes 294920 | tf_op jit(solution)/shard_map/ppermute | solution.py:18
  96.6 9.1 %collective-permute-start.10 = (f32[64,384]{0,1:T(8,128)}, f32[64,384]{0,1:T(8,128)}, u32[]{:S(2)}, u32[]{:S(2)}) collective-permute-start(f32[64,384]{0,1:T(8,128)} %slice_select_fusion.1), channel_id=1, source_target_pairs={{0,2},{2,0},{1,3},{3,1},{4,6},{6,4},{5,7},{7,5},{8,10},{10,8},{9,1... | collective-permute-start | bytes 294920 | tf_op jit(solution)/shard_map/ppermute | solution.py:18
  106.7 12.8 %copy-start.4 = (bf16[1,256,768]{2,1,0:T(8,128)(2,1)S(1)}, bf16[1,256,768]{2,1,0:T(8,128)(2,1)}, u32[]{:S(2)}) copy-start(bf16[1,256,768]{2,1,0:T(8,128)(2,1)} %param.9) | copy-start | bytes 1179652
  106.7 12.8 %copy-start.19 = (bf16[256,192]{1,0:T(8,128)(2,1)S(1)}, bf16[256,192]{1,0:T(8,128)(2,1)}, u32[]{:S(2)}) copy-start(bf16[256,192]{1,0:T(8,128)(2,1)} %copy.156) | copy-start | bytes 294916
  107.5 6.7 %collective-permute-start.11 = (f32[32,384]{0,1:T(8,128)}, f32[32,384]{0,1:T(8,128)}, u32[]{:S(2)}, u32[]{:S(2)}) collective-permute-start(f32[32,384]{0,1:T(8,128)} %slice_select_fusion), channel_id=1, source_target_pairs={{0,1},{1,0},{2,3},{3,2},{4,5},{5,4},{6,7},{7,6},{8,9},{9,8},{10,11... | collective-permute-start | bytes 147464 | tf_op jit(solution)/shard_map/ppermute | solution.py:18
  119.6 153.7 %copy-start.6 = (bf16[256,192]{0,1:T(8,128)(2,1)S(1)}, bf16[256,192]{0,1:T(8,128)(2,1)}, u32[]{:S(2)}) copy-start(bf16[256,192]{0,1:T(8,128)(2,1)} %copy-done.5) | copy-start | bytes 294916
  122.7 208.8 %copy-start.14 = (bf16[256,192]{0,1:T(8,128)(2,1)S(1)}, bf16[256,192]{0,1:T(8,128)(2,1)}, u32[]{:S(2)}) copy-start(bf16[256,192]{0,1:T(8,128)(2,1)} %copy-done.13) | copy-start | bytes 294916
  271.0 68.8 %copy-start.9 = (bf16[64,4,4,48]{3,2,1,0:T(4,128)(2,1)S(1)}, bf16[64,4,4,48]{3,2,1,0:T(4,128)(2,1)}, u32[]{:S(2)}) copy-start(bf16[64,4,4,48]{3,2,1,0:T(4,128)(2,1)} %get-tuple-element.53) | copy-start | bytes 294916
  271.8 68.2 %copy-start.8 = (bf16[64,4,4,48]{3,2,1,0:T(4,128)(2,1)S(1)}, bf16[64,4,4,48]{3,2,1,0:T(4,128)(2,1)}, u32[]{:S(2)}) copy-start(bf16[64,4,4,48]{3,2,1,0:T(4,128)(2,1)} %get-tuple-element.54) | copy-start | bytes 294916
  271.8 25.1 %collective-permute-start.27 = (f32[12,768]{1,0:T(8,128)S(1)}, f32[12,768]{1,0:T(8,128)S(1)}, u32[]{:S(2)}, u32[]{:S(2)}) collective-permute-start(f32[12,768]{1,0:T(8,128)S(1)} %slice.225), channel_id=1, source_target_pairs={{0,16},{1,17},{2,18},{3,19},{4,20},{5,21},{6,22},{7,23},{8,24},{9,... | collective-permute-start | bytes 110600
  274.2 66.0 %copy-start.7 = (bf16[64,4,4,48]{3,2,1,0:T(4,128)(2,1)S(1)}, bf16[64,4,4,48]{3,2,1,0:T(4,128)(2,1)}, u32[]{:S(2)}) copy-start(bf16[64,4,4,48]{3,2,1,0:T(4,128)(2,1)} %get-tuple-element.55) | copy-start | bytes 294916
  274.2 66.2 %copy-start.12 = (bf16[32,8,4,48]{3,2,1,0:T(4,128)(2,1)S(1)}, bf16[32,8,4,48]{3,2,1,0:T(4,128)(2,1)}, u32[]{:S(2)}) copy-start(bf16[32,8,4,48]{3,2,1,0:T(4,128)(2,1)} %get-tuple-element.45) | copy-start | bytes 294916
  274.2 66.4 %copy-start.11 = (bf16[32,8,4,48]{3,2,1,0:T(4,128)(2,1)S(1)}, bf16[32,8,4,48]{3,2,1,0:T(4,128)(2,1)}, u32[]{:S(2)}) copy-start(bf16[32,8,4,48]{3,2,1,0:T(4,128)(2,1)} %get-tuple-element.46) | copy-start | bytes 294916
  274.2 29.7 %collective-permute-start.26 = (f32[16,768]{1,0:T(8,128)}, f32[16,768]{1,0:T(8,128)S(1)}, u32[]{:S(2)}, u32[]{:S(2)}) collective-permute-start(f32[16,768]{1,0:T(8,128)} %fusion), channel_id=1, source_target_pairs={{0,15},{1,16},{2,17},{3,18},{4,19},{5,20},{6,21},{7,22},{8,23},{9,... | collective-permute-start | bytes 147464
  293.0 18.5 %collective-permute-start.25 = (f32[16,768]{1,0:T(8,128)}, f32[16,768]{1,0:T(8,128)S(1)}, u32[]{:S(2)}, u32[]{:S(2)}) collective-permute-start(f32[16,768]{1,0:T(8,128)} %fusion), channel_id=1, source_target_pairs={{0,14},{1,15},{2,16},{3,17},{4,18},{5,19},{6,20},{7,21},{8,22},{9,... | collective-permute-start | bytes 147464
  294.3 19.4 %collective-permute-start.24 = (f32[16,768]{1,0:T(8,128)}, f32[16,768]{1,0:T(8,128)S(1)}, u32[]{:S(2)}, u32[]{:S(2)}) collective-permute-start(f32[16,768]{1,0:T(8,128)} %fusion), channel_id=1, source_target_pairs={{0,13},{1,14},{2,15},{3,16},{4,17},{5,18},{6,19},{7,20},{8,21},{9,... | collective-permute-start | bytes 147464
  295.6 23.5 %collective-permute-start.23 = (f32[16,768]{1,0:T(8,128)}, f32[16,768]{1,0:T(8,128)S(1)}, u32[]{:S(2)}, u32[]{:S(2)}) collective-permute-start(f32[16,768]{1,0:T(8,128)} %fusion), channel_id=1, source_target_pairs={{0,12},{1,13},{2,14},{3,15},{4,16},{5,17},{6,18},{7,19},{8,20},{9,... | collective-permute-start | bytes 147464
  296.9 36.6 %copy-start.36 = (f32[12,768]{1,0:T(8,128)}, f32[12,768]{1,0:T(8,128)S(1)}, u32[]{:S(2)}) copy-start(f32[12,768]{1,0:T(8,128)S(1)} %collective-permute-done.27) | copy-start | bytes 110596
  296.9 32.7 %collective-permute-start.22 = (f32[16,768]{1,0:T(8,128)}, f32[16,768]{1,0:T(8,128)S(1)}, u32[]{:S(2)}, u32[]{:S(2)}) collective-permute-start(f32[16,768]{1,0:T(8,128)} %fusion), channel_id=1, source_target_pairs={{0,11},{1,12},{2,13},{3,14},{4,15},{5,16},{6,17},{7,18},{8,19},{9,... | collective-permute-start | bytes 147464
  303.9 29.5 %copy-start.37 = (f32[16,768]{1,0:T(8,128)}, f32[16,768]{1,0:T(8,128)S(1)}, u32[]{:S(2)}) copy-start(f32[16,768]{1,0:T(8,128)S(1)} %collective-permute-done.26) | copy-start | bytes 147460
  303.9 36.9 %collective-permute-start.21 = (f32[16,768]{1,0:T(8,128)}, f32[16,768]{1,0:T(8,128)}, u32[]{:S(2)}, u32[]{:S(2)}) collective-permute-start(f32[16,768]{1,0:T(8,128)} %fusion), channel_id=1, source_target_pairs={{0,10},{1,11},{2,12},{3,13},{4,14},{5,15},{6,16},{7,17},{8,18},{9,... | collective-permute-start | bytes 147464
  311.5 22.0 %copy-start.38 = (f32[16,768]{1,0:T(8,128)}, f32[16,768]{1,0:T(8,128)S(1)}, u32[]{:S(2)}) copy-start(f32[16,768]{1,0:T(8,128)S(1)} %collective-permute-done.25) | copy-start | bytes 147460
  311.5 30.8 %collective-permute-start.20 = (f32[16,768]{1,0:T(8,128)}, f32[16,768]{1,0:T(8,128)}, u32[]{:S(2)}, u32[]{:S(2)}) collective-permute-start(f32[16,768]{1,0:T(8,128)} %fusion), channel_id=1, source_target_pairs={{0,9},{1,10},{2,11},{3,12},{4,13},{5,14},{6,15},{7,16},{8,17},{9,1... | collective-permute-start | bytes 147464
  313.7 16.0 %copy-start.39 = (f32[16,768]{1,0:T(8,128)}, f32[16,768]{1,0:T(8,128)S(1)}, u32[]{:S(2)}) copy-start(f32[16,768]{1,0:T(8,128)S(1)} %collective-permute-done.24) | copy-start | bytes 147460
  313.7 32.9 %collective-permute-start.19 = (f32[16,768]{1,0:T(8,128)}, f32[16,768]{1,0:T(8,128)}, u32[]{:S(2)}, u32[]{:S(2)}) collective-permute-start(f32[16,768]{1,0:T(8,128)} %fusion), channel_id=1, source_target_pairs={{0,8},{1,9},{2,10},{3,11},{4,12},{5,13},{6,14},{7,15},{8,16},{9,17... | collective-permute-start | bytes 147464
  319.1 10.5 %copy-start.40 = (f32[16,768]{1,0:T(8,128)}, f32[16,768]{1,0:T(8,128)S(1)}, u32[]{:S(2)}) copy-start(f32[16,768]{1,0:T(8,128)S(1)} %collective-permute-done.23) | copy-start | bytes 147460
  319.1 31.4 %collective-permute-start.18 = (f32[16,768]{1,0:T(8,128)}, f32[16,768]{1,0:T(8,128)}, u32[]{:S(2)}, u32[]{:S(2)}) collective-permute-start(f32[16,768]{1,0:T(8,128)} %fusion), channel_id=1, source_target_pairs={{0,7},{1,8},{2,9},{3,10},{4,11},{5,12},{6,13},{7,14},{8,15},{9,16}... | collective-permute-start | bytes 147464
  329.6 10.3 %copy-start.41 = (f32[16,768]{1,0:T(8,128)}, f32[16,768]{1,0:T(8,128)S(1)}, u32[]{:S(2)}) copy-start(f32[16,768]{1,0:T(8,128)S(1)} %collective-permute-done.22) | copy-start | bytes 147460
  329.7 22.8 %collective-permute-start.17 = (f32[16,768]{1,0:T(8,128)}, f32[16,768]{1,0:T(8,128)}, u32[]{:S(2)}, u32[]{:S(2)}) collective-permute-start(f32[16,768]{1,0:T(8,128)} %fusion), channel_id=1, source_target_pairs={{0,6},{1,7},{2,8},{3,9},{4,10},{5,11},{6,12},{7,13},{8,14},{9,15},... | collective-permute-start | bytes 147464
  336.7 19.7 %copy-start.10 = (bf16[32,8,4,48]{3,2,1,0:T(4,128)(2,1)S(1)}, bf16[32,8,4,48]{3,2,1,0:T(4,128)(2,1)}, u32[]{:S(2)}) copy-start(bf16[32,8,4,48]{3,2,1,0:T(4,128)(2,1)} %get-tuple-element.47) | copy-start | bytes 294916
  340.0 16.7 %copy-start.42 = (f32[16,768]{1,0:T(8,128)S(1)}, f32[16,768]{1,0:T(8,128)}, u32[]{:S(2)}) copy-start(f32[16,768]{1,0:T(8,128)} %copy-done.41) | copy-start | bytes 147460
  340.8 27.2 %copy-start.20 = (bf16[1,256,192]{2,1,0:T(8,128)(2,1)S(1)}, bf16[1,256,192]{2,1,0:T(8,128)(2,1)}, u32[]{:S(2)}) copy-start(bf16[1,256,192]{2,1,0:T(8,128)(2,1)} %copy.152) | copy-start | bytes 294916
  340.8 27.2 %copy-start.21 = (bf16[1,256,192]{2,1,0:T(8,128)(2,1)S(1)}, bf16[1,256,192]{2,1,0:T(8,128)(2,1)}, u32[]{:S(2)}) copy-start(bf16[1,256,192]{2,1,0:T(8,128)(2,1)} %concatenate.143) | copy-start | bytes 294916
  340.8 15.8 %collective-permute-start.16 = (f32[16,768]{1,0:T(8,128)}, f32[16,768]{1,0:T(8,128)S(1)}, u32[]{:S(2)}, u32[]{:S(2)}) collective-permute-start(f32[16,768]{1,0:T(8,128)} %fusion), channel_id=1, source_target_pairs={{0,5},{1,6},{2,7},{3,8},{4,9},{5,10},{6,11},{7,12},{8,13},{9,14},{... | collective-permute-start | bytes 147464
  342.2 14.4 %collective-permute-start.15 = (f32[16,768]{1,0:T(8,128)}, f32[16,768]{1,0:T(8,128)S(1)}, u32[]{:S(2)}, u32[]{:S(2)}) collective-permute-start(f32[16,768]{1,0:T(8,128)} %fusion), channel_id=1, source_target_pairs={{0,4},{1,5},{2,6},{3,7},{4,8},{5,9},{6,10},{7,11},{8,12},{9,13},{1... | collective-permute-start | bytes 147464
  346.6 10.0 %collective-permute-start.14 = (f32[16,768]{1,0:T(8,128)}, f32[16,768]{1,0:T(8,128)S(1)}, u32[]{:S(2)}, u32[]{:S(2)}) collective-permute-start(f32[16,768]{1,0:T(8,128)} %fusion), channel_id=1, source_target_pairs={{0,3},{1,4},{2,5},{3,6},{4,7},{5,8},{6,9},{7,10},{8,11},{9,12},{10... | collective-permute-start | bytes 147464
  350.6 6.1 %collective-permute-start.13 = (f32[16,768]{1,0:T(8,128)}, f32[16,768]{1,0:T(8,128)S(1)}, u32[]{:S(2)}, u32[]{:S(2)}) collective-permute-start(f32[16,768]{1,0:T(8,128)} %fusion), channel_id=1, source_target_pairs={{0,2},{1,3},{2,4},{3,5},{4,6},{5,7},{6,8},{7,9},{8,10},{9,11},{10,... | collective-permute-start | bytes 147464
  352.5 4.2 %collective-permute-start.12 = (f32[16,768]{1,0:T(8,128)}, f32[16,768]{1,0:T(8,128)S(1)}, u32[]{:S(2)}, u32[]{:S(2)}) collective-permute-start(f32[16,768]{1,0:T(8,128)} %fusion), channel_id=1, source_target_pairs={{0,1},{1,2},{2,3},{3,4},{4,5},{5,6},{6,7},{7,8},{8,9},{9,10},{10,1... | collective-permute-start | bytes 147464
  (8 other events, 14.7 us)
Sparse Core Ops, SparseCore 0:
  368.1 36.1 reduce-scatter.5
where the time goes:
time: 419 us; the launch traced here: 413 us
  blocking collectives  148 us (35%)
  starting transfers between devices  105 us (25%)
  local copies, waits for them, and re-layouts  50.3 us (12%)
  waiting for transfers between devices  43.8 us (10%)
  other arithmetic  31.8 us (8%)
  matrix products  17.2 us (4%)
  between operations  16 us (4%)
    unnamed x1, blocking collectives  148 us
    unnamed x17, starting transfers between devices  67.4 us
    unnamed x18, waiting for transfers between devices  40 us
    ppermute x12, starting transfers between devices, partner_2(): return lax.ppermute(block, axis, route)  37.8 us
    unnamed x92, local copies, waits for them, and re-layouts  15.4 us
  transfers between devices with their start and end apart: 29, of which 4 were waited for; matrix products, arithmetic and copies ran while one was open for 16% of the time, Pallas kernels for 0%

commit v1 on v0

v1 whole, which is shorter than its diff:
```python
import functools
import math

import jax
import jax.numpy as jnp
from jax import lax
from jax.experimental import pallas as pl
from jax.experimental.pallas import tpu as pltpu
from jax.sharding import PartitionSpec as P

LEVELS = 4
HEADS = 16
HEAD_WIDTH = 48
PAIR_WIDTH = 2 * HEAD_WIDTH
LEVEL_WIDTH = 4 * HEAD_WIDTH
LANES = 128
ROWS = 256
MODEL = 768
SCALE = 1.0 / math.sqrt(HEAD_WIDTH)
BF = jnp.bfloat16
F32 = jnp.float32
VMEM_LIMIT = 48 * 1024 * 1024


def groups_over(bits, count):
    found = {}
    for index in range(count):
        rest = index
        for bit in bits:
            rest &= ~(1 << bit)
        found.setdefault(rest, []).append(index)
    return list(found.values())


def mm(a, b):
    return jnp.dot(a, b, preferred_element_type=F32)


def mm_nt(a, b):
    return lax.dot_general(a, b, (((1,), (1,)), ((), ())), preferred_element_type=F32)


def mm_tn(a, b):
    return lax.dot_general(a, b, (((0,), (0,)), ((), ())), preferred_element_type=F32)


def iota(shape, dim):
    return lax.broadcasted_iota(jnp.int32, shape, dim)


def one_hot(condition):
    return jnp.where(condition, 1.0, 0.0).astype(BF)


def first_head(shape):
    return (iota(shape, 1) & (LANES - 1)) < HEAD_WIDTH


def pack_kernel(off_ref, q_ref, k_ref, v_ref, c_ref, w_ref, near_ref, four_ref, eight_ref, wide):
    wide[...] = jnp.zeros_like(wide)
    grad = mm_nt(c_ref[...], w_ref[...]).astype(BF)
    for half in range(2):
        for level in range(LEVELS):
            start = LEVEL_WIDTH * level + PAIR_WIDTH * half
            for place, rows in enumerate((q_ref[...], k_ref[...], v_ref[...], grad)):
                wide[half, level, :, LANES * place : LANES * place + PAIR_WIDTH] = rows[
                    :, start : start + PAIR_WIDTH
                ]
    for half in range(2):
        near_ref[half, 0:ROWS, :] = wide[half, 0]
        for level in range(1, LEVELS):
            dilation = 1 << level
            count = ROWS // dilation
            source = wide[half, level]
            target = iota((count, ROWS), 1) - dilation * iota((count, ROWS), 0)
            picked = []
            for head in range(2):
                offset = off_ref[4 * level + 2 * half + head] & (dilation - 1)
                picked.append(mm(one_hot(target == offset), source))
            chosen = jnp.where(first_head(picked[0].shape), picked[0], picked[1]).astype(BF)
            if level == 1:
                near_ref[half, ROWS : ROWS + count, :] = chosen
            elif level == 2:
                four_ref[half] = chosen
                four_ref[half + 2] = chosen
            else:
                for chip in range(4):
                    eight_ref[half + 2 * chip] = chosen


def attend(packed):
    q, k, v, g = (packed[:, LANES * i : LANES * (i + 1)] for i in range(4))
    lane = iota(q.shape, 1)
    zero = jnp.zeros((), BF)
    total = [None] * 4
    for head in range(2):
        own = (lane >= HEAD_WIDTH * head) & (lane < HEAD_WIDTH * (head + 1))
        qh, kh, vh, gh = (jnp.where(own, part, zero) for part in (q, k, v, g))
        scores = mm_nt(q, kh) * SCALE
        top = jnp.max(scores, axis=1, keepdims=True)
        raw = jnp.exp(scores - top)
        weights = raw * (1.0 / jnp.sum(raw, axis=1, keepdims=True))
        low = weights.astype(BF)
        attended = mm(low, vh).astype(BF)
        row_dots = jnp.sum(gh.astype(F32) * attended.astype(F32), axis=1, keepdims=True)
        grad_scores = (weights * (mm_nt(g, vh) - row_dots)).astype(BF)
        parts = (
            attended,
            (mm(grad_scores, kh) * SCALE).astype(BF),
            (mm_tn(grad_scores, qh) * SCALE).astype(BF),
            mm_tn(low, gh).astype(BF),
        )
        total = [new if old is None else old + new for old, new in zip(total, parts)]
    return jnp.concatenate(total, axis=1)


def attention_kernel(off_ref, near_ref, four_ref, eight_ref, c_ref, weight_ref, grads_ref):
    position = lax.axis_index("ctx")
    half = position & 1
    chip = position >> 1
    folded = None
    for level in range(LEVELS):
        dilation = 1 << level
        if level == 0:
            placed = jnp.concatenate([attend(near_ref[core, 0:ROWS, :]) for core in range(2)], axis=0)
        else:
            if level == 1:
                packed = jnp.concatenate([near_ref[core, ROWS:, :] for core in range(2)], axis=0)
            elif level == 2:
                packed = four_ref[...].reshape(ROWS, 4 * LANES)
            else:
                packed = eight_ref[...].reshape(ROWS, 4 * LANES)
            done = attend(packed)
            first_row = (chip & (dilation // 2 - 1)) * (2 * ROWS)
            shape = (2 * ROWS, ROWS)
            target = iota(shape, 0) - dilation * iota(shape, 1) + first_row
            spread = []
            for head in range(2):
                offset = off_ref[4 * level + 2 * half + head] & (dilation - 1)
                spread.append(mm(one_hot(target == offset), done))
            placed = jnp.where(first_head(spread[0].shape), spread[0], spread[1]).astype(BF)
        shape = (LANES, LEVELS * PAIR_WIDTH)
        fold = one_hot(iota(shape, 1) == jnp.where(iota(shape, 0) < PAIR_WIDTH, iota(shape, 0) + PAIR_WIDTH * level, -1))
        part = mm(placed[:, 0:LANES], fold)
        folded = part if folded is None else folded + part
        for core in range(2):
            for array in range(3):
                lanes = LEVELS * LANES * array + LANES * level
                grads_ref[core, :, lanes : lanes + LANES] = placed[
                    ROWS * core : ROWS * (core + 1), LANES * (array + 1) : LANES * (array + 2)
                ]
    weight_ref[...] = mm_tn(c_ref[...], folded.astype(BF)).astype(BF)


def merge_kernel(grads_ref, dq_ref, dk_ref, dv_ref):
    for array, out_ref in enumerate((dq_ref, dk_ref, dv_ref)):
        for level in range(LEVELS):
            lanes = LEVELS * LANES * array + LANES * level
            for half in range(2):
                start = LEVEL_WIDTH * level + PAIR_WIDTH * half
                out_ref[:, start : start + PAIR_WIDTH] = grads_ref[half, :, lanes : lanes + PAIR_WIDTH]


def split_kernel(sums_ref, out_ref):
    core = lax.axis_index("ctx") & 1
    shape = (512, LEVELS * PAIR_WIDTH)
    row = iota(shape, 0)
    column = iota(shape, 1)
    inner = row & 15
    source = 24 * (row >> 4) + 12 * core + inner
    level = (source >= 192).astype(jnp.int32) + (source >= 384).astype(jnp.int32) + (source >= 576).astype(jnp.int32)
    rest = source - LEVEL_WIDTH * level
    second = rest >= PAIR_WIDTH
    wanted = PAIR_WIDTH * level + jnp.where(second, rest - PAIR_WIDTH, rest)
    hit = (column == wanted) & (inner < 12)
    out = mm_nt(one_hot(hit & ~second), sums_ref[0]) + mm_nt(one_hot(hit & second), sums_ref[1])
    out_ref[...] = out.astype(BF)


def call(kernel, out_shape, *operands, scalars=0, scratch=()):
    vmem = pl.BlockSpec(memory_space=pltpu.VMEM)
    smem = pl.BlockSpec(memory_space=pltpu.SMEM)
    return pl.pallas_call(
        kernel,
        out_shape=out_shape,
        in_specs=[smem] * scalars + [vmem] * (len(operands) - scalars),
        out_specs=jax.tree.map(lambda _: vmem, out_shape),
        scratch_shapes=list(scratch),
        compiler_params=pltpu.CompilerParams(vmem_limit_bytes=VMEM_LIMIT),
    )(*operands)


def exchange(block, bits):
    return lax.all_to_all(block, "ctx", 0, 0, tiled=True, axis_index_groups=groups_over(bits, 64))


def local(queries, keys, values, cotangent, out_weight, offsets):
    def bf(*shape):
        return jax.ShapeDtypeStruct(shape, BF)

    near, four, eight = call(
        pack_kernel,
        (bf(2, 384, 512), bf(4, 64, 512), bf(8, 32, 512)),
        offsets, queries[0], keys[0], values[0], cotangent[0], out_weight,
        scalars=1,
        scratch=(pltpu.VMEM((2, LEVELS, ROWS, 4 * LANES), BF),),
    )
    near = exchange(near, (0,))
    four = exchange(four, (0, 1))
    eight = exchange(eight, (0, 1, 2))
    both = lax.all_gather(cotangent[0], "ctx", axis=0, tiled=True, axis_index_groups=groups_over((0,), 64))
    weight_part, grads = call(
        attention_kernel,
        (bf(MODEL, 384), bf(2, ROWS, 3 * 512)),
        offsets, near, four, eight, both,
        scalars=1,
    )
    column_parts = lax.all_to_all(weight_part.reshape(8, 96, 384), "batch", 0, 0, tiled=True)
    column_sum = jnp.sum(column_parts.astype(F32), axis=0).astype(BF)
    sums = lax.all_gather(column_sum, "ctx", axis=0, tiled=False, axis_index_groups=groups_over((0,), 64))
    row_parts = call(split_kernel, bf(512, 96), sums)
    row_parts = exchange(row_parts.reshape(32, 16, 96), (1, 2, 3, 4, 5))
    weight_grad = jnp.sum(row_parts.astype(F32), axis=0)[:12]
    grads = exchange(grads, (0,))
    dq, dk, dv = call(merge_kernel, (bf(ROWS, MODEL),) * 3, grads)
    return dq[None], dk[None], dv[None], weight_grad


def solution(mesh):
    rows = P("batch", "ctx", None)
    return jax.shard_map(
        local,
        mesh=mesh,
        in_specs=(rows, rows, rows, rows, P(), P()),
        out_specs=(rows, rows, rows, P("ctx", "batch")),
        check_vma=False,
    )
```

time: 419 us -> 106 us (0.25); the launches traced: 413 us -> 105 us
  blocking collectives: 148 us -> 34.8 us
  starting transfers between devices: 105 us -> 25 us
  local copies, waits for them, and re-layouts: 50.3 us -> 5.91 us
  other arithmetic: 31.8 us -> 0.72 us
  waiting for transfers between devices: 43.8 us -> 21.4 us
  matrix products: 17.2 us -> 0 us
  Pallas kernels: 0 us -> 16.2 us
  between operations: 16 us -> 0.67 us
    unnamed x1 -> x0, blocking collectives: 148 us -> none
    unnamed x17 -> x0, starting transfers between devices: 67.4 us -> none
    unnamed x18 -> x0, waiting for transfers between devices: 40 us -> none
    ppermute x12 -> x0, starting transfers between devices: 37.8 us -> none  [partner_2(): return lax.ppermute(block, axis, route)]
    all_to_all x0 -> x3, blocking collectives: none -> 30.5 us  [the longest x2 18.8 us: exchange(): lax.all_to_all(block, 'ctx', 0, 0, tiled=True, axis_index_groups=groups_o...]
    all_to_all x0 -> x3, starting transfers between devices: none -> 25 us  [exchange(): lax.all_to_all(block, 'ctx', 0, 0, tiled=True, axis_index_groups=groups_o...]
    all_to_all x0 -> x3, waiting for transfers between devices: none -> 21.4 us  [exchange(): lax.all_to_all(block, 'ctx', 0, 0, tiled=True, axis_index_groups=groups_o...]
    select_n x16 -> x0, other arithmetic: 18.2 us -> none  [the longest x6 6.81 us: gather_class(): jnp.where(upper_half, jnp.concatenate([partner, gathered], 0), jnp.concat...]
  transfers between devices with their start and end apart: 29 -> 3, of which waited for: 4 -> 2; matrix products, arithmetic and copies ran while one was open for 16% -> 0% of each run, Pallas kernels for 0% -> 3%
where the time goes in v1:
time: 106 us; the launch traced here: 105 us
  blocking collectives  34.8 us (33%)
  starting transfers between devices  25 us (24%)
  waiting for transfers between devices  21.4 us (20%)
  Pallas kernels  16.2 us (15%)
  local copies, waits for them, and re-layouts  5.91 us (6%)
    all_to_all x3, starting transfers between devices, exchange(): lax.all_to_all(block, 'ctx', 0, 0, tiled=True, axis_index_groups=groups_o...  25 us
    all_to_all x3, waiting for transfers between devices, exchange(): lax.all_to_all(block, 'ctx', 0, 0, tiled=True, axis_index_groups=groups_o...  21.4 us
    all_to_all x2, blocking collectives, exchange(): lax.all_to_all(block, 'ctx', 0, 0, tiled=True, axis_index_groups=groups_o...  18.8 us
    pallas_call x4, Pallas kernels, call(): pl.pallas_call(kernel, out_shape=out_shape, in_specs=[smem] * scalars + [...  16.2 us
    all_to_all x1, blocking collectives, local(): lax.all_to_all(weight_part.reshape(8, 96, 384), 'batch', 0, 0, tiled=True)  11.7 us
    unnamed x16, local copies, waits for them, and re-layouts  5.91 us
    all_gather x1, blocking collectives, local(): lax.all_gather(cotangent[0], 'ctx', axis=0, tiled=True, axis_index_groups...  2.36 us
  transfers between devices with their start and end apart: 3, of which 2 were waited for; matrix products, arithmetic and copies ran while one was open for 0% of the time, Pallas kernels for 3%

profile of v1, /device:TPU:1, one launch (start us, length us, event | category | flops | bytes accessed | tf_op | source)
XLA Modules:
  0.0 104.7 jit_solution(17845030094176121618)
XLA Ops:
  0.6 0.0 copy-start
  0.6 1.0 copy-done
  1.6 0.0 copy-start.2
  1.6 1.3 %copy-done.2 = bf16[768,768]{1,0:T(8,128)(2,1)S(1)} copy-done((bf16[768,768]{1,0:T(8,128)(2,1)S(1)}, bf16[768,768]{1,0:T(8,128)(2,1)}, u32[]{:S(2)}) %copy-start.2) | copy-done | bytes 1179672
  2.9 0.0 copy-start.3
  2.9 1.0 copy-done.3
  3.9 0.0 copy-start.4
  3.9 1.0 copy-done.4
  4.9 0.0 copy-start.5
  4.9 1.0 copy-done.5
  5.9 0.0 copy-start.6
  5.9 0.7 copy-done.6
  6.5 2.9 %shard_map.93 = (bf16[2,384,512]{2,1,0:T(8,128)(2,1)S(1)}, bf16[4,64,512]{2,1,0:T(8,128)(2,1)S(1)}, bf16[8,32,512]{2,1,0:T(8,128)(2,1)}) custom-call(s32[16]{0:T(128)S(1)} %copy-done.6, bf16[256,768]{1,0:T(8,128)(2,1)S(1)} %bitcast.16, bf16[256,768]{1,0:T(8,128)(2,1)S(1)} %bitcast.17, bf16[256,768]{1,0:T(8,128)(2,1)S(1)} %bitcast.18, ...), custom_call_target="tpu_custom_call" | custom-call | tf_op jit(solution)/shard_map/pallas_call | solution.py:183
  9.5 0.0 copy-start.1
  9.5 0.0 copy-start.7
  9.5 11.0 %all_to_all.30.near_ref = bf16[2,384,512]{2,1,0:T(8,128)(2,1)S(1)} all-to-all(bf16[2,384,512]{2,1,0:T(8,128)(2,1)S(1)} %get-tuple-element.12), channel_id=1, replica_groups={{0,1},{2,3},{4,5},{6,7},{8,9},{10,11},{12,13},{14,15},{16,17},{18,19},{..., dimensions={0} | all-to-all | bytes 1572864 | tf_op jit(solution)/shard_map/all_to_all | solution.py:194
  20.5 7.7 %all_to_all.31.four_ref = bf16[4,64,512]{2,1,0:T(8,128)(2,1)S(1)} all-to-all(bf16[4,64,512]{2,1,0:T(8,128)(2,1)S(1)} %get-tuple-element.13), channel_id=1, replica_groups={{0,1,2,3},{4,5,6,7},{8,9,10,11},{12,13,14,15},{16,17,18,19},{20,21,22,2..., dimensions={0} | all-to-all | bytes 524288 | tf_op jit(solution)/shard_map/all_to_all | solution.py:194
  28.2 4.4 %all-to-all-start.2 = ((bf16[8,32,512]{2,1,0:T(8,128)(2,1)}), bf16[8,32,512]{2,1,0:T(8,128)(2,1)S(1)}, u32[]{:S(2)}, u32[]{:S(2)}) async-start(bf16[8,32,512]{2,1,0:T(8,128)(2,1)} %get-tuple-element.14), calls=%async_computation.2 | async-start | bytes 524288 | tf_op jit(solution)/shard_map/all_to_all | solution.py:194
  32.6 0.0 copy-done.1
  32.6 2.4 %all-gather = bf16[1,512,768]{2,1,0:T(8,128)(2,1)S(1)} all-gather(bf16[1,256,768]{2,1,0:T(8,128)(2,1)S(1)} %copy-done.1), channel_id=2, replica_groups={{0,1},{2,3},{4,5},{6,7},{8,9},{10,11},{12,13},{14,15},{16,17},{18,19},{..., dimensions={1}, use_global_device_ids=true | all-gather | bytes 1179648 | tf_op jit(solution)/shard_map/all_gather | solution.py:211
  35.0 6.4 %all-to-all-done.2.eight_ref = bf16[8,32,512]{2,1,0:T(8,128)(2,1)S(1)} async-done(((bf16[8,32,512]{2,1,0:T(8,128)(2,1)}), bf16[8,32,512]{2,1,0:T(8,128)(2,1)S(1)}, u32[]{:S(2)}, u32[]{:S(2)}) %all-to-all-start.2) | async-done | bytes 262176 | tf_op jit(solution)/shard_map/all_to_all | solution.py:194
  41.3 0.0 copy-done.7
  41.3 10.5 %shard_map.94 = (bf16[768,384]{1,0:T(8,128)(2,1)S(1)}, bf16[2,256,1536]{2,1,0:T(8,128)(2,1)}) custom-call(s32[16]{0:T(128)S(1)} %copy-done.7, bf16[2,384,512]{2,1,0:T(8,128)(2,1)S(1)} %all_to_all.30.near_ref, bf16[4,64,512]{2,1,0:T(8,128)(2,1)S(1)} %all_to_all.31.four_ref, bf16[8,32,512]{2,1,0:T(8,128)(2,1)S(1)} %all-to-all-done.2.eight_ref, ...), custom_call_target="tpu_custom_call" | custom-call | tf_op jit(solution)/shard_map/pallas_call | solution.py:183
  51.9 11.7 %all_to_all.32 = bf16[8,96,384]{2,1,0:T(8,128)(2,1)S(1)} all-to-all(bf16[8,96,384]{2,1,0:T(8,128)(2,1)S(1)} %bitcast.14), channel_id=1, replica_groups=mesh['batch'=8,'ctx'=64] {'batch'}, dimensions={0} | all-to-all | bytes 1179648 | tf_op jit(solution)/shard_map/all_to_all | solution.py:218
  63.6 6.1 %all-to-all-start.3 = ((bf16[2,256,1536]{2,1,0:T(8,128)(2,1)}), bf16[2,256,1536]{2,1,0:T(8,128)(2,1)S(1)}, u32[]{:S(2)}, u32[]{:S(2)}) async-start(bf16[2,256,1536]{2,1,0:T(8,128)(2,1)} %get-tuple-element.15), calls=%async_computation.3 | async-start | bytes 3145728 | tf_op jit(solution)/shard_map/all_to_all | solution.py:194
  69.7 0.1 reduce_sum.21
  69.7 1.9 %all-gather.1 = bf16[192,384]{1,0:T(8,128)(2,1)S(1)} all-gather(bf16[96,384]{1,0:T(8,128)(2,1)S(1)} %reduce_sum.21), channel_id=3, replica_groups={{0,1},{2,3},{4,5},{6,7},{8,9},{10,11},{12,13},{14,15},{16,17},{18,19},{..., dimensions={0}, use_global_device_ids=true | all-gather | bytes 221184 | tf_op jit(solution)/shard_map/all_gather | solution.py:220
  71.7 1.2 %shard_map.96 = bf16[512,96]{1,0:T(8,128)(2,1)} custom-call(bf16[2,96,384]{2,1,0:T(8,128)(2,1)S(1)} %bitcast.15), custom_call_target="tpu_custom_call" | custom-call | tf_op jit(solution)/shard_map/pallas_call | solution.py:183
  72.9 0.0 all-to-all-done.3.grads_ref
  72.9 14.6 %all-to-all-start.5 = ((bf16[32,16,96]{2,1,0:T(8,128)(2,1)}), bf16[32,16,96]{2,1,0:T(8,128)(2,1)S(1)}, u32[]{:S(2)}, u32[]{:S(2)}) async-start(bf16[32,16,96]{2,1,0:T(8,128)(2,1)} %bitcast.10), calls=%async_computation.5 | async-start | bytes 262144 | tf_op jit(solution)/shard_map/all_to_all | solution.py:194
  87.5 1.5 %shard_map.95 = (bf16[256,768]{1,0:T(8,128)(2,1)}, bf16[256,768]{1,0:T(8,128)(2,1)}, bf16[256,768]{1,0:T(8,128)(2,1)}) custom-call(bf16[2,256,1536]{2,1,0:T(8,128)(2,1)S(1)} %all-to-all-done.3.grads_ref), custom_call_target="tpu_custom_call" | custom-call | tf_op jit(solution)/shard_map/pallas_call | solution.py:183
  89.0 15.0 %all-to-all-done.5 = bf16[32,16,96]{2,1,0:T(8,128)(2,1)S(1)} async-done(((bf16[32,16,96]{2,1,0:T(8,128)(2,1)}), bf16[32,16,96]{2,1,0:T(8,128)(2,1)S(1)}, u32[]{:S(2)}, u32[]{:S(2)}) %all-to-all-start.5) | async-done | bytes 98336 | tf_op jit(solution)/shard_map/all_to_all | solution.py:194
  104.1 0.6 convert_reduce_fusion
Async XLA Ops:
  0.6 1.0 copy-start
  1.6 1.3 %copy-start.2 = (bf16[768,768]{1,0:T(8,128)(2,1)S(1)}, bf16[768,768]{1,0:T(8,128)(2,1)}, u32[]{:S(2)}) copy-start(bf16[768,768]{1,0:T(8,128)(2,1)} %w_ref.1) | copy-start | bytes 3538948
  2.9 1.0 copy-start.3
  3.9 1.0 copy-start.4
  4.9 1.0 copy-start.5
  5.9 0.7 copy-start.6
  9.5 23.1 %copy-start.1 = (bf16[1,256,768]{2,1,0:T(8,128)(2,1)S(1)}, bf16[1,256,768]{2,1,0:T(8,128)(2,1)}, u32[]{:S(2)}) copy-start(bf16[1,256,768]{2,1,0:T(8,128)(2,1)} %param.9) | copy-start | bytes 1179652
  9.5 31.8 %copy-start.7 = (s32[16]{0:T(128)S(1)}, s32[16]{0:T(128)}, u32[]{:S(2)}) copy-start(s32[16]{0:T(128)} %off_ref.3) | copy-start | bytes 196
  28.2 13.1 %all-to-all-start.2 = ((bf16[8,32,512]{2,1,0:T(8,128)(2,1)}), bf16[8,32,512]{2,1,0:T(8,128)(2,1)S(1)}, u32[]{:S(2)}, u32[]{:S(2)}) async-start(bf16[8,32,512]{2,1,0:T(8,128)(2,1)} %get-tuple-element.14), calls=%async_computation.2 | async-start | bytes 524288 | tf_op jit(solution)/shard_map/all_to_all | solution.py:194
  63.6 9.3 %all-to-all-start.3 = ((bf16[2,256,1536]{2,1,0:T(8,128)(2,1)}), bf16[2,256,1536]{2,1,0:T(8,128)(2,1)S(1)}, u32[]{:S(2)}, u32[]{:S(2)}) async-start(bf16[2,256,1536]{2,1,0:T(8,128)(2,1)} %get-tuple-element.15), calls=%async_computation.3 | async-start | bytes 3145728 | tf_op jit(solution)/shard_map/all_to_all | solution.py:194
  72.9 31.2 %all-to-all-start.5 = ((bf16[32,16,96]{2,1,0:T(8,128)(2,1)}), bf16[32,16,96]{2,1,0:T(8,128)(2,1)S(1)}, u32[]{:S(2)}, u32[]{:S(2)}) async-start(bf16[32,16,96]{2,1,0:T(8,128)(2,1)} %bitcast.10), calls=%async_computation.5 | async-start | bytes 262144 | tf_op jit(solution)/shard_map/all_to_all | solution.py:194

commit v2 on v1

v2 whole, which is shorter than its diff:
```python
import math

import jax
import jax.numpy as jnp
from jax import lax
from jax.experimental import pallas as pl
from jax.experimental.pallas import tpu as pltpu
from jax.sharding import PartitionSpec as P

LEVELS = 4
HEADS = 16
HEAD_WIDTH = 48
PAIR_WIDTH = 2 * HEAD_WIDTH
LEVEL_WIDTH = 4 * HEAD_WIDTH
LANES = 128
ROWS = 256
MODEL = 768
HALF_LANES = 6 * LANES
SCALE = 1.0 / math.sqrt(HEAD_WIDTH)
BF = jnp.bfloat16
F32 = jnp.float32
VMEM_LIMIT = 24 * 1024 * 1024


def groups_over(bits, count):
    found = {}
    for index in range(count):
        rest = index
        for bit in bits:
            rest &= ~(1 << bit)
        found.setdefault(rest, []).append(index)
    return list(found.values())


def mm(a, b):
    return jnp.dot(a, b, preferred_element_type=F32)


def mm_nt(a, b):
    return lax.dot_general(a, b, (((1,), (1,)), ((), ())), preferred_element_type=F32)


def mm_tn(a, b):
    return lax.dot_general(a, b, (((0,), (0,)), ((), ())), preferred_element_type=F32)


def iota(shape, dim):
    return lax.broadcasted_iota(jnp.int32, shape, dim)


def one_hot(condition):
    return jnp.where(condition, 1.0, 0.0).astype(BF)


def first_head(shape):
    return (iota(shape, 1) & (LANES - 1)) < HEAD_WIDTH


def pack_kernel(
    off_ref, q_hbm, k_hbm, v_hbm, c_hbm, w_hbm, mine_ref, other_ref, four_ref, eight_ref, wide, q_ref, k_ref, v_ref, c_ref, w_ref, sems
):
    moves = start_all(((c_hbm, c_ref), (w_hbm, w_ref), (q_hbm, q_ref), (k_hbm, k_ref), (v_hbm, v_ref)), sems)
    core = lax.axis_index("ctx") & 1
    wide[...] = jnp.zeros_like(wide)
    moves[0].wait()
    cotangent = c_ref[...]
    half_rows = ROWS // 2
    other_ref[384:640, :] = cotangent[:, :512]
    other_ref[640:768, 0:256] = cotangent[:half_rows, 512:]
    other_ref[640:768, 256:512] = cotangent[half_rows:, 512:]
    moves[1].wait()
    grad = mm_nt(cotangent, w_ref[...]).astype(BF)
    for place, rows_ref in ((0, q_ref), (1, k_ref), (2, v_ref), (3, None)):
        if rows_ref is not None:
            moves[2 + place].wait()
        rows = grad if rows_ref is None else rows_ref[...]
        for half in range(2):
            for level in range(LEVELS):
                start = LEVEL_WIDTH * level + PAIR_WIDTH * half
                wide[half, level, :, LANES * place : LANES * place + PAIR_WIDTH] = rows[:, start : start + PAIR_WIDTH]
    for half in range(2):
        for level in range(1, LEVELS):
            dilation = 1 << level
            count = ROWS // dilation
            target = iota((count, ROWS), 1) - dilation * iota((count, ROWS), 0)
            hits = [
                one_hot(target == (off_ref[4 * level + 2 * half + head] & (dilation - 1))) for head in range(2)
            ]
            picked = mm(jnp.concatenate(hits, axis=0), wide[half, level])
            chosen = jnp.where(first_head((count, 4 * LANES)), picked[:count], picked[count:]).astype(BF)
            if level == 2:
                four_ref[half] = chosen
                four_ref[half + 2] = chosen
            elif level == 3:
                for chip in range(4):
                    eight_ref[half + 2 * chip] = chosen
            else:

                @pl.when(core == half)
                def _(chosen=chosen, half=half):
                    mine_ref[0:ROWS, :] = wide[half, 0]
                    mine_ref[ROWS:, :] = chosen

                @pl.when(core != half)
                def _(chosen=chosen, half=half):
                    other_ref[0:ROWS, :] = wide[half, 0]
                    other_ref[ROWS:384, :] = chosen


def attend(packed, backward=True):
    q, k, v, g = (packed[:, LANES * i : LANES * (i + 1)] for i in range(4))
    lane = iota(q.shape, 1)
    zero = jnp.zeros((), BF)
    total = None
    for head in range(2):
        own = (lane >= HEAD_WIDTH * head) & (lane < HEAD_WIDTH * (head + 1))
        qh, kh, vh, gh = (jnp.where(own, part, zero) for part in (q, k, v, g))
        scores = mm_nt(q, kh) * SCALE
        top = jnp.max(scores, axis=1, keepdims=True)
        raw = jnp.exp(scores - top)
        weights = raw * (1.0 / jnp.sum(raw, axis=1, keepdims=True))
        low = weights.astype(BF)
        attended = mm(low, vh).astype(BF)
        parts = [attended]
        if backward:
            row_dots = jnp.sum(gh.astype(F32) * attended.astype(F32), axis=1, keepdims=True)
            grad_scores = (weights * (mm_nt(g, vh) - row_dots)).astype(BF)
            parts += [
                (mm(grad_scores, kh) * SCALE).astype(BF),
                (mm_tn(grad_scores, qh) * SCALE).astype(BF),
                mm_tn(low, gh).astype(BF),
            ]
        total = parts if total is None else [old + new for old, new in zip(total, parts)]
    return jnp.concatenate(total, axis=1) if backward else total[0]


def place_rows(off_ref, done, level):
    position = lax.axis_index("ctx")
    core = position & 1
    chip = position >> 1
    dilation = 1 << level
    count = 2 * ROWS
    row = iota((count, ROWS), 0)
    target = row - dilation * iota((count, ROWS), 1)
    if level > 1:
        first_row = (chip & (dilation // 2 - 1)) * count
        target = (row ^ (ROWS * core)) - dilation * iota((count, ROWS), 1) + first_row
    hits = [one_hot(target == (off_ref[4 * level + 2 * core + head] & (dilation - 1))) for head in range(2)]
    spread = mm(jnp.concatenate(hits, axis=0), done)
    return jnp.where(first_head((count, done.shape[1])), spread[:count], spread[count:]).astype(BF)


def fold_lanes(rows, level):
    shape = (LANES, LEVELS * PAIR_WIDTH)
    lane = iota(shape, 0)
    return mm(rows, one_hot(iota(shape, 1) == jnp.where(lane < PAIR_WIDTH, lane + PAIR_WIDTH * level, -1)))


def grad_lanes(array, level):
    return LANES * (2 * array + level % 2)


def store_grads(keep_ref, send_ref, placed, level):
    for array in range(3):
        lanes = grad_lanes(array, level)
        part = placed[:, LANES * (array + 1) : LANES * (array + 2)]
        keep_ref[:, lanes : lanes + LANES] = part[:ROWS]
        send_ref[:, lanes : lanes + LANES] = part[ROWS:]


def start_all(pairs, sems):
    moves = [pltpu.make_async_copy(source, target, sems.at[index]) for index, (source, target) in enumerate(pairs)]
    for move in moves:
        move.start()
    return moves


def wait_all(moves):
    for move in moves:
        move.wait()


def near_segments(mine_ref, other_ref):
    return (
        mine_ref[0:ROWS, :],
        other_ref[0:ROWS, :],
        jnp.concatenate([mine_ref[ROWS:384, :], other_ref[ROWS:384, :]], axis=0),
    )


def near_attended_kernel(off_ref, mine_ref, other_ref, attended_ref):
    done = [attend(segment, backward=False) for segment in near_segments(mine_ref, other_ref)]
    folded = fold_lanes(jnp.concatenate(done[:2], axis=0), 0)
    folded += fold_lanes(place_rows(off_ref, done[2], 1), 1)
    attended_ref[...] = folded.astype(BF)


def near_grads_kernel(off_ref, mine_ref, other_ref, keep_hbm, send_hbm, keep_ref, send_ref, sems):
    done = [attend(segment) for segment in near_segments(mine_ref, other_ref)]
    store_grads(keep_ref, send_ref, jnp.concatenate(done[:2], axis=0), 0)
    store_grads(keep_ref, send_ref, place_rows(off_ref, done[2], 1), 1)
    wait_all(start_all(((keep_ref, keep_hbm), (send_ref, send_hbm)), sems))


def weight_kernel(off_ref, own_ref, other_ref, four_ref, eight_ref, attended_ref, weight_ref):
    folded = attended_ref[...]
    for level, segment_ref in ((2, four_ref), (3, eight_ref)):
        done = attend(segment_ref[...].reshape(ROWS, 4 * LANES), backward=False)
        folded += fold_lanes(place_rows(off_ref, done, level), level).astype(BF)
    narrow = jnp.concatenate([other_ref[640:768, 0:256], other_ref[640:768, 256:512]], axis=0)
    other = jnp.concatenate([other_ref[384:640, :], narrow], axis=1)
    part = mm_tn(jnp.concatenate([own_ref[...], other], axis=0), folded).astype(BF)
    for column in range(8):
        rows = part[96 * column : 96 * (column + 1)]
        weight_ref[2 * column, 0:96, :] = rows[:, 0:128]
        weight_ref[2 * column, 96:144, 0:64] = rows[0:48, 128:192]
        weight_ref[2 * column, 96:144, 64:128] = rows[48:96, 128:192]
        weight_ref[2 * column + 1, 0:96, :] = rows[:, 256:384]
        weight_ref[2 * column + 1, 96:144, 0:64] = rows[0:48, 192:256]
        weight_ref[2 * column + 1, 96:144, 64:128] = rows[48:96, 192:256]


def far_grads_kernel(off_ref, four_ref, eight_ref, keep_hbm, send_hbm, keep_ref, send_ref, sems):
    for level, segment_ref in ((2, four_ref), (3, eight_ref)):
        done = attend(segment_ref[...].reshape(ROWS, 4 * LANES))
        store_grads(keep_ref, send_ref, place_rows(off_ref, done, level), level)
    wait_all(start_all(((keep_ref, keep_hbm), (send_ref, send_hbm)), sems))


def merge_kernel(near_hbm, far_hbm, got_near_hbm, got_far_hbm, dq_hbm, dk_hbm, dv_hbm, keep_ref, got_ref, out_ref, sems):
    core = lax.axis_index("ctx") & 1
    wait_all(
        start_all(
            (
                (near_hbm, keep_ref.at[0]),
                (far_hbm, keep_ref.at[1]),
                (got_near_hbm.at[1 - core], got_ref.at[0]),
                (got_far_hbm.at[1 - core], got_ref.at[1]),
            ),
            sems,
        )
    )
    for own in range(2):

        @pl.when(core == own)
        def _(own=own):
            for array in range(3):
                for level in range(LEVELS):
                    lanes = grad_lanes(array, level)
                    for half in range(2):
                        source = keep_ref if half == own else got_ref
                        start = LEVEL_WIDTH * level + PAIR_WIDTH * half
                        out_ref[array, :, start : start + PAIR_WIDTH] = source[level // 2, :, lanes : lanes + PAIR_WIDTH]

    wait_all(start_all([(out_ref.at[array], out) for array, out in enumerate((dq_hbm, dk_hbm, dv_hbm))], sems))


def split_kernel(sums_ref, out_ref):
    position = lax.axis_index("ctx")
    core = position & 1
    upper = position >> 5
    shape = (256, LANES)
    row = iota(shape, 0)
    lane = iota(shape, 1)
    inner = row & 15
    source = 24 * (row >> 4) + 12 * core + inner
    second_level = (source >= LEVEL_WIDTH).astype(jnp.int32)
    rest = source - LEVEL_WIDTH * second_level
    second_half = rest >= PAIR_WIDTH
    column = PAIR_WIDTH * second_level + jnp.where(second_half, rest - PAIR_WIDTH, rest)
    wide_first = jnp.where(upper == 0, 0, 64)
    narrow_first = jnp.where(upper == 0, 128, 0)
    in_wide = (lane == column - wide_first) & (inner < 12)
    in_narrow = (lane == column - narrow_first) & (inner < 12)
    out = None
    for half in range(2):
        mine = second_half if half else ~second_half
        wide = one_hot(in_wide & mine)
        narrow = one_hot(in_narrow & mine & (lane < 64))
        sums = sums_ref[half]
        tail = sums[96:144]
        tail_rows = jnp.concatenate([tail, pltpu.roll(tail.astype(F32), 64, 1).astype(BF)], axis=0)
        part = mm_nt(wide, sums[0:96]) + mm_nt(narrow, tail_rows)
        out = part if out is None else out + part
    out_ref[:, 0:96] = out.astype(BF)
    out_ref[:, 96:128] = jnp.zeros((256, 32), BF)


def call(kernel, out_shape, *operands, smem=True, hbm=0, hbm_out=False, scratch=(), flops=0):
    vmem = pl.BlockSpec(memory_space=pltpu.VMEM)
    far = pl.BlockSpec(memory_space=pltpu.HBM)
    specs = [pl.BlockSpec(memory_space=pltpu.SMEM)] * smem
    specs += [vmem] * (len(operands) - smem - hbm) + [far] * hbm
    near = len(operands) - hbm
    operands = operands[:near] + tuple(pltpu.with_memory_space_constraint(x, pltpu.HBM) for x in operands[near:])
    return pl.pallas_call(
        kernel,
        out_shape=jax.tree.map(lambda x: pltpu.HBM(x.shape, x.dtype), out_shape) if hbm_out else out_shape,
        in_specs=specs,
        out_specs=jax.tree.map(lambda _: far if hbm_out else vmem, out_shape),
        scratch_shapes=list(scratch),
        compiler_params=pltpu.CompilerParams(vmem_limit_bytes=VMEM_LIMIT),
        cost_estimate=pl.CostEstimate(flops=flops, bytes_accessed=0, transcendentals=0) if flops else None,
    )(*operands)


def exchange(block, bits):
    return lax.all_to_all(block, "ctx", 0, 0, tiled=True, axis_index_groups=groups_over(bits, 64))


def pair_gather(block):
    return lax.all_gather(block, "ctx", axis=0, tiled=False, axis_index_groups=groups_over((0,), 64))


def swap(block):
    return lax.ppermute(block, "ctx", [(index, index ^ 1) for index in range(64)])


def local(queries, keys, values, cotangent, out_weight, offsets):
    def bf(*shape):
        return jax.ShapeDtypeStruct(shape, BF)

    def vmem(*shape):
        return pltpu.VMEM(shape, BF)

    def dma(count):
        return pltpu.SemaphoreType.DMA((count,))

    rows = vmem(ROWS, MODEL)
    mine, other, four, eight = call(
        pack_kernel,
        (bf(384, 512), bf(768, 512), bf(4, 64, 512), bf(8, 32, 512)),
        offsets, queries[0], keys[0], values[0], cotangent[0], out_weight,
        hbm=5,
        scratch=(vmem(2, LEVELS, ROWS, 4 * LANES), rows, rows, rows, rows, vmem(MODEL, MODEL), dma(5)),
    )
    other = swap(other)
    four = exchange(four, (0, 1))
    attended = call(near_attended_kernel, bf(2 * ROWS, 384), offsets, mine, other, flops=2_000_000_000)
    attended, eight = lax.optimization_barrier((attended, eight))
    eight = exchange(eight, (0, 1, 2))
    half = vmem(ROWS, HALF_LANES)
    grads = dict(hbm_out=True, scratch=(half, half, dma(2)), flops=5_000_000_000)
    near_keep, near_send = call(near_grads_kernel, (bf(ROWS, HALF_LANES),) * 2, offsets, mine, other, **grads)
    attended, near_send = lax.optimization_barrier((attended, near_send))
    weight_parts = call(
        weight_kernel, bf(16, 144, 128), offsets, cotangent[0], other, four, eight, attended, flops=2_000_000_000
    )
    weight_parts, four, eight = lax.optimization_barrier((weight_parts, four, eight))
    plane = [[64 * batch + 32 * top + rest for batch in range(8) for top in range(2)] for rest in range(32)]
    column_parts = lax.all_to_all(weight_parts, ("batch", "ctx"), 0, 0, tiled=True, axis_index_groups=plane)
    far_keep, far_send = call(far_grads_kernel, (bf(ROWS, HALF_LANES),) * 2, offsets, four, eight, **grads)
    column_sum = jnp.sum(column_parts.astype(F32), axis=0).astype(BF)
    row_parts = call(split_kernel, bf(256, 128), pair_gather(column_sum), smem=False)
    row_parts, near_send, far_send = lax.optimization_barrier((row_parts, near_send, far_send))
    row_parts = exchange(row_parts.reshape(16, 16, 128), (1, 2, 3, 4))
    weight_grad = jnp.sum(row_parts.astype(F32), axis=0)[:12, :96]
    both = vmem(2, ROWS, HALF_LANES)
    dq, dk, dv = call(
        merge_kernel,
        (bf(ROWS, MODEL),) * 3,
        near_keep, far_keep, pair_gather(near_send), pair_gather(far_send),
        smem=False, hbm=4, hbm_out=True, scratch=(both, both, vmem(3, ROWS, MODEL), dma(4)), flops=2_000_000_000,
    )
    return dq[None], dk[None], dv[None], weight_grad


def solution(mesh):
    rows = P("batch", "ctx", None)
    return jax.shard_map(
        local,
        mesh=mesh,
        in_specs=(rows, rows, rows, rows, P(), P()),
        out_specs=(rows, rows, rows, P("ctx", "batch")),
        check_vma=False,
    )
```

time: 106 us -> 86 us (0.81)
  blocking collectives: 34.8 us -> 8.95 us
  Pallas kernels: 16.2 us -> 27.9 us
  starting transfers between devices: 25 us -> 32.9 us
  waiting for transfers between devices: 21.4 us -> 13.5 us
  local copies, waits for them, and re-layouts: 5.91 us -> 0.67 us
    all_to_all x3 -> x0, blocking collectives: 30.5 us -> none  [the longest x2 18.8 us: exchange(): lax.all_to_all(block, 'ctx', 0, 0, tiled=True, axis_index_groups=groups_o...]
    all_to_all x3, waiting for transfers between devices: 21.4 us -> 8.01 us  [exchange(): lax.all_to_all(block, 'ctx', 0, 0, tiled=True, axis_index_groups=groups_o...]
    pallas_call x4 -> x7, Pallas kernels: 16.2 us -> 27.9 us  [call(): pl.pallas_call(kernel, out_shape=jax.tree.map(lambda x: pltpu.HBM(x.shape...]
    ppermute x0 -> x1, starting transfers between devices: none -> 8.79 us  [swap(): lax.ppermute(block, 'ctx', [(index, index ^ 1) for index in range(64)])]
    all_to_all x0 -> x1, waiting for transfers between devices: none -> 5.51 us  [local(): lax.all_to_all(weight_parts, ('batch', 'ctx'), 0, 0, tiled=True, axis_ind...]
    unnamed x16 -> x10, local copies, waits for them, and re-layouts: 5.91 us -> 0.67 us
    all_gather x2 -> x3, blocking collectives: 4.29 us -> 8.95 us  [pair_gather(): lax.all_gather(block, 'ctx', axis=0, tiled=False, axis_index_groups=group...]
    all_to_all x3, starting transfers between devices: 25 us -> 20.4 us  [exchange(): lax.all_to_all(block, 'ctx', 0, 0, tiled=True, axis_index_groups=groups_o...]
  transfers between devices with their start and end apart: 3 -> 5, of which waited for: 2 -> 4; matrix products, arithmetic and copies ran while one was open for 0% -> 0% of each run, Pallas kernels for 3% -> 20%
where the time goes in v2:
time: 86 us; the launch traced here: 85.5 us
  starting transfers between devices  32.9 us (38%)
  Pallas kernels  27.9 us (32%)
  waiting for transfers between devices  13.5 us (16%)
  blocking collectives  8.95 us (10%)
    pallas_call x7, Pallas kernels, call(): pl.pallas_call(kernel, out_shape=jax.tree.map(lambda x: pltpu.HBM(x.shape...  27.9 us
    all_to_all x3, starting transfers between devices, exchange(): lax.all_to_all(block, 'ctx', 0, 0, tiled=True, axis_index_groups=groups_o...  20.4 us
    all_gather x3, blocking collectives, pair_gather(): lax.all_gather(block, 'ctx', axis=0, tiled=False, axis_index_groups=group...  8.95 us
    ppermute x1, starting transfers between devices, swap(): lax.ppermute(block, 'ctx', [(index, index ^ 1) for index in range(64)])  8.79 us
    all_to_all x3, waiting for transfers between devices, exchange(): lax.all_to_all(block, 'ctx', 0, 0, tiled=True, axis_index_groups=groups_o...  8.01 us
    all_to_all x1, waiting for transfers between devices, local(): lax.all_to_all(weight_parts, ('batch', 'ctx'), 0, 0, tiled=True, axis_ind...  5.51 us
    all_to_all x1, starting transfers between devices, local(): lax.all_to_all(weight_parts, ('batch', 'ctx'), 0, 0, tiled=True, axis_ind...  3.76 us
  transfers between devices with their start and end apart: 5, of which 4 were waited for; matrix products, arithmetic and copies ran while one was open for 0% of the time, Pallas kernels for 20%

profile of v2, /device:TPU:1, one launch (start us, length us, event | category | flops | bytes accessed | tf_op | source)
XLA Modules:
  0.0 85.5 jit_solution(17643495367337568011)
XLA Ops:
  0.6 0.0 copy-start.1
  0.6 0.6 copy-done.1
  1.3 0.0 copy-start.2
  1.3 5.2 %shard_map.93 = (bf16[384,512]{1,0:T(8,128)(2,1)S(1)}, bf16[768,512]{1,0:T(8,128)(2,1)S(1)}, bf16[4,64,512]{2,1,0:T(8,128)(2,1)}, bf16[8,32,512]{2,1,0:T(8,128)(2,1)}) custom-call(s32[16]{0:T(128)S(1)} %copy-done.1, bf16[256,768]{1,0:T(8,128)(2,1)} %bitcast.17, bf16[256,768]{1,0:T(8,128)(2,1)} %bitcast.18, bf16[256,768]{1,0:T(8,128)(2,1)} %bitcast.19, ...), custom_call_target="tpu_custom_call" | custom-call | tf_op jit(solution)/shard_map/pallas_call | solution.py:296
  6.5 8.8 %collective-permute-start = (bf16[768,512]{1,0:T(8,128)(2,1)S(1)}, bf16[768,512]{1,0:T(8,128)(2,1)S(1)}, u32[]{:S(2)}, u32[]{:S(2)}) collective-permute-start(bf16[768,512]{1,0:T(8,128)(2,1)S(1)} %get-tuple-element.26), channel_id=1, source_target_pairs={{0,1},{1,0},{2,3},{3,2},{4,5},{5,4},{6,7},{7,6},{8,9},{9,8},{10,11... | collective-permute-start | bytes 2359304 | tf_op jit(solution)/shard_map/ppermute | solution.py:316
  15.3 3.4 %all-to-all-start = ((bf16[4,64,512]{2,1,0:T(8,128)(2,1)}), bf16[4,64,512]{2,1,0:T(8,128)(2,1)S(1)}, u32[]{:S(2)}, u32[]{:S(2)}) async-start(bf16[4,64,512]{2,1,0:T(8,128)(2,1)} %get-tuple-element.28), calls=%async_computation | async-start | bytes 524288 | tf_op jit(solution)/shard_map/all_to_all | solution.py:308
  18.7 0.0 collective-permute-done.other_ref
  18.8 0.0 copy-done.2
  18.8 2.9 %shard_map.95.attended_ref = bf16[512,384]{1,0:T(8,128)(2,1)S(1)} custom-call(s32[16]{0:T(128)S(1)} %copy-done.2, bf16[384,512]{1,0:T(8,128)(2,1)S(1)} %get-tuple-element.25.mine_ref, bf16[768,512]{1,0:T(8,128)(2,1)S(1)} %collective-permute-done.other_ref), custom_call_target="tpu_custom_call" | custom-call | flops 2000000000 | tf_op jit(solution)/shard_map/pallas_call | solution.py:296
  21.7 2.2 %all-to-all-done.four_ref = bf16[4,64,512]{2,1,0:T(8,128)(2,1)S(1)} async-done(((bf16[4,64,512]{2,1,0:T(8,128)(2,1)}), bf16[4,64,512]{2,1,0:T(8,128)(2,1)S(1)}, u32[]{:S(2)}, u32[]{:S(2)}) %all-to-all-start) | async-done | bytes 262176 | tf_op jit(solution)/shard_map/all_to_all | solution.py:308
  23.9 4.2 %all-to-all-start.1 = ((bf16[8,32,512]{2,1,0:T(8,128)(2,1)}), bf16[8,32,512]{2,1,0:T(8,128)(2,1)S(1)}, u32[]{:S(2)}, u32[]{:S(2)}) async-start(bf16[8,32,512]{2,1,0:T(8,128)(2,1)} %get-tuple-element.30), calls=%async_computation.1 | async-start | bytes 524288 | tf_op jit(solution)/shard_map/all_to_all | solution.py:308
  28.1 0.0 copy-start
  28.1 6.3 %shard_map.94 = (bf16[256,768]{1,0:T(8,128)(2,1)}, bf16[256,768]{1,0:T(8,128)(2,1)}) custom-call(s32[16]{0:T(128)S(1)} %copy-done.2, bf16[384,512]{1,0:T(8,128)(2,1)S(1)} %get-tuple-element.25.mine_ref, bf16[768,512]{1,0:T(8,128)(2,1)S(1)} %collective-permute-done.other_ref), custom_call_target="tpu_custom_call" | custom-call | flops 5000000000 | tf_op jit(solution)/shard_map/pallas_call | solution.py:296
  34.4 2.4 %all-to-all-done.1.eight_ref = bf16[8,32,512]{2,1,0:T(8,128)(2,1)S(1)} async-done(((bf16[8,32,512]{2,1,0:T(8,128)(2,1)}), bf16[8,32,512]{2,1,0:T(8,128)(2,1)S(1)}, u32[]{:S(2)}, u32[]{:S(2)}) %all-to-all-start.1) | async-done | bytes 262176 | tf_op jit(solution)/shard_map/all_to_all | solution.py:308
  36.8 0.0 copy-done
  36.8 4.4 %shard_map.96 = bf16[16,144,128]{2,1,0:T(8,128)(2,1)} custom-call(s32[16]{0:T(128)S(1)} %copy-done.2, bf16[256,768]{1,0:T(8,128)(2,1)S(1)} %bitcast.13, bf16[768,512]{1,0:T(8,128)(2,1)S(1)} %collective-permute-done.other_ref, bf16[4,64,512]{2,1,0:T(8,128)(2,1)S(1)} %all-to-all-done.four_ref, bf16[8,32,512]{2,1,0:T(8,128)(2,1)S(1)} %all-to-all-done.1.eight_ref, ...), custom_call_target="tpu_custom_call" | custom-call | flops 2000000000 | tf_op jit(solution)/shard_map/pallas_call | solution.py:296
  41.2 3.8 %all-to-all-start.2 = ((bf16[16,144,128]{2,1,0:T(8,128)(2,1)}), bf16[16,144,128]{2,1,0:T(8,128)(2,1)S(1)}, u32[]{:S(2)}, u32[]{:S(2)}) async-start(bf16[16,144,128]{2,1,0:T(8,128)(2,1)} %shard_map.96), calls=%async_computation.2 | async-start | bytes 1179648 | tf_op jit(solution)/shard_map/all_to_all | solution.py:351
  45.0 5.1 %shard_map.97 = (bf16[256,768]{1,0:T(8,128)(2,1)}, bf16[256,768]{1,0:T(8,128)(2,1)}) custom-call(s32[16]{0:T(128)S(1)} %copy-done.2, bf16[4,64,512]{2,1,0:T(8,128)(2,1)S(1)} %all-to-all-done.four_ref, bf16[8,32,512]{2,1,0:T(8,128)(2,1)S(1)} %all-to-all-done.1.eight_ref), custom_call_target="tpu_custom_call" | custom-call | flops 5000000000 | tf_op jit(solution)/shard_map/pallas_call | solution.py:296
  50.1 0.0 copy-start.3
  50.1 0.0 copy-start.4
  50.1 5.5 %all-to-all-done.2 = bf16[16,144,128]{2,1,0:T(8,128)(2,1)S(1)} async-done(((bf16[16,144,128]{2,1,0:T(8,128)(2,1)}), bf16[16,144,128]{2,1,0:T(8,128)(2,1)S(1)}, u32[]{:S(2)}, u32[]{:S(2)}) %all-to-all-start.2) | async-done | bytes 589856 | tf_op jit(solution)/shard_map/all_to_all | solution.py:351
  55.7 0.1 reduce_sum.21
  55.7 3.7 %all-gather = bf16[288,128]{1,0:T(8,128)(2,1)S(1)} all-gather(bf16[144,128]{1,0:T(8,128)(2,1)S(1)} %reduce_sum.21), channel_id=2, replica_groups={{0,1},{2,3},{4,5},{6,7},{8,9},{10,11},{12,13},{14,15},{16,17},{18,19},{..., dimensions={0}, use_global_device_ids=true | all-gather | bytes 110592 | tf_op jit(solution)/shard_map/all_gather | solution.py:312
  59.4 0.9 %shard_map.98 = bf16[256,128]{1,0:T(8,128)(2,1)} custom-call(bf16[2,144,128]{2,1,0:T(8,128)(2,1)S(1)} %bitcast.14), custom_call_target="tpu_custom_call" | custom-call | tf_op jit(solution)/shard_map/pallas_call | solution.py:296
  60.4 12.8 %all-to-all-start.3 = ((bf16[16,16,128]{2,1,0:T(8,128)(2,1)}), bf16[16,16,128]{2,1,0:T(8,128)(2,1)S(1)}, u32[]{:S(2)}, u32[]{:S(2)}) async-start(bf16[16,16,128]{2,1,0:T(8,128)(2,1)} %bitcast.10), calls=%async_computation.3 | async-start | bytes 131072 | tf_op jit(solution)/shard_map/all_to_all | solution.py:308
  73.2 0.0 copy-done.3
  73.2 2.8 %all-gather.1 = bf16[512,768]{1,0:T(8,128)(2,1)} all-gather(bf16[256,768]{1,0:T(8,128)(2,1)S(1)} %copy-done.3), channel_id=3, replica_groups={{0,1},{2,3},{4,5},{6,7},{8,9},{10,11},{12,13},{14,15},{16,17},{18,19},{..., dimensions={0}, use_global_device_ids=true | all-gather | bytes 1179648 | tf_op jit(solution)/shard_map/all_gather | solution.py:312
  75.9 0.0 copy-done.4
  75.9 2.5 %all-gather.2 = bf16[512,768]{1,0:T(8,128)(2,1)} all-gather(bf16[256,768]{1,0:T(8,128)(2,1)S(1)} %copy-done.4), channel_id=4, replica_groups={{0,1},{2,3},{4,5},{6,7},{8,9},{10,11},{12,13},{14,15},{16,17},{18,19},{..., dimensions={0}, use_global_device_ids=true | all-gather | bytes 1179648 | tf_op jit(solution)/shard_map/all_gather | solution.py:312
  78.4 3.1 %shard_map.99 = (bf16[256,768]{1,0:T(8,128)(2,1)}, bf16[256,768]{1,0:T(8,128)(2,1)}, bf16[256,768]{1,0:T(8,128)(2,1)}) custom-call(bf16[256,768]{1,0:T(8,128)(2,1)} %get-tuple-element.27.near_hbm, bf16[256,768]{1,0:T(8,128)(2,1)} %get-tuple-element.36.far_hbm, bf16[2,256,768]{2,1,0:T(8,128)(2,1)} %bitcast.15, bf16[2,256,768]{2,1,0:T(8,128)(2,1)} %bitcast.16), custom_call_target="tpu_custom_call" | custom-call | flops 2000000000 | tf_op jit(solution)/shard_map/pallas_call | solution.py:296
  81.5 3.4 %all-to-all-done.3 = bf16[16,16,128]{2,1,0:T(8,128)(2,1)S(1)} async-done(((bf16[16,16,128]{2,1,0:T(8,128)(2,1)}), bf16[16,16,128]{2,1,0:T(8,128)(2,1)S(1)}, u32[]{:S(2)}, u32[]{:S(2)}) %all-to-all-start.3) | async-done | bytes 65568 | tf_op jit(solution)/shard_map/all_to_all | solution.py:308
  84.9 0.6 convert_reduce_fusion
Async XLA Ops:
  0.6 0.7 copy-start.1
  1.3 17.5 %copy-start.2 = (s32[16]{0:T(128)S(1)}, s32[16]{0:T(128)}, u32[]{:S(2)}) copy-start(s32[16]{0:T(128)} %off_ref.9) | copy-start | bytes 196
  6.5 12.2 %collective-permute-start = (bf16[768,512]{1,0:T(8,128)(2,1)S(1)}, bf16[768,512]{1,0:T(8,128)(2,1)S(1)}, u32[]{:S(2)}, u32[]{:S(2)}) collective-permute-start(bf16[768,512]{1,0:T(8,128)(2,1)S(1)} %get-tuple-element.26), channel_id=1, source_target_pairs={{0,1},{1,0},{2,3},{3,2},{4,5},{5,4},{6,7},{7,6},{8,9},{9,8},{10,11... | collective-permute-start | bytes 2359304 | tf_op jit(solution)/shard_map/ppermute | solution.py:316
  15.3 8.6 %all-to-all-start = ((bf16[4,64,512]{2,1,0:T(8,128)(2,1)}), bf16[4,64,512]{2,1,0:T(8,128)(2,1)S(1)}, u32[]{:S(2)}, u32[]{:S(2)}) async-start(bf16[4,64,512]{2,1,0:T(8,128)(2,1)} %get-tuple-element.28), calls=%async_computation | async-start | bytes 524288 | tf_op jit(solution)/shard_map/all_to_all | solution.py:308
  23.9 12.9 %all-to-all-start.1 = ((bf16[8,32,512]{2,1,0:T(8,128)(2,1)}), bf16[8,32,512]{2,1,0:T(8,128)(2,1)S(1)}, u32[]{:S(2)}, u32[]{:S(2)}) async-start(bf16[8,32,512]{2,1,0:T(8,128)(2,1)} %get-tuple-element.30), calls=%async_computation.1 | async-start | bytes 524288 | tf_op jit(solution)/shard_map/all_to_all | solution.py:308
  28.1 8.7 %copy-start = (bf16[1,256,768]{2,1,0:T(8,128)(2,1)S(1)}, bf16[1,256,768]{2,1,0:T(8,128)(2,1)}, u32[]{:S(2)}) copy-start(bf16[1,256,768]{2,1,0:T(8,128)(2,1)} %param.9) | copy-start | bytes 1179652
  41.2 14.4 %all-to-all-start.2 = ((bf16[16,144,128]{2,1,0:T(8,128)(2,1)}), bf16[16,144,128]{2,1,0:T(8,128)(2,1)S(1)}, u32[]{:S(2)}, u32[]{:S(2)}) async-start(bf16[16,144,128]{2,1,0:T(8,128)(2,1)} %shard_map.96), calls=%async_computation.2 | async-start | bytes 1179648 | tf_op jit(solution)/shard_map/all_to_all | solution.py:351
  50.1 23.0 %copy-start.3 = (bf16[256,768]{1,0:T(8,128)(2,1)S(1)}, bf16[256,768]{1,0:T(8,128)(2,1)}, u32[]{:S(2)}) copy-start(bf16[256,768]{1,0:T(8,128)(2,1)} %get-tuple-element.40) | copy-start | bytes 1179652
  50.1 25.8 %copy-start.4 = (bf16[256,768]{1,0:T(8,128)(2,1)S(1)}, bf16[256,768]{1,0:T(8,128)(2,1)}, u32[]{:S(2)}) copy-start(bf16[256,768]{1,0:T(8,128)(2,1)} %get-tuple-element.41) | copy-start | bytes 1179652
  60.4 24.5 %all-to-all-start.3 = ((bf16[16,16,128]{2,1,0:T(8,128)(2,1)}), bf16[16,16,128]{2,1,0:T(8,128)(2,1)S(1)}, u32[]{:S(2)}, u32[]{:S(2)}) async-start(bf16[16,16,128]{2,1,0:T(8,128)(2,1)} %bitcast.10), calls=%async_computation.3 | async-start | bytes 131072 | tf_op jit(solution)/shard_map/all_to_all | solution.py:308

commit v3 on v2

v3 whole, which is shorter than its diff:
```python
import math

import jax
import jax.numpy as jnp
from jax import lax
from jax.experimental import pallas as pl
from jax.experimental.pallas import tpu as pltpu
from jax.sharding import PartitionSpec as P

LEVELS = 4
HEADS = 16
HEAD_WIDTH = 48
PAIR_WIDTH = 2 * HEAD_WIDTH
LEVEL_WIDTH = 4 * HEAD_WIDTH
LANES = 128
ROWS = 256
MODEL = 768
GRAD_LANES = 3 * LANES
SENT = 448
SCALE = 1.0 / math.sqrt(HEAD_WIDTH)
BF = jnp.bfloat16
F32 = jnp.float32
VMEM_LIMIT = 24 * 1024 * 1024


def groups_over(bits, count):
    found = {}
    for index in range(count):
        rest = index
        for bit in bits:
            rest &= ~(1 << bit)
        found.setdefault(rest, []).append(index)
    return list(found.values())


def mm(a, b):
    return jnp.dot(a, b, preferred_element_type=F32)


def mm_nt(a, b):
    return lax.dot_general(a, b, (((1,), (1,)), ((), ())), preferred_element_type=F32)


def mm_tn(a, b):
    return lax.dot_general(a, b, (((0,), (0,)), ((), ())), preferred_element_type=F32)


def iota(shape, dim):
    return lax.broadcasted_iota(jnp.int32, shape, dim)


def one_hot(condition):
    return jnp.where(condition, 1.0, 0.0).astype(BF)


def first_head(shape):
    return (iota(shape, 1) & (LANES - 1)) < HEAD_WIDTH


def pack_kernel(
    off_ref, q_hbm, k_hbm, v_hbm, c_hbm, w_hbm, mine_ref, other_ref, eight_ref, wide, q_ref, k_ref, v_ref, c_ref, w_ref, sems
):
    moves = start_all(((c_hbm, c_ref), (w_hbm, w_ref), (q_hbm, q_ref), (k_hbm, k_ref), (v_hbm, v_ref)), sems)
    core = lax.axis_index("ctx") & 1
    wide[...] = jnp.zeros_like(wide)
    moves[0].wait()
    cotangent = c_ref[...]
    half_rows = ROWS // 2
    other_ref[SENT:704, :] = cotangent[:, :512]
    other_ref[704:832, 0:256] = cotangent[:half_rows, 512:]
    other_ref[704:832, 256:512] = cotangent[half_rows:, 512:]
    moves[1].wait()
    grad = mm_nt(cotangent, w_ref[...]).astype(BF)
    for place, rows_ref in ((0, q_ref), (1, k_ref), (2, v_ref), (3, None)):
        if rows_ref is not None:
            moves[2 + place].wait()
        rows = grad if rows_ref is None else rows_ref[...]
        for half in range(2):
            for level in range(LEVELS):
                start = LEVEL_WIDTH * level + PAIR_WIDTH * half
                wide[half, level, :, LANES * place : LANES * place + PAIR_WIDTH] = rows[:, start : start + PAIR_WIDTH]
    for half in range(2):
        for level in range(1, LEVELS):
            dilation = 1 << level
            count = ROWS // dilation
            target = iota((count, ROWS), 1) - dilation * iota((count, ROWS), 0)
            hits = [
                one_hot(target == (off_ref[4 * level + 2 * half + head] & (dilation - 1))) for head in range(2)
            ]
            picked = mm(jnp.concatenate(hits, axis=0), wide[half, level])
            chosen = jnp.where(first_head((count, 4 * LANES)), picked[:count], picked[count:]).astype(BF)
            if level == 3:
                for chip in range(4):
                    eight_ref[half + 2 * chip] = chosen
            else:
                first = ROWS if level == 1 else 384

                @pl.when(core == half)
                def _(chosen=chosen, first=first, count=count):
                    mine_ref[first : first + count, :] = chosen

                @pl.when(core != half)
                def _(chosen=chosen, first=first, count=count):
                    other_ref[first : first + count, :] = chosen

        @pl.when(core == half)
        def _(half=half):
            mine_ref[0:ROWS, :] = wide[half, 0]

        @pl.when(core != half)
        def _(half=half):
            other_ref[0:ROWS, :] = wide[half, 0]


def attend(packed, backward=True):
    q, k, v, g = (packed[:, LANES * i : LANES * (i + 1)] for i in range(4))
    lane = iota(q.shape, 1)
    zero = jnp.zeros((), BF)
    total = None
    for head in range(2):
        own = (lane >= HEAD_WIDTH * head) & (lane < HEAD_WIDTH * (head + 1))
        qh, kh, vh, gh = (jnp.where(own, part, zero) for part in (q, k, v, g))
        scores = mm_nt(q, kh) * SCALE
        top = jnp.max(scores, axis=1, keepdims=True)
        raw = jnp.exp(scores - top)
        weights = raw * (1.0 / jnp.sum(raw, axis=1, keepdims=True))
        low = weights.astype(BF)
        attended = mm(low, vh).astype(BF)
        parts = [attended]
        if backward:
            row_dots = jnp.sum(gh.astype(F32) * attended.astype(F32), axis=1, keepdims=True)
            grad_scores = (weights * (mm_nt(g, vh) - row_dots)).astype(BF)
            parts += [
                (mm(grad_scores, kh) * SCALE).astype(BF),
                (mm_tn(grad_scores, qh) * SCALE).astype(BF),
                mm_tn(low, gh).astype(BF),
            ]
        total = parts if total is None else [old + new for old, new in zip(total, parts)]
    return jnp.concatenate(total, axis=1) if backward else total[0]


def place_rows(off_ref, done, level):
    position = lax.axis_index("ctx")
    core = position & 1
    dilation = 1 << level
    count = 2 * ROWS
    shape = (count, done.shape[0])
    row = iota(shape, 0)
    if level == 3:
        row = (row ^ (ROWS * core)) + ((position >> 1) & 3) * count
    target = row - dilation * iota(shape, 1)
    hits = [one_hot(target == (off_ref[4 * level + 2 * core + head] & (dilation - 1))) for head in range(2)]
    spread = mm(jnp.concatenate(hits, axis=0), done)
    return jnp.where(first_head((count, done.shape[1])), spread[:count], spread[count:]).astype(BF)


def fold_lanes(rows, level):
    shape = (LANES, LEVELS * PAIR_WIDTH)
    lane = iota(shape, 0)
    return mm(rows, one_hot(iota(shape, 1) == jnp.where(lane < PAIR_WIDTH, lane + PAIR_WIDTH * level, -1)))


def store_grads(target_ref, rows, place):
    target_ref[:, GRAD_LANES * place : GRAD_LANES * (place + 1)] = rows[:, LANES:]


def start_all(pairs, sems):
    moves = [pltpu.make_async_copy(source, target, sems.at[index]) for index, (source, target) in enumerate(pairs)]
    for move in moves:
        move.start()
    return moves


def wait_all(moves):
    for move in moves:
        move.wait()


def first_kernel(off_ref, mine_ref, other_ref, attended_ref, two_ref, keep_hbm, send_hbm, keep_ref, send_ref, sems):
    two_ref[0:64, :] = mine_ref[384:SENT, :]
    two_ref[64:128, :] = other_ref[384:SENT, :]
    packed = jnp.concatenate([mine_ref[ROWS:384, :], other_ref[ROWS:384, :]], axis=0)
    placed = place_rows(off_ref, attend(packed), 1)
    store_grads(keep_ref, placed[:ROWS], 0)
    store_grads(send_ref, placed[ROWS:], 0)
    moves = start_all(((keep_ref, keep_hbm), (send_ref, send_hbm)), sems)
    done = [attend(source[0:ROWS, :], backward=False) for source in (mine_ref, other_ref)]
    folded = fold_lanes(jnp.concatenate(done, axis=0), 0) + fold_lanes(placed[:, :LANES], 1)
    attended_ref[...] = folded.astype(BF)
    wait_all(moves)


def second_kernel(off_ref, eight_ref, old_ref, first_hbm, attended_ref, keep_hbm, send_hbm, keep_ref, send_ref, sems):
    first = start_all(((first_hbm, send_ref.at[:, pl.ds(0, GRAD_LANES)]),), sems)
    placed = place_rows(off_ref, attend(eight_ref[...].reshape(ROWS, 4 * LANES)), 3)
    store_grads(keep_ref, placed[:ROWS], 0)
    store_grads(send_ref, placed[ROWS:], 1)
    attended_ref[...] = old_ref[...] + fold_lanes(placed[:, :LANES], 3).astype(BF)
    wait_all(first)
    wait_all(start_all(((keep_ref, keep_hbm), (send_ref, send_hbm)), sems))


def weight_kernel(off_ref, own_ref, other_ref, two_ref, got_two_ref, attended_ref, weight_ref):
    done = attend(jnp.concatenate([two_ref[...], got_two_ref[...]], axis=0), backward=False)
    folded = attended_ref[...] + fold_lanes(place_rows(off_ref, done[:ROWS // 2], 2), 2).astype(BF)
    narrow = jnp.concatenate([other_ref[704:832, 0:256], other_ref[704:832, 256:512]], axis=0)
    other = jnp.concatenate([other_ref[SENT:704, :], narrow], axis=1)
    part = mm_tn(jnp.concatenate([own_ref[...], other], axis=0), folded).astype(BF)
    for column in range(8):
        rows = part[96 * column : 96 * (column + 1)]
        weight_ref[2 * column, 0:96, :] = rows[:, 0:128]
        weight_ref[2 * column, 96:144, 0:64] = rows[0:48, 128:192]
        weight_ref[2 * column, 96:144, 64:128] = rows[48:96, 128:192]
        weight_ref[2 * column + 1, 0:96, :] = rows[:, 256:384]
        weight_ref[2 * column + 1, 96:144, 0:64] = rows[0:48, 192:256]
        weight_ref[2 * column + 1, 96:144, 64:128] = rows[48:96, 192:256]


def last_kernel(off_ref, mine_ref, other_ref, two_ref, got_two_ref, keep_hbm, send_hbm, keep_ref, send_ref, sems):
    store_grads(keep_ref, attend(mine_ref[0:ROWS, :]), 0)
    store_grads(send_ref, attend(other_ref[0:ROWS, :]), 0)
    done = attend(jnp.concatenate([two_ref[...], got_two_ref[...]], axis=0))
    placed = place_rows(off_ref, done[: ROWS // 2], 2)
    store_grads(keep_ref, placed[:ROWS], 1)
    store_grads(send_ref, placed[ROWS:], 1)
    wait_all(start_all(((keep_ref, keep_hbm), (send_ref, send_hbm)), sems))


def merge_kernel(
    keep1_hbm, keep3_hbm, keep02_hbm, got13_hbm, got02_hbm, dq_hbm, dk_hbm, dv_hbm, keep_ref, got_ref, out_ref, sems
):
    core = lax.axis_index("ctx") & 1
    moves = start_all(
        (
            (keep1_hbm, keep_ref.at[:, pl.ds(GRAD_LANES, GRAD_LANES)]),
            (keep3_hbm, keep_ref.at[:, pl.ds(3 * GRAD_LANES, GRAD_LANES)]),
            (keep02_hbm.at[:, pl.ds(0, GRAD_LANES)], keep_ref.at[:, pl.ds(0, GRAD_LANES)]),
            (keep02_hbm.at[:, pl.ds(GRAD_LANES, GRAD_LANES)], keep_ref.at[:, pl.ds(2 * GRAD_LANES, GRAD_LANES)]),
            (got02_hbm.at[1 - core], got_ref.at[0]),
            (got13_hbm.at[1 - core], got_ref.at[1]),
        ),
        sems,
    )
    wait_all(moves)
    out_moves = []
    for array, out_hbm in enumerate((dq_hbm, dk_hbm, dv_hbm)):
        for own in range(2):

            @pl.when(core == own)
            def _(own=own, array=array):
                for level in range(LEVELS):
                    for half in range(2):
                        start = LEVEL_WIDTH * level + PAIR_WIDTH * half
                        if half == own:
                            lanes = GRAD_LANES * level + LANES * array
                            part = keep_ref[:, lanes : lanes + PAIR_WIDTH]
                        else:
                            lanes = GRAD_LANES * (level // 2) + LANES * array
                            part = got_ref[level % 2, :, lanes : lanes + PAIR_WIDTH]
                        out_ref[array, :, start : start + PAIR_WIDTH] = part

        out_moves.append(pltpu.make_async_copy(out_ref.at[array], out_hbm, sems.at[array]))
        out_moves[-1].start()
    wait_all(out_moves)


def split_kernel(sums_ref, out_ref):
    position = lax.axis_index("ctx")
    core = position & 1
    upper = position >> 5
    shape = (256, LANES)
    row = iota(shape, 0)
    lane = iota(shape, 1)
    inner = row & 15
    source = 24 * (row >> 4) + 12 * core + inner
    second_level = (source >= LEVEL_WIDTH).astype(jnp.int32)
    rest = source - LEVEL_WIDTH * second_level
    second_half = rest >= PAIR_WIDTH
    column = PAIR_WIDTH * second_level + jnp.where(second_half, rest - PAIR_WIDTH, rest)
    wide_first = jnp.where(upper == 0, 0, 64)
    narrow_first = jnp.where(upper == 0, 128, 0)
    in_wide = (lane == column - wide_first) & (inner < 12)
    in_narrow = (lane == column - narrow_first) & (inner < 12)
    out = None
    for half in range(2):
        mine = second_half if half else ~second_half
        wide = one_hot(in_wide & mine)
        narrow = one_hot(in_narrow & mine & (lane < 64))
        sums = sums_ref[half]
        tail = sums[96:144]
        tail_rows = jnp.concatenate([tail, pltpu.roll(tail.astype(F32), 64, 1).astype(BF)], axis=0)
        part = mm_nt(wide, sums[0:96]) + mm_nt(narrow, tail_rows)
        out = part if out is None else out + part
    out_ref[:, 0:96] = out.astype(BF)
    out_ref[:, 96:128] = jnp.zeros((256, 32), BF)


def call(kernel, out_shape, *operands, smem=True, hbm=0, hbm_out=(), scratch=(), flops=0):
    vmem = pl.BlockSpec(memory_space=pltpu.VMEM)
    far = pl.BlockSpec(memory_space=pltpu.HBM)
    specs = [pl.BlockSpec(memory_space=pltpu.SMEM)] * smem
    specs += [vmem] * (len(operands) - smem - hbm) + [far] * hbm
    near = len(operands) - hbm
    operands = operands[:near] + tuple(pltpu.with_memory_space_constraint(x, pltpu.HBM) for x in operands[near:])
    out_specs = vmem
    if isinstance(out_shape, tuple):
        out_shape, out_specs = list(out_shape), [vmem] * len(out_shape)
        for index in hbm_out:
            out_shape[index] = pltpu.HBM(out_shape[index].shape, out_shape[index].dtype)
            out_specs[index] = far
    return pl.pallas_call(
        kernel,
        out_shape=out_shape,
        in_specs=specs,
        out_specs=out_specs,
        scratch_shapes=list(scratch),
        compiler_params=pltpu.CompilerParams(vmem_limit_bytes=VMEM_LIMIT),
        cost_estimate=pl.CostEstimate(flops=flops, bytes_accessed=0, transcendentals=0) if flops else None,
    )(*operands)


def pair_gather(block):
    return lax.all_gather(block, "ctx", axis=0, tiled=False, axis_index_groups=groups_over((0,), 64))


def swap(block, bit):
    return lax.ppermute(block, "ctx", [(index, index ^ (1 << bit)) for index in range(64)])


def local(queries, keys, values, cotangent, out_weight, offsets):
    def bf(*shape):
        return jax.ShapeDtypeStruct(shape, BF)

    def vmem(*shape):
        return pltpu.VMEM(shape, BF)

    def dma(count):
        return pltpu.SemaphoreType.DMA((count,))

    rows = vmem(ROWS, MODEL)
    mine, other, eight = call(
        pack_kernel,
        (bf(SENT, 512), bf(832, 512), bf(8, 32, 512)),
        offsets, queries[0], keys[0], values[0], cotangent[0], out_weight,
        hbm=5,
        scratch=(vmem(2, LEVELS, ROWS, 4 * LANES), rows, rows, rows, rows, vmem(MODEL, MODEL), dma(5)),
    )
    eight = lax.all_to_all(eight, "ctx", 0, 0, tiled=True, axis_index_groups=groups_over((0, 1, 2), 64))
    other = swap(other, 0)

    def grads(*widths):
        return dict(
            hbm_out=tuple(range(-len(widths), 0)),
            scratch=tuple(vmem(ROWS, width) for width in widths) + (dma(2),),
            flops=5_000_000_000,
        )

    one, two = GRAD_LANES, 2 * GRAD_LANES
    attended, own_two, keep1, send1 = call(
        first_kernel,
        (bf(2 * ROWS, 384), bf(128, 512), bf(ROWS, one), bf(ROWS, one)),
        offsets, mine, other,
        **grads(one, one),
    )
    got_two = swap(own_two, 1)
    attended, keep3, send13 = call(
        second_kernel,
        (bf(2 * ROWS, 384), bf(ROWS, one), bf(ROWS, two)),
        offsets, eight, attended, send1,
        hbm=1, **grads(one, two),
    )
    weight_parts = call(
        weight_kernel,
        bf(16, 144, 128),
        offsets, cotangent[0], other, own_two, got_two, attended,
        flops=2_000_000_000,
    )
    weight_parts, mine, other, send13 = lax.optimization_barrier((weight_parts, mine, other, send13))
    plane = [[64 * batch + 32 * top + rest for batch in range(8) for top in range(2)] for rest in range(32)]
    column_parts = lax.all_to_all(weight_parts, ("batch", "ctx"), 0, 0, tiled=True, axis_index_groups=plane)
    keep02, send02 = call(
        last_kernel, (bf(ROWS, two), bf(ROWS, two)), offsets, mine, other, own_two, got_two, **grads(two, two)
    )
    column_parts, got13 = lax.optimization_barrier((column_parts, pair_gather(send13)))
    column_sum = jnp.sum(column_parts.astype(F32), axis=0).astype(BF)
    row_parts = call(split_kernel, bf(256, 128), pair_gather(column_sum), smem=False)
    row_parts, send02 = lax.optimization_barrier((row_parts, send02))
    row_parts = lax.all_to_all(
        row_parts.reshape(16, 16, 128), "ctx", 0, 0, tiled=True, axis_index_groups=groups_over((1, 2, 3, 4), 64)
    )
    weight_grad = jnp.sum(row_parts.astype(F32), axis=0)[:12, :96]
    dq, dk, dv = call(
        merge_kernel,
        (bf(ROWS, MODEL),) * 3,
        keep1, keep3, keep02, got13, pair_gather(send02),
        smem=False, hbm=5, hbm_out=(0, 1, 2),
        scratch=(vmem(ROWS, 4 * one), vmem(2, ROWS, two), vmem(3, ROWS, MODEL), dma(6)),
        flops=2_000_000_000,
    )
    return dq[None], dk[None], dv[None], weight_grad


def solution(mesh):
    rows = P("batch", "ctx", None)
    return jax.shard_map(
        local,
        mesh=mesh,
        in_specs=(rows, rows, rows, rows, P(), P()),
        out_specs=(rows, rows, rows, P("ctx", "batch")),
        check_vma=False,
    )
```

time: 86 us -> 79.4 us (0.923)
  waiting for transfers between devices: 13.5 us -> 8.88 us
  Pallas kernels: 27.9 us -> 25.9 us
  blocking collectives: 8.95 us -> 10.1 us
  starting transfers between devices: 32.9 us -> 31.8 us
    all_to_all x3 -> x2, starting transfers between devices: 20.4 us -> 15.6 us  [the longest x1 12.3 us: local(): lax.all_to_all(row_parts.reshape(16, 16, 128), 'ctx', 0, 0, tiled=True, a...]
    all_to_all x1, waiting for transfers between devices: 5.51 us -> 0.96 us  [local(): lax.all_to_all(weight_parts, ('batch', 'ctx'), 0, 0, tiled=True, axis_ind...]
    ppermute x1 -> x2, starting transfers between devices: 8.79 us -> 12 us  [swap(): lax.ppermute(block, 'ctx', [(index, index ^ 1 << bit) for index in range(...]
    pallas_call x7, Pallas kernels: 27.9 us -> 25.9 us  [call(): pl.pallas_call(kernel, out_shape=out_shape, in_specs=specs, out_specs=out...]
    all_gather x3, blocking collectives: 8.95 us -> 10.1 us  [pair_gather(): lax.all_gather(block, 'ctx', axis=0, tiled=False, axis_index_groups=group...]
    all_to_all x3 -> x2, waiting for transfers between devices: 8.01 us -> 7.92 us  [the longest x1 5.84 us: local(): lax.all_to_all(row_parts.reshape(16, 16, 128), 'ctx', 0, 0, tiled=True, a...]
  transfers between devices with their start and end apart: 5 -> 5, of which waited for: 4 -> 3; matrix products, arithmetic and copies ran while one was open for 0% -> 0% of each run, Pallas kernels for 20% -> 21%
where the time goes in v3:
time: 79.4 us; the launch traced here: 78.9 us
  starting transfers between devices  31.8 us (40%)
  Pallas kernels  25.9 us (33%)
  blocking collectives  10.1 us (13%)
  waiting for transfers between devices  8.88 us (11%)
    pallas_call x7, Pallas kernels, call(): pl.pallas_call(kernel, out_shape=out_shape, in_specs=specs, out_specs=out...  25.9 us
    all_to_all x1, starting transfers between devices, local(): lax.all_to_all(row_parts.reshape(16, 16, 128), 'ctx', 0, 0, tiled=True, a...  12.3 us
    ppermute x2, starting transfers between devices, swap(): lax.ppermute(block, 'ctx', [(index, index ^ 1 << bit) for index in range(...  12 us
    all_gather x3, blocking collectives, pair_gather(): lax.all_gather(block, 'ctx', axis=0, tiled=False, axis_index_groups=group...  10.1 us
    all_to_all x1, waiting for transfers between devices, local(): lax.all_to_all(row_parts.reshape(16, 16, 128), 'ctx', 0, 0, tiled=True, a...  5.84 us
    all_to_all x1, starting transfers between devices, local(): lax.all_to_all(weight_parts, ('batch', 'ctx'), 0, 0, tiled=True, axis_ind...  4.17 us
    all_to_all x1, starting transfers between devices, local(): lax.all_to_all(eight, 'ctx', 0, 0, tiled=True, axis_index_groups=groups_o...  3.38 us
    all_to_all x1, waiting for transfers between devices, local(): lax.all_to_all(eight, 'ctx', 0, 0, tiled=True, axis_index_groups=groups_o...  2.08 us
  transfers between devices with their start and end apart: 5, of which 3 were waited for; matrix products, arithmetic and copies ran while one was open for 0% of the time, Pallas kernels for 21%

profile of v3, /device:TPU:1, one launch (start us, length us, event | category | flops | bytes accessed | tf_op | source)
XLA Modules:
  0.0 78.9 jit_solution(348034801202442933)
XLA Ops:
  0.6 0.0 copy-start.1
  0.6 0.6 copy-done.1
  1.3 0.0 copy-start.2
  1.3 5.6 %shard_map.93 = (bf16[448,512]{1,0:T(8,128)(2,1)S(1)}, bf16[832,512]{1,0:T(8,128)(2,1)S(1)}, bf16[8,32,512]{2,1,0:T(8,128)(2,1)}) custom-call(s32[16]{0:T(128)S(1)} %copy-done.1, bf16[256,768]{1,0:T(8,128)(2,1)} %bitcast.17, bf16[256,768]{1,0:T(8,128)(2,1)} %bitcast.18, bf16[256,768]{1,0:T(8,128)(2,1)} %bitcast.19, bf16[256,768]{1,0:T(8,128)(2,1)} %bitcast.12, ...), custom_call_target="tpu_custom_call" | custom-call | tf_op jit(solution)/shard_map/pallas_call | solution.py:311
  6.9 8.8 %collective-permute-start = (bf16[832,512]{1,0:T(8,128)(2,1)S(1)}, bf16[832,512]{1,0:T(8,128)(2,1)S(1)}, u32[]{:S(2)}, u32[]{:S(2)}) collective-permute-start(bf16[832,512]{1,0:T(8,128)(2,1)S(1)} %get-tuple-element.28), channel_id=1, source_target_pairs={{0,1},{1,0},{2,3},{3,2},{4,5},{5,4},{6,7},{7,6},{8,9},{9,8},{10,11... | collective-permute-start | bytes 2555912 | tf_op jit(solution)/shard_map/ppermute | solution.py:327
  15.7 3.4 %all-to-all-start = ((bf16[8,32,512]{2,1,0:T(8,128)(2,1)}), bf16[8,32,512]{2,1,0:T(8,128)(2,1)S(1)}, u32[]{:S(2)}, u32[]{:S(2)}) async-start(bf16[8,32,512]{2,1,0:T(8,128)(2,1)} %get-tuple-element.30), calls=%async_computation | async-start | bytes 524288 | tf_op jit(solution)/shard_map/all_to_all | solution.py:348
  19.1 0.0 collective-permute-done.other_ref
  19.1 0.0 copy-done.2
  19.1 3.4 %shard_map.94 = (bf16[512,384]{1,0:T(8,128)(2,1)S(1)}, bf16[128,512]{1,0:T(8,128)(2,1)S(1)}, bf16[256,384]{1,0:T(8,128)(2,1)}, bf16[256,384]{1,0:T(8,128)(2,1)}) custom-call(s32[16]{0:T(128)S(1)} %copy-done.2, bf16[448,512]{1,0:T(8,128)(2,1)S(1)} %get-tuple-element.37.mine_ref, bf16[832,512]{1,0:T(8,128)(2,1)S(1)} %collective-permute-done.other_ref), custom_call_target="tpu_custom_call" | custom-call | flops 5000000000 | tf_op jit(solution)/shard_map/pallas_call | solution.py:311
  22.5 3.2 %collective-permute-start.1 = (bf16[128,512]{1,0:T(8,128)(2,1)S(1)}, bf16[128,512]{1,0:T(8,128)(2,1)S(1)}, u32[]{:S(2)}, u32[]{:S(2)}) collective-permute-start(bf16[128,512]{1,0:T(8,128)(2,1)S(1)} %get-tuple-element.34.two_ref), channel_id=1, source_target_pairs={{0,2},{1,3},{2,0},{3,1},{4,6},{5,7},{6,4},{7,5},{8,10},{9,11},{10,... | collective-permute-start | bytes 393224 | tf_op jit(solution)/shard_map/ppermute | solution.py:327
  25.8 2.1 %all-to-all-done.eight_ref = bf16[8,32,512]{2,1,0:T(8,128)(2,1)S(1)} async-done(((bf16[8,32,512]{2,1,0:T(8,128)(2,1)}), bf16[8,32,512]{2,1,0:T(8,128)(2,1)S(1)}, u32[]{:S(2)}, u32[]{:S(2)}) %all-to-all-start) | async-done | bytes 262176 | tf_op jit(solution)/shard_map/all_to_all | solution.py:348
  27.9 0.0 copy-start
  27.9 3.4 %shard_map.95 = (bf16[512,384]{1,0:T(8,128)(2,1)S(1)}, bf16[256,384]{1,0:T(8,128)(2,1)}, bf16[256,768]{1,0:T(8,128)(2,1)}) custom-call(s32[16]{0:T(128)S(1)} %copy-done.2, bf16[8,32,512]{2,1,0:T(8,128)(2,1)S(1)} %all-to-all-done.eight_ref, bf16[512,384]{1,0:T(8,128)(2,1)S(1)} %get-tuple-element.31.old_ref, bf16[256,384]{1,0:T(8,128)(2,1)} %get-tuple-element.32.first_hbm), custom_call_target="tpu_custom_call" | custom-call | flops 5000000000 | tf_op jit(solution)/shard_map/pallas_call | solution.py:311
  31.3 0.0 collective-permute-done.1.got_two_ref
  31.3 0.0 copy-done
  31.3 3.2 %shard_map.96 = bf16[16,144,128]{2,1,0:T(8,128)(2,1)} custom-call(s32[16]{0:T(128)S(1)} %copy-done.2, bf16[256,768]{1,0:T(8,128)(2,1)S(1)} %bitcast.13, bf16[832,512]{1,0:T(8,128)(2,1)S(1)} %collective-permute-done.other_ref, bf16[128,512]{1,0:T(8,128)(2,1)S(1)} %get-tuple-element.34.two_ref, bf16[128,512]{1,0:T(8,128)(2,1)S(1)} %collective-permute-done.1.got_two_ref, ...), custom_call_target="tpu_custom_call" | custom-call | flops 2000000000 | tf_op jit(solution)/shard_map/pallas_call | solution.py:311
  34.5 0.0 copy-start.4
  34.5 4.2 %all-to-all-start.1 = ((bf16[16,144,128]{2,1,0:T(8,128)(2,1)}), bf16[16,144,128]{2,1,0:T(8,128)(2,1)S(1)}, u32[]{:S(2)}, u32[]{:S(2)}) async-start(bf16[16,144,128]{2,1,0:T(8,128)(2,1)} %shard_map.96), calls=%async_computation.1 | async-start | bytes 1179648 | tf_op jit(solution)/shard_map/all_to_all | solution.py:380
  38.7 0.0 copy-done.4
  38.7 3.5 %all-gather = bf16[512,768]{1,0:T(8,128)(2,1)} all-gather(bf16[256,768]{1,0:T(8,128)(2,1)S(1)} %copy-done.4), channel_id=2, replica_groups={{0,1},{2,3},{4,5},{6,7},{8,9},{10,11},{12,13},{14,15},{16,17},{18,19},{..., dimensions={0}, use_global_device_ids=true | all-gather | bytes 1179648 | tf_op jit(solution)/shard_map/all_gather | solution.py:323
  42.2 6.2 %shard_map.97 = (bf16[256,768]{1,0:T(8,128)(2,1)}, bf16[256,768]{1,0:T(8,128)(2,1)}) custom-call(s32[16]{0:T(128)S(1)} %copy-done.2, bf16[448,512]{1,0:T(8,128)(2,1)S(1)} %get-tuple-element.37.mine_ref, bf16[832,512]{1,0:T(8,128)(2,1)S(1)} %collective-permute-done.other_ref, bf16[128,512]{1,0:T(8,128)(2,1)S(1)} %get-tuple-element.34.two_ref, ...), custom_call_target="tpu_custom_call" | custom-call | flops 5000000000 | tf_op jit(solution)/shard_map/pallas_call | solution.py:311
  48.4 0.0 copy-start.3
  48.4 1.0 %all-to-all-done.1 = bf16[16,144,128]{2,1,0:T(8,128)(2,1)S(1)} async-done(((bf16[16,144,128]{2,1,0:T(8,128)(2,1)}), bf16[16,144,128]{2,1,0:T(8,128)(2,1)S(1)}, u32[]{:S(2)}, u32[]{:S(2)}) %all-to-all-start.1) | async-done | bytes 589856 | tf_op jit(solution)/shard_map/all_to_all | solution.py:380
  49.4 0.1 reduce_sum.21
  49.5 3.9 %all-gather.1 = bf16[288,128]{1,0:T(8,128)(2,1)S(1)} all-gather(bf16[144,128]{1,0:T(8,128)(2,1)S(1)} %reduce_sum.21), channel_id=3, replica_groups={{0,1},{2,3},{4,5},{6,7},{8,9},{10,11},{12,13},{14,15},{16,17},{18,19},{..., dimensions={0}, use_global_device_ids=true | all-gather | bytes 110592 | tf_op jit(solution)/shard_map/all_gather | solution.py:323
  53.4 0.9 %shard_map.98 = bf16[256,128]{1,0:T(8,128)(2,1)} custom-call(bf16[2,144,128]{2,1,0:T(8,128)(2,1)S(1)} %bitcast.14), custom_call_target="tpu_custom_call" | custom-call | tf_op jit(solution)/shard_map/pallas_call | solution.py:311
  54.3 12.3 %all-to-all-start.2 = ((bf16[16,16,128]{2,1,0:T(8,128)(2,1)}), bf16[16,16,128]{2,1,0:T(8,128)(2,1)S(1)}, u32[]{:S(2)}, u32[]{:S(2)}) async-start(bf16[16,16,128]{2,1,0:T(8,128)(2,1)} %bitcast.10), calls=%async_computation.2 | async-start | bytes 131072 | tf_op jit(solution)/shard_map/all_to_all | solution.py:388
  66.6 0.0 copy-done.3
  66.6 2.8 %all-gather.2 = bf16[512,768]{1,0:T(8,128)(2,1)} all-gather(bf16[256,768]{1,0:T(8,128)(2,1)S(1)} %copy-done.3), channel_id=4, replica_groups={{0,1},{2,3},{4,5},{6,7},{8,9},{10,11},{12,13},{14,15},{16,17},{18,19},{..., dimensions={0}, use_global_device_ids=true | all-gather | bytes 1179648 | tf_op jit(solution)/shard_map/all_gather | solution.py:323
  69.4 3.1 %shard_map.99 = (bf16[256,768]{1,0:T(8,128)(2,1)}, bf16[256,768]{1,0:T(8,128)(2,1)}, bf16[256,768]{1,0:T(8,128)(2,1)}) custom-call(bf16[256,384]{1,0:T(8,128)(2,1)} %get-tuple-element.29.keep1_hbm, bf16[256,384]{1,0:T(8,128)(2,1)} %get-tuple-element.33.keep3_hbm, bf16[256,768]{1,0:T(8,128)(2,1)} %get-tuple-element.39.keep02_hbm, ...), custom_call_target="tpu_custom_call" | custom-call | flops 2000000000 | tf_op jit(solution)/shard_map/pallas_call | solution.py:311
  72.4 5.8 %all-to-all-done.2 = bf16[16,16,128]{2,1,0:T(8,128)(2,1)S(1)} async-done(((bf16[16,16,128]{2,1,0:T(8,128)(2,1)}), bf16[16,16,128]{2,1,0:T(8,128)(2,1)S(1)}, u32[]{:S(2)}, u32[]{:S(2)}) %all-to-all-start.2) | async-done | bytes 65568 | tf_op jit(solution)/shard_map/all_to_all | solution.py:388
  78.3 0.6 convert_reduce_fusion
Async XLA Ops:
  0.6 0.7 copy-start.1
  1.3 17.8 %copy-start.2 = (s32[16]{0:T(128)S(1)}, s32[16]{0:T(128)}, u32[]{:S(2)}) copy-start(s32[16]{0:T(128)} %off_ref.9) | copy-start | bytes 196
  6.9 12.2 %collective-permute-start = (bf16[832,512]{1,0:T(8,128)(2,1)S(1)}, bf16[832,512]{1,0:T(8,128)(2,1)S(1)}, u32[]{:S(2)}, u32[]{:S(2)}) collective-permute-start(bf16[832,512]{1,0:T(8,128)(2,1)S(1)} %get-tuple-element.28), channel_id=1, source_target_pairs={{0,1},{1,0},{2,3},{3,2},{4,5},{5,4},{6,7},{7,6},{8,9},{9,8},{10,11... | collective-permute-start | bytes 2555912 | tf_op jit(solution)/shard_map/ppermute | solution.py:327
  15.7 12.2 %all-to-all-start = ((bf16[8,32,512]{2,1,0:T(8,128)(2,1)}), bf16[8,32,512]{2,1,0:T(8,128)(2,1)S(1)}, u32[]{:S(2)}, u32[]{:S(2)}) async-start(bf16[8,32,512]{2,1,0:T(8,128)(2,1)} %get-tuple-element.30), calls=%async_computation | async-start | bytes 524288 | tf_op jit(solution)/shard_map/all_to_all | solution.py:348
  22.5 8.8 %collective-permute-start.1 = (bf16[128,512]{1,0:T(8,128)(2,1)S(1)}, bf16[128,512]{1,0:T(8,128)(2,1)S(1)}, u32[]{:S(2)}, u32[]{:S(2)}) collective-permute-start(bf16[128,512]{1,0:T(8,128)(2,1)S(1)} %get-tuple-element.34.two_ref), channel_id=1, source_target_pairs={{0,2},{1,3},{2,0},{3,1},{4,6},{5,7},{6,4},{7,5},{8,10},{9,11},{10,... | collective-permute-start | bytes 393224 | tf_op jit(solution)/shard_map/ppermute | solution.py:327
  27.9 3.5 %copy-start = (bf16[1,256,768]{2,1,0:T(8,128)(2,1)S(1)}, bf16[1,256,768]{2,1,0:T(8,128)(2,1)}, u32[]{:S(2)}) copy-start(bf16[1,256,768]{2,1,0:T(8,128)(2,1)} %param.9) | copy-start | bytes 1179652
  34.5 4.2 %copy-start.4 = (bf16[256,768]{1,0:T(8,128)(2,1)S(1)}, bf16[256,768]{1,0:T(8,128)(2,1)}, u32[]{:S(2)}) copy-start(bf16[256,768]{1,0:T(8,128)(2,1)} %get-tuple-element.41) | copy-start | bytes 1179652
  34.5 14.9 %all-to-all-start.1 = ((bf16[16,144,128]{2,1,0:T(8,128)(2,1)}), bf16[16,144,128]{2,1,0:T(8,128)(2,1)S(1)}, u32[]{:S(2)}, u32[]{:S(2)}) async-start(bf16[16,144,128]{2,1,0:T(8,128)(2,1)} %shard_map.96), calls=%async_computation.1 | async-start | bytes 1179648 | tf_op jit(solution)/shard_map/all_to_all | solution.py:380
  48.4 18.2 %copy-start.3 = (bf16[256,768]{1,0:T(8,128)(2,1)S(1)}, bf16[256,768]{1,0:T(8,128)(2,1)}, u32[]{:S(2)}) copy-start(bf16[256,768]{1,0:T(8,128)(2,1)} %get-tuple-element.45) | copy-start | bytes 1179652
  54.3 23.9 %all-to-all-start.2 = ((bf16[16,16,128]{2,1,0:T(8,128)(2,1)}), bf16[16,16,128]{2,1,0:T(8,128)(2,1)S(1)}, u32[]{:S(2)}, u32[]{:S(2)}) async-start(bf16[16,16,128]{2,1,0:T(8,128)(2,1)} %bitcast.10), calls=%async_computation.2 | async-start | bytes 131072 | tf_op jit(solution)/shard_map/all_to_all | solution.py:388

commit v4 on v3

v4 whole, which is shorter than its diff:
```python
import math

import jax
import jax.numpy as jnp
from jax import lax
from jax.experimental import pallas as pl
from jax.experimental.pallas import tpu as pltpu
from jax.sharding import PartitionSpec as P

LEVELS = 4
HEADS = 16
HEAD_WIDTH = 48
PAIR_WIDTH = 2 * HEAD_WIDTH
LEVEL_WIDTH = 4 * HEAD_WIDTH
LANES = 128
ROWS = 256
MODEL = 768
SENT = 448
SCALE = 1.0 / math.sqrt(HEAD_WIDTH)
BF = jnp.bfloat16
F32 = jnp.float32
VMEM_LIMIT = 24 * 1024 * 1024


def groups_over(bits, count):
    found = {}
    for index in range(count):
        rest = index
        for bit in bits:
            rest &= ~(1 << bit)
        found.setdefault(rest, []).append(index)
    return list(found.values())


def mm(a, b):
    return jnp.dot(a, b, preferred_element_type=F32)


def mm_nt(a, b):
    return lax.dot_general(a, b, (((1,), (1,)), ((), ())), preferred_element_type=F32)


def mm_tn(a, b):
    return lax.dot_general(a, b, (((0,), (0,)), ((), ())), preferred_element_type=F32)


def iota(shape, dim):
    return lax.broadcasted_iota(jnp.int32, shape, dim)


def one_hot(condition):
    return jnp.where(condition, 1.0, 0.0).astype(BF)


def turn(level, half):
    return (LEVEL_WIDTH * level + PAIR_WIDTH * half) & (LANES - 1)


def straight(shape, first):
    return (iota(shape, 1) - first) & (LANES - 1)


def first_head(shape, first):
    return straight(shape, first) < HEAD_WIDTH


def own_lanes(rows, head, first):
    lane = straight(rows.shape, first)
    return jnp.where((lane >= HEAD_WIDTH * head) & (lane < HEAD_WIDTH * (head + 1)), rows, jnp.zeros((), BF))


def start_all(pairs, sems, first=0):
    moves = [
        pltpu.make_async_copy(source, target, sems.at[first + index]) for index, (source, target) in enumerate(pairs)
    ]
    for move in moves:
        move.start()
    return moves


def wait_all(moves):
    for move in moves:
        move.wait()


def pack_kernel(
    off_hbm, q_hbm, k_hbm, v_hbm, c_hbm, w_hbm, tile_ref, mine_ref, other_ref, eight_ref,
    wide, q_ref, k_ref, v_ref, c_ref, w_ref, off_ref, sems,
):
    moves = start_all(
        ((off_hbm, off_ref), (c_hbm, c_ref), (w_hbm, w_ref), (q_hbm, q_ref), (k_hbm, k_ref), (v_hbm, v_ref)), sems
    )
    core = lax.axis_index("ctx") & 1
    moves[0].wait()
    for head in range(HEADS):
        tile_ref[head : head + 1, :] = jnp.full((1, LANES), off_ref[head], jnp.int32)
    hits = {}
    for half in range(2):
        for level in range(1, LEVELS):
            dilation = 1 << level
            count = ROWS // dilation
            target = iota((count, ROWS), 1) - dilation * iota((count, ROWS), 0)
            picked = [one_hot(target == (off_ref[4 * level + 2 * half + head] & (dilation - 1))) for head in range(2)]
            hits[half, level] = jnp.concatenate(picked, axis=0)

    def widen(place, rows):
        for half in range(2):
            for level in range(LEVELS):
                start = LEVEL_WIDTH * level + PAIR_WIDTH * half
                first = turn(level, half)
                block = rows[:, start - first : start - first + LANES]
                if first + PAIR_WIDTH > LANES:
                    later = rows[:, start - first + LANES : start - first + 2 * LANES]
                    block = jnp.where(iota(block.shape, 1) >= first, block, later)
                wide[half, level, :, LANES * place : LANES * (place + 1)] = block

    def select(lanes):
        for half in range(2):
            for level in range(1, LEVELS):
                count = ROWS >> level
                picked = mm(hits[half, level], wide[half, level, :, lanes])
                first = turn(level, half)
                chosen = jnp.where(first_head((count, picked.shape[1]), first), picked[:count], picked[count:])
                if level == 3:
                    for place in range(2):
                        part = pltpu.roll(chosen[:, LANES * place : LANES * (place + 1)], (-first) % LANES, 1)
                        part = part[:, :PAIR_WIDTH].astype(BF)
                        target = PAIR_WIDTH * (lanes.start // LANES + place)
                        eight_ref[half, :, target : target + PAIR_WIDTH] = part
                else:
                    chosen = chosen.astype(BF)
                    target = ROWS if level == 1 else 384

                    @pl.when(core == half)
                    def _(chosen=chosen, target=target, count=count):
                        mine_ref[target : target + count, lanes] = chosen

                    @pl.when(core != half)
                    def _(chosen=chosen, target=target, count=count):
                        other_ref[target : target + count, lanes] = chosen

    moves[1].wait()
    cotangent = c_ref[...]
    half_rows = ROWS // 2
    other_ref[SENT:704, :] = cotangent[:, :512]
    other_ref[704:832, 0:256] = cotangent[:half_rows, 512:]
    other_ref[704:832, 256:512] = cotangent[half_rows:, 512:]
    moves[2].wait()
    widen(0, mm_nt(cotangent, w_ref[...]).astype(BF))
    for place, rows_ref in ((1, q_ref), (2, k_ref), (3, v_ref)):
        moves[2 + place].wait()
        widen(place, rows_ref[...])
        if place != 2:
            select(slice(2 * LANES * (place // 2), 2 * LANES * (place // 2 + 1)))
    for half in range(2):
        for chip in range(1, 4):
            eight_ref[half + 2 * chip] = eight_ref[half]
    for half in range(2):

        @pl.when(core == half)
        def _(half=half):
            mine_ref[0:ROWS, :] = wide[half, 0]

        @pl.when(core != half)
        def _(half=half):
            other_ref[0:ROWS, :] = wide[half, 0]


def lanes_of(packed):
    return tuple(packed[:, LANES * index : LANES * (index + 1)] for index in (1, 2, 3, 0))


def attend(packed, first, queries=ROWS, weights_ref=None, low_ref=None, place=0):
    q, k, v, _ = lanes_of(packed)
    total = None
    for head in range(2):
        scores = mm_nt(q[:queries], own_lanes(k, head, first)) * SCALE
        raw = jnp.exp(scores - jnp.max(scores, axis=1, keepdims=True))
        weights = raw * (1.0 / jnp.sum(raw, axis=1, keepdims=True))
        low = weights.astype(BF)
        if weights_ref is not None:
            weights_ref[place + head] = weights
            low_ref[place + head] = low
        part = mm(low, own_lanes(v, head, first))
        total = part if total is None else total + part
    return total.astype(BF)


def attend_all(units, weights_ref, low_ref, scores_ref):
    done, dots = [], []
    for index, (packed, first) in enumerate(units):
        attended = attend(packed, first, ROWS, weights_ref, low_ref, 2 * index)
        grad = lanes_of(packed)[3]
        done.append(attended)
        for head in range(2):
            product = own_lanes(grad, head, first).astype(F32) * attended.astype(F32)
            dots.append(jnp.sum(product, axis=1, keepdims=True))
    for index, (packed, first) in enumerate(units):
        _, _, v, grad = lanes_of(packed)
        for head in range(2):
            place = 2 * index + head
            grad_weights = mm_nt(grad, own_lanes(v, head, first))
            scores_ref[place] = (weights_ref[place] * (grad_weights - dots[place])).astype(BF)
    grads = []
    for index, (packed, first) in enumerate(units):
        q, k, _, grad = lanes_of(packed)
        dq = dk = dv = None
        for head in range(2):
            place = 2 * index + head
            parts = (
                mm(scores_ref[place], own_lanes(k, head, first)),
                mm_tn(scores_ref[place], own_lanes(q, head, first)),
                mm_tn(low_ref[place], own_lanes(grad, head, first)),
            )
            dq, dk, dv = parts if head == 0 else (dq + parts[0], dk + parts[1], dv + parts[2])
        grads.append(jnp.concatenate([part.astype(BF) for part in (dq * SCALE, dk * SCALE, dv)], axis=1))
    return done, grads


def place_rows(tile_ref, rows, level, half, lane):
    dilation = 1 << level
    count = ROWS // dilation
    offsets = [tile_ref[pl.ds(4 * level + 2 * half + head, 1), :] & (dilation - 1) for head in range(2)]
    if level == 1:
        offset = jnp.concatenate(offsets, axis=1)
    else:
        offset = jnp.where(iota((1, LANES), 1) < count, offsets[0], offsets[1])[:, : 2 * count]
    shape = (ROWS, 2 * count)
    hits = one_hot(iota(shape, 0) - dilation * (iota(shape, 1) & (count - 1)) == offset)
    first = first_head(rows.shape, lane)
    zero = jnp.zeros((), BF)
    stacked = jnp.concatenate([jnp.where(first, rows, zero), jnp.where(first, zero, rows)], axis=0)
    return mm(hits, stacked).astype(BF)


def place_chip(tile_ref, mine, other, level, lane):
    core = lax.axis_index("ctx") & 1
    return jnp.concatenate([place_rows(tile_ref, rows, level, core, lane) for rows in (mine, other)], axis=0)


def fold_lanes(rows, level, first):
    shape = (LANES, LEVELS * PAIR_WIDTH)
    lane = (iota(shape, 0) - first) & (LANES - 1)
    return mm(rows, one_hot(iota(shape, 1) == jnp.where(lane < PAIR_WIDTH, lane + PAIR_WIDTH * level, -1)))


def first_kernel(
    tile_ref, mine_ref, other_ref, attended_ref, keep_hbm, send_hbm, grads_ref, weights_ref, low_ref, scores_ref, sems
):
    core = lax.axis_index("ctx") & 1
    zero_level = [attend(source[0:ROWS, :], turn(0, core)) for source in (mine_ref, other_ref)]
    packed = jnp.concatenate([mine_ref[ROWS:384, :], other_ref[ROWS:384, :]], axis=0)
    (done,), (grads,) = attend_all([(packed, turn(1, core))], weights_ref, low_ref, scores_ref)
    grads_ref[...] = grads
    half = ROWS // 2
    moves = start_all(((grads_ref.at[pl.ds(0, half)], keep_hbm), (grads_ref.at[pl.ds(half, half)], send_hbm)), sems)
    folded = fold_lanes(jnp.concatenate(zero_level, axis=0), 0, turn(0, core))
    folded += fold_lanes(place_chip(tile_ref, done[:half], done[half:], 1, turn(1, core)), 1, turn(1, core))
    attended_ref[...] = folded.astype(BF)
    wait_all(moves)


def second_kernel(
    tile_ref, eight_ref, old_ref, attended_ref, keep_ref, send_ref, done_ref, grads_ref, weights_ref, low_ref, scores_ref
):
    position = lax.axis_index("ctx")
    mine = pl.ds(pl.multiple_of(32 * (position & 7), 32), 32)
    other = pl.ds(pl.multiple_of(32 * ((position & 7) ^ 1), 32), 32)
    narrow = eight_ref[...].reshape(ROWS, 4 * PAIR_WIDTH)
    blank = jnp.zeros((ROWS, LANES - PAIR_WIDTH), BF)
    parts = []
    for place in range(4):
        parts += [narrow[:, PAIR_WIDTH * place : PAIR_WIDTH * (place + 1)], blank]
    (done,), (grads,) = attend_all([(jnp.concatenate(parts, axis=1), 0)], weights_ref, low_ref, scores_ref)
    done_ref[...] = done
    placed = place_chip(tile_ref, done_ref[mine, :], done_ref[other, :], 3, 0)
    attended_ref[...] = old_ref[...] + fold_lanes(placed, 3, 0).astype(BF)
    grads_ref[...] = grads
    keep_ref[...] = grads_ref[mine, :]
    send_ref[...] = grads_ref[other, :]


def weight_kernel(tile_ref, own_ref, other_ref, two_ref, got_two_ref, attended_ref, weight_ref):
    first = turn(2, lax.axis_index("ctx") & 1)
    done = attend(jnp.concatenate([two_ref[...], got_two_ref[...]], axis=0), first, ROWS // 2)
    placed = place_chip(tile_ref, done[:64], done[64:], 2, first)
    folded = attended_ref[...] + fold_lanes(placed, 2, first).astype(BF)
    narrow = jnp.concatenate([other_ref[704:832, 0:256], other_ref[704:832, 256:512]], axis=0)
    other = jnp.concatenate([other_ref[SENT:704, :], narrow], axis=1)
    part = mm_tn(jnp.concatenate([own_ref[...], other], axis=0), folded).astype(BF)
    for column in range(8):
        rows = part[96 * column : 96 * (column + 1)]
        weight_ref[2 * column, 0:96, :] = rows[:, 0:128]
        weight_ref[2 * column, 96:144, 0:64] = rows[0:48, 128:192]
        weight_ref[2 * column, 96:144, 64:128] = rows[48:96, 128:192]
        weight_ref[2 * column + 1, 0:96, :] = rows[:, 256:384]
        weight_ref[2 * column + 1, 96:144, 0:64] = rows[0:48, 192:256]
        weight_ref[2 * column + 1, 96:144, 64:128] = rows[48:96, 192:256]


def last_kernel(
    mine_ref, other_ref, two_ref, got_two_ref, send3_ref, keep_hbm, send_hbm, keep_ref, send_ref, weights_ref, low_ref, scores_ref, sems
):
    two = jnp.concatenate([two_ref[...], got_two_ref[...]], axis=0)
    core = lax.axis_index("ctx") & 1
    units = [(mine_ref[0:ROWS, :], turn(0, core)), (other_ref[0:ROWS, :], turn(0, core)), (two, turn(2, core))]
    _, grads = attend_all(units, weights_ref, low_ref, scores_ref)
    keep_ref[0:ROWS, :] = grads[0]
    send_ref[0:ROWS, :] = grads[1]
    keep_ref[ROWS:320, :] = grads[2][:64]
    send_ref[ROWS:320, :] = grads[2][64:128]
    send_ref[320:352, :] = send3_ref[...]
    wait_all(start_all(((keep_ref, keep_hbm), (send_ref, send_hbm)), sems))


def merge_kernel(
    tile_ref, keep3_ref, keep1_hbm, keep02_hbm, got1_hbm, got023_hbm, dq_hbm, dk_hbm, dv_hbm,
    keep1_ref, keep02_ref, got1_ref, got023_ref, full_ref, out_ref, sems,
):
    core = lax.axis_index("ctx") & 1
    moves = start_all(
        (
            (keep1_hbm, keep1_ref),
            (keep02_hbm, keep02_ref),
            (got1_hbm.at[1 - core], got1_ref),
            (got023_hbm.at[1 - core], got023_ref),
        ),
        sems,
    )
    wait_all(moves)
    for source, (one, two, three) in enumerate(
        (
            (keep1_ref[...], keep02_ref[ROWS:, :], keep3_ref[...]),
            (got1_ref[...], got023_ref[ROWS:320, :], got023_ref[320:, :]),
        )
    ):
        half = 1 - core if source else core
        slots = [three[:, LANES * array : LANES * (array + 1)].astype(F32) for array in range(3)]
        three = jnp.concatenate([pltpu.roll(slot, turn(3, half), 1) for slot in slots], axis=1).astype(BF)
        for level, rows in ((1, one), (2, two), (3, three)):
            full_ref[source, level - 1] = place_rows(tile_ref, rows, level, half, turn(level, half))
    out_moves = []
    lane = iota((ROWS, LANES), 1)
    for array, out_hbm in enumerate((dq_hbm, dk_hbm, dv_hbm)):
        lanes = slice(LANES * array, LANES * (array + 1))
        for own in range(2):

            @pl.when(core == own)
            def _(own=own, array=array, lanes=lanes):
                def piece(index):
                    level, half = index // 2, index % 2
                    if level:
                        return full_ref[int(half != own), level - 1, :, lanes]
                    return (keep02_ref if half == own else got023_ref)[0:ROWS, lanes]

                for block in range(MODEL // LANES):
                    index = LANES * block // PAIR_WIDTH
                    bound = PAIR_WIDTH * (index + 1) - LANES * block
                    out_ref[array, :, LANES * block : LANES * (block + 1)] = jnp.where(
                        lane < bound, piece(index), piece(index + 1)
                    )

        out_moves.append(pltpu.make_async_copy(out_ref.at[array], out_hbm, sems.at[array]))
        out_moves[-1].start()
    wait_all(out_moves)


def split_kernel(sums_ref, out_ref):
    position = lax.axis_index("ctx")
    core = position & 1
    upper = position >> 5
    shape = (256, LANES)
    row = iota(shape, 0)
    lane = iota(shape, 1)
    inner = row & 15
    source = 24 * (row >> 4) + 12 * core + inner
    second_level = (source >= LEVEL_WIDTH).astype(jnp.int32)
    rest = source - LEVEL_WIDTH * second_level
    second_half = rest >= PAIR_WIDTH
    column = PAIR_WIDTH * second_level + jnp.where(second_half, rest - PAIR_WIDTH, rest)
    wide_first = jnp.where(upper == 0, 0, 64)
    narrow_first = jnp.where(upper == 0, 128, 0)
    in_wide = (lane == column - wide_first) & (inner < 12)
    in_narrow = (lane == column - narrow_first) & (inner < 12)
    out = None
    for half in range(2):
        mine = second_half if half else ~second_half
        wide = one_hot(in_wide & mine)
        narrow = one_hot(in_narrow & mine & (lane < 64))
        sums = sums_ref[half]
        tail = sums[96:144]
        tail_rows = jnp.concatenate([tail, pltpu.roll(tail.astype(F32), 64, 1).astype(BF)], axis=0)
        part = mm_nt(wide, sums[0:96]) + mm_nt(narrow, tail_rows)
        out = part if out is None else out + part
    out_ref[:, 0:96] = out.astype(BF)
    out_ref[:, 96:128] = jnp.zeros((256, 32), BF)


def call(kernel, out_shape, *operands, hbm=0, hbm_out=(), scratch=(), flops=0):
    vmem = pl.BlockSpec(memory_space=pltpu.VMEM)
    far = pl.BlockSpec(memory_space=pltpu.HBM)
    near = len(operands) - hbm
    operands = operands[:near] + tuple(pltpu.with_memory_space_constraint(x, pltpu.HBM) for x in operands[near:])
    out_specs = vmem
    if isinstance(out_shape, tuple):
        out_shape, out_specs = list(out_shape), [vmem] * len(out_shape)
        for index in hbm_out:
            out_shape[index] = pltpu.HBM(out_shape[index].shape, out_shape[index].dtype)
            out_specs[index] = far
    return pl.pallas_call(
        kernel,
        out_shape=out_shape,
        in_specs=[vmem] * near + [far] * hbm,
        out_specs=out_specs,
        scratch_shapes=list(scratch),
        compiler_params=pltpu.CompilerParams(vmem_limit_bytes=VMEM_LIMIT),
        cost_estimate=pl.CostEstimate(flops=flops, bytes_accessed=0, transcendentals=0) if flops else None,
    )(*operands)


def pair_gather(block):
    return lax.all_gather(block, "ctx", axis=0, tiled=False, axis_index_groups=groups_over((0,), 64))


def swap(block, bit):
    return lax.ppermute(block, "ctx", [(index, index ^ (1 << bit)) for index in range(64)])


def local(queries, keys, values, cotangent, out_weight, offsets):
    def bf(*shape):
        return jax.ShapeDtypeStruct(shape, BF)

    def vmem(*shape):
        return pltpu.VMEM(shape, BF)

    def dma(count):
        return pltpu.SemaphoreType.DMA((count,))

    def steps(units):
        shape = (2 * units, ROWS, ROWS)
        return (pltpu.VMEM(shape, F32), vmem(*shape), vmem(*shape))

    wide = 3 * LANES
    rows = vmem(ROWS, MODEL)
    tile, mine, other, eight = call(
        pack_kernel,
        (jax.ShapeDtypeStruct((HEADS, LANES), jnp.int32), bf(SENT, 512), bf(832, 512), bf(8, 32, 384)),
        offsets, queries[0], keys[0], values[0], cotangent[0], out_weight,
        hbm=6,
        scratch=(
            vmem(2, LEVELS, ROWS, 4 * LANES), rows, rows, rows, rows, vmem(MODEL, MODEL),
            pltpu.SMEM((HEADS,), jnp.int32), dma(6),
        ),
    )
    eight = lax.all_to_all(eight, "ctx", 0, 0, tiled=True, axis_index_groups=groups_over((0, 1, 2), 64))
    other = swap(other, 0)
    own_two = jnp.concatenate([mine[384:SENT], other[384:SENT]], axis=0)
    got_two = swap(own_two, 1)
    attended, keep1, send1 = call(
        first_kernel,
        (bf(2 * ROWS, 384), bf(128, wide), bf(128, wide)),
        tile, mine, other,
        hbm_out=(1, 2), scratch=(vmem(ROWS, wide), *steps(1), dma(2)), flops=3_000_000_000,
    )
    attended, keep3, send3 = call(
        second_kernel,
        (bf(2 * ROWS, 384), bf(32, wide), bf(32, wide)),
        tile, eight, attended,
        scratch=(vmem(ROWS, LANES), vmem(ROWS, wide), *steps(1)), flops=3_000_000_000,
    )
    weight_parts = call(
        weight_kernel,
        bf(16, 144, 128),
        tile, cotangent[0], other, own_two, got_two, attended,
        flops=2_000_000_000,
    )
    weight_parts, mine, other, send1 = lax.optimization_barrier((weight_parts, mine, other, send1))
    plane = [[64 * batch + 32 * top + rest for batch in range(8) for top in range(2)] for rest in range(32)]
    column_parts = lax.all_to_all(weight_parts, ("batch", "ctx"), 0, 0, tiled=True, axis_index_groups=plane)
    keep02, send023 = call(
        last_kernel,
        (bf(320, wide), bf(352, wide)),
        mine, other, own_two, got_two, send3,
        hbm_out=(0, 1), scratch=(vmem(320, wide), vmem(352, wide), *steps(3), dma(2)), flops=5_000_000_000,
    )
    column_parts, got1 = lax.optimization_barrier((column_parts, pair_gather(send1)))
    column_sum = jnp.sum(column_parts.astype(F32), axis=0).astype(BF)
    row_parts = call(split_kernel, bf(256, 128), pair_gather(column_sum))
    row_parts, send023 = lax.optimization_barrier((row_parts, send023))
    row_parts = lax.all_to_all(
        row_parts.reshape(16, 16, 128), "ctx", 0, 0, tiled=True, axis_index_groups=groups_over((1, 2, 3, 4), 64)
    )
    weight_grad = jnp.sum(row_parts.astype(F32), axis=0)[:12, :96]
    dq, dk, dv = call(
        merge_kernel,
        (bf(ROWS, MODEL),) * 3,
        tile, keep3, keep1, keep02, got1, pair_gather(send023),
        hbm=4, hbm_out=(0, 1, 2),
        scratch=(
            vmem(128, wide), vmem(320, wide), vmem(128, wide), vmem(352, wide),
            vmem(2, 3, ROWS, wide), vmem(3, ROWS, MODEL), dma(4),
        ),
        flops=2_000_000_000,
    )
    return dq[None], dk[None], dv[None], weight_grad


def solution(mesh):
    rows = P("batch", "ctx", None)
    return jax.shard_map(
        local,
        mesh=mesh,
        in_specs=(rows, rows, rows, rows, P(), P()),
        out_specs=(rows, rows, rows, P("ctx", "batch")),
        check_vma=False,
    )
```

time: 79.4 us -> 74.2 us (0.935)
  Pallas kernels: 25.9 us -> 18.4 us
  waiting for transfers between devices: 8.88 us -> 12.8 us
  blocking collectives: 10.1 us -> 9.12 us
    pallas_call x7, Pallas kernels: 25.9 us -> 18.4 us  [call(): pl.pallas_call(kernel, out_shape=out_shape, in_specs=[vmem] * near + [far...]
    all_to_all x1, waiting for transfers between devices: 0.96 us -> 4.99 us  [local(): lax.all_to_all(weight_parts, ('batch', 'ctx'), 0, 0, tiled=True, axis_ind...]
    all_to_all x1, waiting for transfers between devices: 2.08 us -> 0.42 us  [local(): lax.all_to_all(eight, 'ctx', 0, 0, tiled=True, axis_index_groups=groups_o...]
    ppermute x2, waiting for transfers between devices: 0.01 us -> 1.12 us  [swap(): lax.ppermute(block, 'ctx', [(index, index ^ 1 << bit) for index in range(...]
    all_gather x3, blocking collectives: 10.1 us -> 9.12 us  [pair_gather(): lax.all_gather(block, 'ctx', axis=0, tiled=False, axis_index_groups=group...]
  transfers between devices with their start and end apart: 5 -> 5, of which waited for: 3 -> 4; matrix products, arithmetic and copies ran while one was open for 0% -> 0% of each run, Pallas kernels for 21% -> 13%
where the time goes in v4:
time: 74.2 us; the launch traced here: 73.7 us
  starting transfers between devices  31.8 us (43%)
  Pallas kernels  18.4 us (25%)
  waiting for transfers between devices  12.8 us (17%)
  blocking collectives  9.12 us (12%)
  between operations  0.77 us (1%)
    pallas_call x7, Pallas kernels, call(): pl.pallas_call(kernel, out_shape=out_shape, in_specs=[vmem] * near + [far...  18.4 us
    all_to_all x1, starting transfers between devices, local(): lax.all_to_all(row_parts.reshape(16, 16, 128), 'ctx', 0, 0, tiled=True, a...  12.2 us
    ppermute x2, starting transfers between devices, swap(): lax.ppermute(block, 'ctx', [(index, index ^ 1 << bit) for index in range(...  12 us
    all_gather x3, blocking collectives, pair_gather(): lax.all_gather(block, 'ctx', axis=0, tiled=False, axis_index_groups=group...  9.12 us
    all_to_all x1, waiting for transfers between devices, local(): lax.all_to_all(row_parts.reshape(16, 16, 128), 'ctx', 0, 0, tiled=True, a...  6.3 us
    all_to_all x1, waiting for transfers between devices, local(): lax.all_to_all(weight_parts, ('batch', 'ctx'), 0, 0, tiled=True, axis_ind...  4.99 us
    all_to_all x1, starting transfers between devices, local(): lax.all_to_all(weight_parts, ('batch', 'ctx'), 0, 0, tiled=True, axis_ind...  4.19 us
    all_to_all x1, starting transfers between devices, local(): lax.all_to_all(eight, 'ctx', 0, 0, tiled=True, axis_index_groups=groups_o...  3.35 us
  transfers between devices with their start and end apart: 5, of which 4 were waited for; matrix products, arithmetic and copies ran while one was open for 0% of the time, Pallas kernels for 13%

profile of v4, /device:TPU:1, one launch (start us, length us, event | category | flops | bytes accessed | tf_op | source)
XLA Modules:
  0.0 73.7 jit_solution(1272090283155231869)
XLA Ops:
  0.6 5.4 %shard_map.93 = (s32[16,128]{1,0:T(8,128)S(1)}, bf16[448,512]{1,0:T(8,128)(2,1)S(1)}, bf16[832,512]{1,0:T(8,128)(2,1)S(1)}, bf16[8,32,384]{2,1,0:T(8,128)(2,1)}) custom-call(s32[16]{0:T(128)} %off_hbm.1, bf16[256,768]{1,0:T(8,128)(2,1)} %bitcast.16, bf16[256,768]{1,0:T(8,128)(2,1)} %bitcast.17, bf16[256,768]{1,0:T(8,128)(2,1)} %bitcast.18, ...), custom_call_target="tpu_custom_call" | custom-call | tf_op jit(solution)/shard_map/pallas_call | solution.py:410
  6.0 8.8 %collective-permute-start = (bf16[832,512]{1,0:T(8,128)(2,1)S(1)}, bf16[832,512]{1,0:T(8,128)(2,1)S(1)}, u32[]{:S(2)}, u32[]{:S(2)}) collective-permute-start(bf16[832,512]{1,0:T(8,128)(2,1)S(1)} %get-tuple-element.30), channel_id=1, source_target_pairs={{0,1},{1,0},{2,3},{3,2},{4,5},{5,4},{6,7},{7,6},{8,9},{9,8},{10,11... | collective-permute-start | bytes 2555912 | tf_op jit(solution)/shard_map/ppermute | solution.py:426
  14.8 3.4 %all-to-all-start = ((bf16[8,32,384]{2,1,0:T(8,128)(2,1)}), bf16[8,32,384]{2,1,0:T(8,128)(2,1)S(1)}, u32[]{:S(2)}, u32[]{:S(2)}) async-start(bf16[8,32,384]{2,1,0:T(8,128)(2,1)} %get-tuple-element.28), calls=%async_computation | async-start | bytes 393216 | tf_op jit(solution)/shard_map/all_to_all | solution.py:455
  18.2 0.0 collective-permute-done.other_ref
  18.2 3.2 %collective-permute-start.1 = (bf16[128,512]{1,0:T(8,128)(2,1)S(1)}, bf16[128,512]{1,0:T(8,128)(2,1)S(1)}, u32[]{:S(2)}, u32[]{:S(2)}) collective-permute-start(bf16[128,512]{1,0:T(8,128)(2,1)S(1)} %pad_maximum_fusion.two_ref), channel_id=1, source_target_pairs={{0,2},{1,3},{2,0},{3,1},{4,6},{5,7},{6,4},{7,5},{8,10},{9,11},{10,... | collective-permute-start | bytes 393224 | tf_op jit(solution)/shard_map/ppermute | solution.py:426
  21.5 2.7 %shard_map.94 = (bf16[512,384]{1,0:T(8,128)(2,1)S(1)}, bf16[128,384]{1,0:T(8,128)(2,1)}, bf16[128,384]{1,0:T(8,128)(2,1)}) custom-call(s32[16,128]{1,0:T(8,128)S(1)} %get-tuple-element.27.tile_ref, bf16[448,512]{1,0:T(8,128)(2,1)S(1)} %get-tuple-element.36.mine_ref, bf16[832,512]{1,0:T(8,128)(2,1)S(1)} %collective-permute-done.other_ref), custom_call_target="tpu_custom_call" | custom-call | flops 3000000000 | tf_op jit(solution)/shard_map/pallas_call | solution.py:410
  24.2 0.4 all-to-all-done.eight_ref
  24.6 0.0 copy-start
  24.6 1.3 %shard_map.95 = (bf16[512,384]{1,0:T(8,128)(2,1)S(1)}, bf16[32,384]{1,0:T(8,128)(2,1)S(1)}, bf16[32,384]{1,0:T(8,128)(2,1)S(1)}) custom-call(s32[16,128]{1,0:T(8,128)S(1)} %get-tuple-element.27.tile_ref, bf16[8,32,384]{2,1,0:T(8,128)(2,1)S(1)} %all-to-all-done.eight_ref, bf16[512,384]{1,0:T(8,128)(2,1)S(1)} %get-tuple-element.31.old_ref), custom_call_target="tpu_custom_call" | custom-call | flops 3000000000 | tf_op jit(solution)/shard_map/pallas_call | solution.py:410
  25.9 1.1 %collective-permute-done.1.got_two_ref = bf16[128,512]{1,0:T(8,128)(2,1)S(1)} collective-permute-done((bf16[128,512]{1,0:T(8,128)(2,1)S(1)}, bf16[128,512]{1,0:T(8,128)(2,1)S(1)}, u32[]{:S(2)}, u32[]{:S(2)}) %collective-permute-start.1) | collective-permute-done | bytes 131104 | tf_op jit(solution)/shard_map/ppermute | solution.py:426
  27.1 0.0 copy-done
  27.1 2.3 %shard_map.96 = bf16[16,144,128]{2,1,0:T(8,128)(2,1)} custom-call(s32[16,128]{1,0:T(8,128)S(1)} %get-tuple-element.27.tile_ref, bf16[256,768]{1,0:T(8,128)(2,1)S(1)} %bitcast.13, bf16[832,512]{1,0:T(8,128)(2,1)S(1)} %collective-permute-done.other_ref, bf16[128,512]{1,0:T(8,128)(2,1)S(1)} %pad_maximum_fusion.two_ref, ...), custom_call_target="tpu_custom_call" | custom-call | flops 2000000000 | tf_op jit(solution)/shard_map/pallas_call | solution.py:410
  29.3 0.0 copy-start.2
  29.3 4.2 %all-to-all-start.1 = ((bf16[16,144,128]{2,1,0:T(8,128)(2,1)}), bf16[16,144,128]{2,1,0:T(8,128)(2,1)S(1)}, u32[]{:S(2)}, u32[]{:S(2)}) async-start(bf16[16,144,128]{2,1,0:T(8,128)(2,1)} %shard_map.96), calls=%async_computation.1 | async-start | bytes 1179648 | tf_op jit(solution)/shard_map/all_to_all | solution.py:479
  33.5 0.0 copy-done.2
  33.5 2.8 %all-gather = bf16[256,384]{1,0:T(8,128)(2,1)} all-gather(bf16[128,384]{1,0:T(8,128)(2,1)S(1)} %copy-done.2), channel_id=2, replica_groups={{0,1},{2,3},{4,5},{6,7},{8,9},{10,11},{12,13},{14,15},{16,17},{18,19},{..., dimensions={0}, use_global_device_ids=true | all-gather | bytes 294912 | tf_op jit(solution)/shard_map/all_gather | solution.py:422
  36.3 3.0 %shard_map.97 = (bf16[320,384]{1,0:T(8,128)(2,1)}, bf16[352,384]{1,0:T(8,128)(2,1)}) custom-call(bf16[448,512]{1,0:T(8,128)(2,1)S(1)} %get-tuple-element.36.mine_ref, bf16[832,512]{1,0:T(8,128)(2,1)S(1)} %collective-permute-done.other_ref, bf16[128,512]{1,0:T(8,128)(2,1)S(1)} %pad_maximum_fusion.two_ref, ...), custom_call_target="tpu_custom_call" | custom-call | flops 5000000000 | tf_op jit(solution)/shard_map/pallas_call | solution.py:410
  39.4 0.0 copy-start.1
  39.4 5.0 %all-to-all-done.1 = bf16[16,144,128]{2,1,0:T(8,128)(2,1)S(1)} async-done(((bf16[16,144,128]{2,1,0:T(8,128)(2,1)}), bf16[16,144,128]{2,1,0:T(8,128)(2,1)S(1)}, u32[]{:S(2)}, u32[]{:S(2)}) %all-to-all-start.1) | async-done | bytes 589856 | tf_op jit(solution)/shard_map/all_to_all | solution.py:479
  44.4 0.1 reduce_sum.21
  44.5 3.8 %all-gather.1 = bf16[288,128]{1,0:T(8,128)(2,1)S(1)} all-gather(bf16[144,128]{1,0:T(8,128)(2,1)S(1)} %reduce_sum.21), channel_id=3, replica_groups={{0,1},{2,3},{4,5},{6,7},{8,9},{10,11},{12,13},{14,15},{16,17},{18,19},{..., dimensions={0}, use_global_device_ids=true | all-gather | bytes 110592 | tf_op jit(solution)/shard_map/all_gather | solution.py:422
  48.2 0.9 %shard_map.98 = bf16[256,128]{1,0:T(8,128)(2,1)} custom-call(bf16[2,144,128]{2,1,0:T(8,128)(2,1)S(1)} %bitcast.14), custom_call_target="tpu_custom_call" | custom-call | tf_op jit(solution)/shard_map/pallas_call | solution.py:410
  49.1 12.2 %all-to-all-start.2 = ((bf16[16,16,128]{2,1,0:T(8,128)(2,1)}), bf16[16,16,128]{2,1,0:T(8,128)(2,1)S(1)}, u32[]{:S(2)}, u32[]{:S(2)}) async-start(bf16[16,16,128]{2,1,0:T(8,128)(2,1)} %bitcast.10), calls=%async_computation.2 | async-start | bytes 131072 | tf_op jit(solution)/shard_map/all_to_all | solution.py:490
  61.4 0.0 copy-done.1
  61.4 2.6 %all-gather.2 = bf16[704,384]{1,0:T(8,128)(2,1)} all-gather(bf16[352,384]{1,0:T(8,128)(2,1)S(1)} %copy-done.1), channel_id=4, replica_groups={{0,1},{2,3},{4,5},{6,7},{8,9},{10,11},{12,13},{14,15},{16,17},{18,19},{..., dimensions={0}, use_global_device_ids=true | all-gather | bytes 811008 | tf_op jit(solution)/shard_map/all_gather | solution.py:422
  64.0 2.8 %shard_map.99 = (bf16[256,768]{1,0:T(8,128)(2,1)}, bf16[256,768]{1,0:T(8,128)(2,1)}, bf16[256,768]{1,0:T(8,128)(2,1)}) custom-call(s32[16,128]{1,0:T(8,128)S(1)} %get-tuple-element.27.tile_ref, bf16[32,384]{1,0:T(8,128)(2,1)S(1)} %get-tuple-element.32.keep3_ref, bf16[128,384]{1,0:T(8,128)(2,1)} %get-tuple-element.33.keep1_hbm, ...), custom_call_target="tpu_custom_call" | custom-call | flops 2000000000 | tf_op jit(solution)/shard_map/pallas_call | solution.py:410
  66.8 6.3 %all-to-all-done.2 = bf16[16,16,128]{2,1,0:T(8,128)(2,1)S(1)} async-done(((bf16[16,16,128]{2,1,0:T(8,128)(2,1)}), bf16[16,16,128]{2,1,0:T(8,128)(2,1)S(1)}, u32[]{:S(2)}, u32[]{:S(2)}) %all-to-all-start.2) | async-done | bytes 65568 | tf_op jit(solution)/shard_map/all_to_all | solution.py:490
  73.1 0.6 convert_reduce_fusion
  (3 shorter events, 0.0 us)
Async XLA Ops:
  6.0 12.2 %collective-permute-start = (bf16[832,512]{1,0:T(8,128)(2,1)S(1)}, bf16[832,512]{1,0:T(8,128)(2,1)S(1)}, u32[]{:S(2)}, u32[]{:S(2)}) collective-permute-start(bf16[832,512]{1,0:T(8,128)(2,1)S(1)} %get-tuple-element.30), channel_id=1, source_target_pairs={{0,1},{1,0},{2,3},{3,2},{4,5},{5,4},{6,7},{7,6},{8,9},{9,8},{10,11... | collective-permute-start | bytes 2555912 | tf_op jit(solution)/shard_map/ppermute | solution.py:426
  14.8 9.8 %all-to-all-start = ((bf16[8,32,384]{2,1,0:T(8,128)(2,1)}), bf16[8,32,384]{2,1,0:T(8,128)(2,1)S(1)}, u32[]{:S(2)}, u32[]{:S(2)}) async-start(bf16[8,32,384]{2,1,0:T(8,128)(2,1)} %get-tuple-element.28), calls=%async_computation | async-start | bytes 393216 | tf_op jit(solution)/shard_map/all_to_all | solution.py:455
  18.2 8.8 %collective-permute-start.1 = (bf16[128,512]{1,0:T(8,128)(2,1)S(1)}, bf16[128,512]{1,0:T(8,128)(2,1)S(1)}, u32[]{:S(2)}, u32[]{:S(2)}) collective-permute-start(bf16[128,512]{1,0:T(8,128)(2,1)S(1)} %pad_maximum_fusion.two_ref), channel_id=1, source_target_pairs={{0,2},{1,3},{2,0},{3,1},{4,6},{5,7},{6,4},{7,5},{8,10},{9,11},{10,... | collective-permute-start | bytes 393224 | tf_op jit(solution)/shard_map/ppermute | solution.py:426
  24.6 2.5 %copy-start = (bf16[1,256,768]{2,1,0:T(8,128)(2,1)S(1)}, bf16[1,256,768]{2,1,0:T(8,128)(2,1)}, u32[]{:S(2)}) copy-start(bf16[1,256,768]{2,1,0:T(8,128)(2,1)} %param.9) | copy-start | bytes 1179652
  29.3 4.2 %copy-start.2 = (bf16[128,384]{1,0:T(8,128)(2,1)S(1)}, bf16[128,384]{1,0:T(8,128)(2,1)}, u32[]{:S(2)}) copy-start(bf16[128,384]{1,0:T(8,128)(2,1)} %get-tuple-element.41) | copy-start | bytes 294916
  29.3 15.0 %all-to-all-start.1 = ((bf16[16,144,128]{2,1,0:T(8,128)(2,1)}), bf16[16,144,128]{2,1,0:T(8,128)(2,1)S(1)}, u32[]{:S(2)}, u32[]{:S(2)}) async-start(bf16[16,144,128]{2,1,0:T(8,128)(2,1)} %shard_map.96), calls=%async_computation.1 | async-start | bytes 1179648 | tf_op jit(solution)/shard_map/all_to_all | solution.py:479
  39.4 22.0 %copy-start.1 = (bf16[352,384]{1,0:T(8,128)(2,1)S(1)}, bf16[352,384]{1,0:T(8,128)(2,1)}, u32[]{:S(2)}) copy-start(bf16[352,384]{1,0:T(8,128)(2,1)} %get-tuple-element.45) | copy-start | bytes 811012
  49.1 23.9 %all-to-all-start.2 = ((bf16[16,16,128]{2,1,0:T(8,128)(2,1)}), bf16[16,16,128]{2,1,0:T(8,128)(2,1)S(1)}, u32[]{:S(2)}, u32[]{:S(2)}) async-start(bf16[16,16,128]{2,1,0:T(8,128)(2,1)} %bitcast.10), calls=%async_computation.2 | async-start | bytes 131072 | tf_op jit(solution)/shard_map/all_to_all | solution.py:490

commit v5 on v4

--- a/solution.py
+++ b/solution.py
@@ -16,20 +16,22 @@
 ROWS = 256
 MODEL = 768
 SENT = 448
+NEAR_FIRST = 2
+FAR_FIRST = 10
 SCALE = 1.0 / math.sqrt(HEAD_WIDTH)
 BF = jnp.bfloat16
 F32 = jnp.float32
 VMEM_LIMIT = 24 * 1024 * 1024
 
 
-def groups_over(bits, count):
+def groups_over(bits, count, first=0):
     found = {}
     for index in range(count):
         rest = index
         for bit in bits:
             rest &= ~(1 << bit)
         found.setdefault(rest, []).append(index)
-    return list(found.values())
+    return [group[first:] + group[:first] for group in found.values()]
 
 
 def mm(a, b):
@@ -114,6 +116,8 @@
                     block = jnp.where(iota(block.shape, 1) >= first, block, later)
                 wide[half, level, :, LANES * place : LANES * (place + 1)] = block
 
+    turned = {}
+
     def select(lanes):
         for half in range(2):
             for level in range(1, LEVELS):
@@ -121,23 +125,46 @@
                 picked = mm(hits[half, level], wide[half, level, :, lanes])
                 first = turn(level, half)
                 chosen = jnp.where(first_head((count, picked.shape[1]), first), picked[:count], picked[count:])
+                if level == 1:
+                    chosen = chosen.astype(BF)
+
+                    @pl.when(core == half)
+                    def _(chosen=chosen):
+                        mine_ref[ROWS:384, lanes] = chosen
+
+                    @pl.when(core != half)
+                    def _(chosen=chosen):
+                        other_ref[ROWS:384, lanes] = chosen
+
+                    continue
+                for place in range(2):
+                    slot = lanes.start // LANES + place
+                    shift = (PAIR_WIDTH * slot - first) % LANES
+                    part = chosen[:, LANES * place : LANES * (place + 1)]
+                    turned[half, level, slot] = pltpu.roll(part, shift, 1) if shift else part
+
+    def join():
+        for half in range(2):
+            for level in range(2, LEVELS):
+                slots = [turned[half, level, slot] for slot in range(4)]
+                lane = iota(slots[0].shape, 1)
+                blocks = [
+                    jnp.where(lane < PAIR_WIDTH - 32 * block, slots[block], slots[block + 1]).astype(BF)
+                    for block in range(3)
+                ]
+                joined = jnp.concatenate(blocks, axis=1)
                 if level == 3:
-                    for place in range(2):
-                        part = pltpu.roll(chosen[:, LANES * place : LANES * (place + 1)], (-first) % LANES, 1)
-                        part = part[:, :PAIR_WIDTH].astype(BF)
-                        target = PAIR_WIDTH * (lanes.start // LANES + place)
-                        eight_ref[half, :, target : target + PAIR_WIDTH] = part
+                    for chip in range(4):
+                        eight_ref[half + 2 * chip] = joined
                 else:
-                    chosen = chosen.astype(BF)
-                    target = ROWS if level == 1 else 384
 
                     @pl.when(core == half)
-                    def _(chosen=chosen, target=target, count=count):
-                        mine_ref[target : target + count, lanes] = chosen
+                    def _(joined=joined):
+                        mine_ref[384:SENT, 0:384] = joined
 
                     @pl.when(core != half)
-                    def _(chosen=chosen, target=target, count=count):
-                        other_ref[target : target + count, lanes] = chosen
+                    def _(joined=joined):
+                        other_ref[384:SENT, 0:384] = joined
 
     moves[1].wait()
     cotangent = c_ref[...]
@@ -152,9 +179,7 @@
         widen(place, rows_ref[...])
         if place != 2:
             select(slice(2 * LANES * (place // 2), 2 * LANES * (place // 2 + 1)))
-    for half in range(2):
-        for chip in range(1, 4):
-            eight_ref[half + 2 * chip] = eight_ref[half]
+    join()
     for half in range(2):
 
         @pl.when(core == half)
@@ -168,6 +193,14 @@
 
 def lanes_of(packed):
     return tuple(packed[:, LANES * index : LANES * (index + 1)] for index in (1, 2, 3, 0))
+
+
+def spread_lanes(narrow):
+    blank = jnp.zeros((narrow.shape[0], LANES - PAIR_WIDTH), BF)
+    parts = []
+    for place in range(4):
+        parts += [narrow[:, PAIR_WIDTH * place : PAIR_WIDTH * (place + 1)], blank]
+    return jnp.concatenate(parts, axis=1)
 
 
 def attend(packed, first, queries=ROWS, weights_ref=None, low_ref=None, place=0):
@@ -264,14 +297,11 @@
     tile_ref, eight_ref, old_ref, attended_ref, keep_ref, send_ref, done_ref, grads_ref, weights_ref, low_ref, scores_ref
 ):
     position = lax.axis_index("ctx")
-    mine = pl.ds(pl.multiple_of(32 * (position & 7), 32), 32)
-    other = pl.ds(pl.multiple_of(32 * ((position & 7) ^ 1), 32), 32)
-    narrow = eight_ref[...].reshape(ROWS, 4 * PAIR_WIDTH)
-    blank = jnp.zeros((ROWS, LANES - PAIR_WIDTH), BF)
-    parts = []
-    for place in range(4):
-        parts += [narrow[:, PAIR_WIDTH * place : PAIR_WIDTH * (place + 1)], blank]
-    (done,), (grads,) = attend_all([(jnp.concatenate(parts, axis=1), 0)], weights_ref, low_ref, scores_ref)
+    place = (position - NEAR_FIRST) & 7
+    mine = pl.ds(pl.multiple_of(32 * place, 32), 32)
+    other = pl.ds(pl.multiple_of(32 * (place ^ 1), 32), 32)
+    packed = spread_lanes(eight_ref[...].reshape(ROWS, 4 * PAIR_WIDTH))
+    (done,), (grads,) = attend_all([(packed, 0)], weights_ref, low_ref, scores_ref)
     done_ref[...] = done
     placed = place_chip(tile_ref, done_ref[mine, :], done_ref[other, :], 3, 0)
     attended_ref[...] = old_ref[...] + fold_lanes(placed, 3, 0).astype(BF)
@@ -280,30 +310,36 @@
     send_ref[...] = grads_ref[other, :]
 
 
-def weight_kernel(tile_ref, own_ref, other_ref, two_ref, got_two_ref, attended_ref, weight_ref):
-    first = turn(2, lax.axis_index("ctx") & 1)
-    done = attend(jnp.concatenate([two_ref[...], got_two_ref[...]], axis=0), first, ROWS // 2)
-    placed = place_chip(tile_ref, done[:64], done[64:], 2, first)
-    folded = attended_ref[...] + fold_lanes(placed, 2, first).astype(BF)
+def weight_kernel(tile_ref, own_ref, other_ref, two_ref, got_two_ref, attended_ref, weight_hbm, weight_ref, sems):
+    done = attend(spread_lanes(jnp.concatenate([two_ref[...], got_two_ref[...]], axis=0)), 0, ROWS // 2)
+    placed = place_chip(tile_ref, done[:64], done[64:], 2, 0)
+    folded = attended_ref[...] + fold_lanes(placed, 2, 0).astype(BF)
     narrow = jnp.concatenate([other_ref[704:832, 0:256], other_ref[704:832, 256:512]], axis=0)
     other = jnp.concatenate([other_ref[SENT:704, :], narrow], axis=1)
-    part = mm_tn(jnp.concatenate([own_ref[...], other], axis=0), folded).astype(BF)
-    for column in range(8):
-        rows = part[96 * column : 96 * (column + 1)]
-        weight_ref[2 * column, 0:96, :] = rows[:, 0:128]
-        weight_ref[2 * column, 96:144, 0:64] = rows[0:48, 128:192]
-        weight_ref[2 * column, 96:144, 64:128] = rows[48:96, 128:192]
-        weight_ref[2 * column + 1, 0:96, :] = rows[:, 256:384]
-        weight_ref[2 * column + 1, 96:144, 0:64] = rows[0:48, 192:256]
-        weight_ref[2 * column + 1, 96:144, 64:128] = rows[48:96, 192:256]
+    cotangent = jnp.concatenate([own_ref[...], other], axis=0)
+    moves = []
+    for side in range(2):
+        part = mm_tn(cotangent[:, 384 * side : 384 * (side + 1)], folded).astype(BF)
+        for column in range(4):
+            rows = part[96 * column : 96 * (column + 1)]
+            place = 8 * side + 2 * column
+            weight_ref[place, 0:96, :] = rows[:, 0:128]
+            weight_ref[place, 96:144, 0:64] = rows[0:48, 128:192]
+            weight_ref[place, 96:144, 64:128] = rows[48:96, 128:192]
+            weight_ref[place + 1, 0:96, :] = rows[:, 256:384]
+            weight_ref[place + 1, 96:144, 0:64] = rows[0:48, 192:256]
+            weight_ref[place + 1, 96:144, 64:128] = rows[48:96, 192:256]
+        blocks = pl.ds(8 * side, 8)
+        moves += start_all(((weight_ref.at[blocks], weight_hbm.at[blocks]),), sems, side)
+    wait_all(moves)
 
 
 def last_kernel(
     mine_ref, other_ref, two_ref, got_two_ref, send3_ref, keep_hbm, send_hbm, keep_ref, send_ref, weights_ref, low_ref, scores_ref, sems
 ):
-    two = jnp.concatenate([two_ref[...], got_two_ref[...]], axis=0)
+    two = spread_lanes(jnp.concatenate([two_ref[...], got_two_ref[...]], axis=0))
     core = lax.axis_index("ctx") & 1
-    units = [(mine_ref[0:ROWS, :], turn(0, core)), (other_ref[0:ROWS, :], turn(0, core)), (two, turn(2, core))]
+    units = [(mine_ref[0:ROWS, :], turn(0, core)), (other_ref[0:ROWS, :], turn(0, core)), (two, 0)]
     _, grads = attend_all(units, weights_ref, low_ref, scores_ref)
     keep_ref[0:ROWS, :] = grads[0]
     send_ref[0:ROWS, :] = grads[1]
@@ -335,9 +371,10 @@
         )
     ):
         half = 1 - core if source else core
-        slots = [three[:, LANES * array : LANES * (array + 1)].astype(F32) for array in range(3)]
-        three = jnp.concatenate([pltpu.roll(slot, turn(3, half), 1) for slot in slots], axis=1).astype(BF)
         for level, rows in ((1, one), (2, two), (3, three)):
+            if level > 1:
+                slots = [rows[:, LANES * array : LANES * (array + 1)].astype(F32) for array in range(3)]
+                rows = jnp.concatenate([pltpu.roll(slot, turn(level, half), 1) for slot in slots], axis=1).astype(BF)
             full_ref[source, level - 1] = place_rows(tile_ref, rows, level, half, turn(level, half))
     out_moves = []
     lane = iota((ROWS, LANES), 1)
@@ -373,7 +410,7 @@
     row = iota(shape, 0)
     lane = iota(shape, 1)
     inner = row & 15
-    source = 24 * (row >> 4) + 12 * core + inner
+    source = 24 * (((row >> 4) + FAR_FIRST) & 15) + 12 * core + inner
     second_level = (source >= LEVEL_WIDTH).astype(jnp.int32)
     rest = source - LEVEL_WIDTH * second_level
     second_half = rest >= PAIR_WIDTH
@@ -452,9 +489,9 @@
             pltpu.SMEM((HEADS,), jnp.int32), dma(6),
         ),
     )
-    eight = lax.all_to_all(eight, "ctx", 0, 0, tiled=True, axis_index_groups=groups_over((0, 1, 2), 64))
+    eight = lax.all_to_all(eight, "ctx", 0, 0, tiled=True, axis_index_groups=groups_over((0, 1, 2), 64, NEAR_FIRST))
     other = swap(other, 0)
-    own_two = jnp.concatenate([mine[384:SENT], other[384:SENT]], axis=0)
+    own_two = jnp.concatenate([mine[384:SENT, :384], other[384:SENT, :384]], axis=0)
     got_two = swap(own_two, 1)
     attended, keep1, send1 = call(
         first_kernel,
@@ -468,11 +505,11 @@
         tile, eight, attended,
         scratch=(vmem(ROWS, LANES), vmem(ROWS, wide), *steps(1)), flops=3_000_000_000,
     )
-    weight_parts = call(
+    (weight_parts,) = call(
         weight_kernel,
-        bf(16, 144, 128),
+        (bf(16, 144, 128),),
         tile, cotangent[0], other, own_two, got_two, attended,
-        flops=2_000_000_000,
+        hbm_out=(0,), scratch=(vmem(16, 144, 128), dma(2)), flops=2_000_000_000,
     )
     weight_parts, mine, other, send1 = lax.optimization_barrier((weight_parts, mine, other, send1))
     plane = [[64 * batch + 32 * top + rest for batch in range(8) for top in range(2)] for rest in range(32)]
@@ -488,7 +525,7 @@
     row_parts = call(split_kernel, bf(256, 128), pair_gather(column_sum))
     row_parts, send023 = lax.optimization_barrier((row_parts, send023))
     row_parts = lax.all_to_all(
-        row_parts.reshape(16, 16, 128), "ctx", 0, 0, tiled=True, axis_index_groups=groups_over((1, 2, 3, 4), 64)
+        row_parts.reshape(16, 16, 128), "ctx", 0, 0, tiled=True, axis_index_groups=groups_over((1, 2, 3, 4), 64, FAR_FIRST)
     )
     weight_grad = jnp.sum(row_parts.astype(F32), axis=0)[:12, :96]
     dq, dk, dv = call(

time: 74.2 us -> 67.7 us (0.912)
  waiting for transfers between devices: 12.8 us -> 7.45 us
  Pallas kernels: 18.4 us -> 17.6 us
    all_to_all x1, waiting for transfers between devices: 6.3 us -> 0.01 us  [local(): lax.all_to_all(row_parts.reshape(16, 16, 128), 'ctx', 0, 0, tiled=True, a...]
    ppermute x2, starting transfers between devices: 12 us -> 10.7 us  [swap(): lax.ppermute(block, 'ctx', [(index, index ^ 1 << bit) for index in range(...]
    all_to_all x1, starting transfers between devices: 12.2 us -> 13.3 us  [local(): lax.all_to_all(row_parts.reshape(16, 16, 128), 'ctx', 0, 0, tiled=True, a...]
    pallas_call x7, Pallas kernels: 18.4 us -> 17.6 us  [call(): pl.pallas_call(kernel, out_shape=out_shape, in_specs=[vmem] * near + [far...]
  transfers between devices with their start and end apart: 5 -> 5, of which waited for: 4 -> 3; matrix products, arithmetic and copies ran while one was open for 0% -> 0% of each run, Pallas kernels for 13% -> 15%
where the time goes in v5:
time: 67.7 us; the launch traced here: 67.2 us
  starting transfers between devices  31.9 us (47%)
  Pallas kernels  17.6 us (26%)
  blocking collectives  8.67 us (13%)
  waiting for transfers between devices  7.45 us (11%)
  between operations  0.78 us (1%)
  other arithmetic  0.72 us (1%)
    pallas_call x7, Pallas kernels, call(): pl.pallas_call(kernel, out_shape=out_shape, in_specs=[vmem] * near + [far...  17.6 us
    all_to_all x1, starting transfers between devices, local(): lax.all_to_all(row_parts.reshape(16, 16, 128), 'ctx', 0, 0, tiled=True, a...  13.3 us
    ppermute x2, starting transfers between devices, swap(): lax.ppermute(block, 'ctx', [(index, index ^ 1 << bit) for index in range(...  10.7 us
    all_gather x3, blocking collectives, pair_gather(): lax.all_gather(block, 'ctx', axis=0, tiled=False, axis_index_groups=group...  8.67 us
    all_to_all x1, waiting for transfers between devices, local(): lax.all_to_all(weight_parts, ('batch', 'ctx'), 0, 0, tiled=True, axis_ind...  5.66 us
    all_to_all x1, starting transfers between devices, local(): lax.all_to_all(weight_parts, ('batch', 'ctx'), 0, 0, tiled=True, axis_ind...  4.59 us
    all_to_all x1, starting transfers between devices, local(): lax.all_to_all(eight, 'ctx', 0, 0, tiled=True, axis_index_groups=groups_o...  3.35 us
    ppermute x2, waiting for transfers between devices, swap(): lax.ppermute(block, 'ctx', [(index, index ^ 1 << bit) for index in range(...  1.4 us
  transfers between devices with their start and end apart: 5, of which 3 were waited for; matrix products, arithmetic and copies ran while one was open for 0% of the time, Pallas kernels for 15%

profile of v5, /device:TPU:1, one launch (start us, length us, event | category | flops | bytes accessed | tf_op | source)
XLA Modules:
  0.0 67.2 jit_solution(17458960752003128478)
XLA Ops:
  0.6 4.5 %shard_map.93 = (s32[16,128]{1,0:T(8,128)S(1)}, bf16[448,512]{1,0:T(8,128)(2,1)S(1)}, bf16[832,512]{1,0:T(8,128)(2,1)S(1)}, bf16[8,32,384]{2,1,0:T(8,128)(2,1)}) custom-call(s32[16]{0:T(128)} %off_hbm.1, bf16[256,768]{1,0:T(8,128)(2,1)} %bitcast.16, bf16[256,768]{1,0:T(8,128)(2,1)} %bitcast.17, bf16[256,768]{1,0:T(8,128)(2,1)} %bitcast.18, ...), custom_call_target="tpu_custom_call" | custom-call | tf_op jit(solution)/shard_map/pallas_call | solution.py:447
  5.2 8.8 %collective-permute-start = (bf16[832,512]{1,0:T(8,128)(2,1)S(1)}, bf16[832,512]{1,0:T(8,128)(2,1)S(1)}, u32[]{:S(2)}, u32[]{:S(2)}) collective-permute-start(bf16[832,512]{1,0:T(8,128)(2,1)S(1)} %get-tuple-element.30), channel_id=1, source_target_pairs={{0,1},{1,0},{2,3},{3,2},{4,5},{5,4},{6,7},{7,6},{8,9},{9,8},{10,11... | collective-permute-start | bytes 2555912 | tf_op jit(solution)/shard_map/ppermute | solution.py:463
  14.0 3.4 %all-to-all-start = ((bf16[8,32,384]{2,1,0:T(8,128)(2,1)}), bf16[8,32,384]{2,1,0:T(8,128)(2,1)S(1)}, u32[]{:S(2)}, u32[]{:S(2)}) async-start(bf16[8,32,384]{2,1,0:T(8,128)(2,1)} %get-tuple-element.28), calls=%async_computation | async-start | bytes 393216 | tf_op jit(solution)/shard_map/all_to_all | solution.py:492
  17.4 0.0 collective-permute-done.other_ref
  17.4 1.9 %collective-permute-start.1 = (bf16[128,384]{1,0:T(8,128)(2,1)S(1)}, bf16[128,384]{1,0:T(8,128)(2,1)S(1)}, u32[]{:S(2)}, u32[]{:S(2)}) collective-permute-start(bf16[128,384]{1,0:T(8,128)(2,1)S(1)} %pad_maximum_fusion.two_ref), channel_id=1, source_target_pairs={{0,2},{1,3},{2,0},{3,1},{4,6},{5,7},{6,4},{7,5},{8,10},{9,11},{10,... | collective-permute-start | bytes 294920 | tf_op jit(solution)/shard_map/ppermute | solution.py:463
  19.3 2.7 %shard_map.94 = (bf16[512,384]{1,0:T(8,128)(2,1)S(1)}, bf16[128,384]{1,0:T(8,128)(2,1)}, bf16[128,384]{1,0:T(8,128)(2,1)}) custom-call(s32[16,128]{1,0:T(8,128)S(1)} %get-tuple-element.27.tile_ref, bf16[448,512]{1,0:T(8,128)(2,1)S(1)} %get-tuple-element.36.mine_ref, bf16[832,512]{1,0:T(8,128)(2,1)S(1)} %collective-permute-done.other_ref), custom_call_target="tpu_custom_call" | custom-call | flops 3000000000 | tf_op jit(solution)/shard_map/pallas_call | solution.py:447
  22.0 0.4 all-to-all-done.eight_ref
  22.4 0.0 copy-start
  22.4 1.3 %shard_map.95 = (bf16[512,384]{1,0:T(8,128)(2,1)S(1)}, bf16[32,384]{1,0:T(8,128)(2,1)S(1)}, bf16[32,384]{1,0:T(8,128)(2,1)S(1)}) custom-call(s32[16,128]{1,0:T(8,128)S(1)} %get-tuple-element.27.tile_ref, bf16[8,32,384]{2,1,0:T(8,128)(2,1)S(1)} %all-to-all-done.eight_ref, bf16[512,384]{1,0:T(8,128)(2,1)S(1)} %get-tuple-element.31.old_ref), custom_call_target="tpu_custom_call" | custom-call | flops 3000000000 | tf_op jit(solution)/shard_map/pallas_call | solution.py:447
  23.8 1.4 %collective-permute-done.1.got_two_ref = bf16[128,384]{1,0:T(8,128)(2,1)S(1)} collective-permute-done((bf16[128,384]{1,0:T(8,128)(2,1)S(1)}, bf16[128,384]{1,0:T(8,128)(2,1)S(1)}, u32[]{:S(2)}, u32[]{:S(2)}) %collective-permute-start.1) | collective-permute-done | bytes 98336 | tf_op jit(solution)/shard_map/ppermute | solution.py:463
  25.2 0.0 copy-done
  25.2 2.3 %shard_map.96 = bf16[16,144,128]{2,1,0:T(8,128)(2,1)} custom-call(s32[16,128]{1,0:T(8,128)S(1)} %get-tuple-element.27.tile_ref, bf16[256,768]{1,0:T(8,128)(2,1)S(1)} %bitcast.13, bf16[832,512]{1,0:T(8,128)(2,1)S(1)} %collective-permute-done.other_ref, bf16[128,384]{1,0:T(8,128)(2,1)S(1)} %pad_maximum_fusion.two_ref, ...), custom_call_target="tpu_custom_call" | custom-call | flops 2000000000 | tf_op jit(solution)/shard_map/pallas_call | solution.py:447
  27.4 0.0 copy-start.2
  27.4 4.6 %all-to-all-start.1 = ((bf16[16,144,128]{2,1,0:T(8,128)(2,1)}), bf16[16,144,128]{2,1,0:T(8,128)(2,1)S(1)}, u32[]{:S(2)}, u32[]{:S(2)}) async-start(bf16[16,144,128]{2,1,0:T(8,128)(2,1)} %shard_map.96), calls=%async_computation.1 | async-start | bytes 1179648 | tf_op jit(solution)/shard_map/all_to_all | solution.py:516
  32.0 0.0 copy-done.2
  32.1 2.5 %all-gather = bf16[256,384]{1,0:T(8,128)(2,1)} all-gather(bf16[128,384]{1,0:T(8,128)(2,1)S(1)} %copy-done.2), channel_id=2, replica_groups={{0,1},{2,3},{4,5},{6,7},{8,9},{10,11},{12,13},{14,15},{16,17},{18,19},{..., dimensions={0}, use_global_device_ids=true | all-gather | bytes 294912 | tf_op jit(solution)/shard_map/all_gather | solution.py:459
  34.6 3.0 %shard_map.97 = (bf16[320,384]{1,0:T(8,128)(2,1)}, bf16[352,384]{1,0:T(8,128)(2,1)}) custom-call(bf16[448,512]{1,0:T(8,128)(2,1)S(1)} %get-tuple-element.36.mine_ref, bf16[832,512]{1,0:T(8,128)(2,1)S(1)} %collective-permute-done.other_ref, bf16[128,384]{1,0:T(8,128)(2,1)S(1)} %pad_maximum_fusion.two_ref, ...), custom_call_target="tpu_custom_call" | custom-call | flops 5000000000 | tf_op jit(solution)/shard_map/pallas_call | solution.py:447
  37.6 0.0 copy-start.1
  37.6 5.7 %all-to-all-done.1 = bf16[16,144,128]{2,1,0:T(8,128)(2,1)S(1)} async-done(((bf16[16,144,128]{2,1,0:T(8,128)(2,1)}), bf16[16,144,128]{2,1,0:T(8,128)(2,1)S(1)}, u32[]{:S(2)}, u32[]{:S(2)}) %all-to-all-start.1) | async-done | bytes 589856 | tf_op jit(solution)/shard_map/all_to_all | solution.py:516
  43.3 0.1 reduce_sum.21
  43.4 3.3 %all-gather.1 = bf16[288,128]{1,0:T(8,128)(2,1)S(1)} all-gather(bf16[144,128]{1,0:T(8,128)(2,1)S(1)} %reduce_sum.21), channel_id=3, replica_groups={{0,1},{2,3},{4,5},{6,7},{8,9},{10,11},{12,13},{14,15},{16,17},{18,19},{..., dimensions={0}, use_global_device_ids=true | all-gather | bytes 110592 | tf_op jit(solution)/shard_map/all_gather | solution.py:459
  46.7 0.9 %shard_map.98 = bf16[256,128]{1,0:T(8,128)(2,1)} custom-call(bf16[2,144,128]{2,1,0:T(8,128)(2,1)S(1)} %bitcast.14), custom_call_target="tpu_custom_call" | custom-call | tf_op jit(solution)/shard_map/pallas_call | solution.py:447
  47.6 13.3 %all-to-all-start.2 = ((bf16[16,16,128]{2,1,0:T(8,128)(2,1)}), bf16[16,16,128]{2,1,0:T(8,128)(2,1)S(1)}, u32[]{:S(2)}, u32[]{:S(2)}) async-start(bf16[16,16,128]{2,1,0:T(8,128)(2,1)} %bitcast.10), calls=%async_computation.2 | async-start | bytes 131072 | tf_op jit(solution)/shard_map/all_to_all | solution.py:527
  60.9 0.0 copy-done.1
  60.9 2.9 %all-gather.2 = bf16[704,384]{1,0:T(8,128)(2,1)} all-gather(bf16[352,384]{1,0:T(8,128)(2,1)S(1)} %copy-done.1), channel_id=4, replica_groups={{0,1},{2,3},{4,5},{6,7},{8,9},{10,11},{12,13},{14,15},{16,17},{18,19},{..., dimensions={0}, use_global_device_ids=true | all-gather | bytes 811008 | tf_op jit(solution)/shard_map/all_gather | solution.py:459
  63.7 2.8 %shard_map.99 = (bf16[256,768]{1,0:T(8,128)(2,1)}, bf16[256,768]{1,0:T(8,128)(2,1)}, bf16[256,768]{1,0:T(8,128)(2,1)}) custom-call(s32[16,128]{1,0:T(8,128)S(1)} %get-tuple-element.27.tile_ref, bf16[32,384]{1,0:T(8,128)(2,1)S(1)} %get-tuple-element.32.keep3_ref, bf16[128,384]{1,0:T(8,128)(2,1)} %get-tuple-element.33.keep1_hbm, ...), custom_call_target="tpu_custom_call" | custom-call | flops 2000000000 | tf_op jit(solution)/shard_map/pallas_call | solution.py:447
  66.6 0.0 all-to-all-done.2
  66.6 0.6 convert_reduce_fusion
  (3 shorter events, 0.0 us)
Async XLA Ops:
  5.2 12.2 %collective-permute-start = (bf16[832,512]{1,0:T(8,128)(2,1)S(1)}, bf16[832,512]{1,0:T(8,128)(2,1)S(1)}, u32[]{:S(2)}, u32[]{:S(2)}) collective-permute-start(bf16[832,512]{1,0:T(8,128)(2,1)S(1)} %get-tuple-element.30), channel_id=1, source_target_pairs={{0,1},{1,0},{2,3},{3,2},{4,5},{5,4},{6,7},{7,6},{8,9},{9,8},{10,11... | collective-permute-start | bytes 2555912 | tf_op jit(solution)/shard_map/ppermute | solution.py:463
  14.0 8.4 %all-to-all-start = ((bf16[8,32,384]{2,1,0:T(8,128)(2,1)}), bf16[8,32,384]{2,1,0:T(8,128)(2,1)S(1)}, u32[]{:S(2)}, u32[]{:S(2)}) async-start(bf16[8,32,384]{2,1,0:T(8,128)(2,1)} %get-tuple-element.28), calls=%async_computation | async-start | bytes 393216 | tf_op jit(solution)/shard_map/all_to_all | solution.py:492
  17.4 7.8 %collective-permute-start.1 = (bf16[128,384]{1,0:T(8,128)(2,1)S(1)}, bf16[128,384]{1,0:T(8,128)(2,1)S(1)}, u32[]{:S(2)}, u32[]{:S(2)}) collective-permute-start(bf16[128,384]{1,0:T(8,128)(2,1)S(1)} %pad_maximum_fusion.two_ref), channel_id=1, source_target_pairs={{0,2},{1,3},{2,0},{3,1},{4,6},{5,7},{6,4},{7,5},{8,10},{9,11},{10,... | collective-permute-start | bytes 294920 | tf_op jit(solution)/shard_map/ppermute | solution.py:463
  22.4 2.8 %copy-start = (bf16[1,256,768]{2,1,0:T(8,128)(2,1)S(1)}, bf16[1,256,768]{2,1,0:T(8,128)(2,1)}, u32[]{:S(2)}) copy-start(bf16[1,256,768]{2,1,0:T(8,128)(2,1)} %param.9) | copy-start | bytes 1179652
  27.4 4.6 %copy-start.2 = (bf16[128,384]{1,0:T(8,128)(2,1)S(1)}, bf16[128,384]{1,0:T(8,128)(2,1)}, u32[]{:S(2)}) copy-start(bf16[128,384]{1,0:T(8,128)(2,1)} %get-tuple-element.41) | copy-start | bytes 294916
  27.4 15.8 %all-to-all-start.1 = ((bf16[16,144,128]{2,1,0:T(8,128)(2,1)}), bf16[16,144,128]{2,1,0:T(8,128)(2,1)S(1)}, u32[]{:S(2)}, u32[]{:S(2)}) async-start(bf16[16,144,128]{2,1,0:T(8,128)(2,1)} %shard_map.96), calls=%async_computation.1 | async-start | bytes 1179648 | tf_op jit(solution)/shard_map/all_to_all | solution.py:516
  37.6 23.3 %copy-start.1 = (bf16[352,384]{1,0:T(8,128)(2,1)S(1)}, bf16[352,384]{1,0:T(8,128)(2,1)}, u32[]{:S(2)}) copy-start(bf16[352,384]{1,0:T(8,128)(2,1)} %get-tuple-element.45) | copy-start | bytes 811012
  47.6 19.0 %all-to-all-start.2 = ((bf16[16,16,128]{2,1,0:T(8,128)(2,1)}), bf16[16,16,128]{2,1,0:T(8,128)(2,1)S(1)}, u32[]{:S(2)}, u32[]{:S(2)}) async-start(bf16[16,16,128]{2,1,0:T(8,128)(2,1)} %bitcast.10), calls=%async_computation.2 | async-start | bytes 131072 | tf_op jit(solution)/shard_map/all_to_all | solution.py:527

commit v6 on v4

v6 whole, which is shorter than its diff:
```python
import math

import jax
import jax.numpy as jnp
from jax import lax
from jax.experimental import pallas as pl
from jax.experimental.pallas import tpu as pltpu
from jax.sharding import PartitionSpec as P

LEVELS = 4
HEADS = 16
HEAD_WIDTH = 48
PAIR_WIDTH = 2 * HEAD_WIDTH
LEVEL_WIDTH = 4 * HEAD_WIDTH
LANES = 128
ROWS = 256
MODEL = 768
SENT = 448
NEAR_FIRST = 2
PLANE_FIRST = 9
FAR_FIRST = 10
SCALE = 1.0 / math.sqrt(HEAD_WIDTH)
BF = jnp.bfloat16
F32 = jnp.float32
VMEM_LIMIT = 24 * 1024 * 1024


def groups_over(bits, count, first=0):
    found = {}
    for index in range(count):
        rest = index
        for bit in bits:
            rest &= ~(1 << bit)
        found.setdefault(rest, []).append(index)
    return [group[first:] + group[:first] for group in found.values()]


def mm(a, b):
    return jnp.dot(a, b, preferred_element_type=F32)


def mm_nt(a, b):
    return lax.dot_general(a, b, (((1,), (1,)), ((), ())), preferred_element_type=F32)


def mm_tn(a, b):
    return lax.dot_general(a, b, (((0,), (0,)), ((), ())), preferred_element_type=F32)


def iota(shape, dim):
    return lax.broadcasted_iota(jnp.int32, shape, dim)


def one_hot(condition):
    return jnp.where(condition, 1.0, 0.0).astype(BF)


def turn(level, half):
    return (LEVEL_WIDTH * level + PAIR_WIDTH * half) & (LANES - 1)


def straight(shape, first):
    return (iota(shape, 1) - first) & (LANES - 1)


def first_head(shape, first):
    return straight(shape, first) < HEAD_WIDTH


def own_lanes(rows, head, first):
    lane = straight(rows.shape, first)
    return jnp.where((lane >= HEAD_WIDTH * head) & (lane < HEAD_WIDTH * (head + 1)), rows, jnp.zeros((), BF))


def start_all(pairs, sems, first=0):
    moves = [
        pltpu.make_async_copy(source, target, sems.at[first + index]) for index, (source, target) in enumerate(pairs)
    ]
    for move in moves:
        move.start()
    return moves


def wait_all(moves):
    for move in moves:
        move.wait()


def select_rows(wide, offsets, level, first):
    dilation = 1 << level
    count = ROWS // dilation
    target = iota((count, ROWS), 1) - dilation * iota((count, ROWS), 0)
    hits = [one_hot(target == (offset & (dilation - 1))) for offset in offsets]
    picked = mm(jnp.concatenate(hits, axis=0), wide)
    return jnp.where(first_head((count, picked.shape[1]), first), picked[:count], picked[count:])


def join_lanes(chosen, first):
    slots = [
        pltpu.roll(chosen[:, LANES * slot : LANES * (slot + 1)], (PAIR_WIDTH * slot - first) & (LANES - 1), 1)
        for slot in range(4)
    ]
    lane = iota(slots[0].shape, 1)
    blocks = [jnp.where(lane < PAIR_WIDTH - 32 * block, slots[block], slots[block + 1]) for block in range(3)]
    return jnp.concatenate([block.astype(BF) for block in blocks], axis=1)


def pack_kernel(
    off_hbm, q_hbm, k_hbm, v_hbm, c_hbm, w_hbm, tile_ref, wide_ref, eight_ref, last_ref,
    q_ref, k_ref, v_ref, c_ref, w_ref, off_ref, sems,
):
    moves = start_all(
        ((off_hbm, off_ref), (c_hbm, c_ref), (w_hbm, w_ref), (q_hbm, q_ref), (k_hbm, k_ref), (v_hbm, v_ref)), sems
    )

    def widen(place, rows):
        for half in range(2):
            for level in range(LEVELS):
                start = LEVEL_WIDTH * level + PAIR_WIDTH * half
                first = turn(level, half)
                block = rows[:, start - first : start - first + LANES]
                if first + PAIR_WIDTH > LANES:
                    later = rows[:, start - first + LANES : start - first + 2 * LANES]
                    block = jnp.where(iota(block.shape, 1) >= first, block, later)
                lanes = slice(LANES * place, LANES * (place + 1))
                if level == 3:
                    last_ref[half, :, lanes] = block
                else:
                    wide_ref[half, level, :, lanes] = block

    moves[0].wait()
    for head in range(HEADS):
        tile_ref[head : head + 1, :] = jnp.full((1, LANES), off_ref[head], jnp.int32)
    moves[1].wait()
    moves[2].wait()
    widen(0, mm_nt(c_ref[...], w_ref[...]).astype(BF))
    for place, rows_ref in ((1, q_ref), (2, k_ref), (3, v_ref)):
        moves[2 + place].wait()
        widen(place, rows_ref[...])
    for half in range(2):
        offsets = [off_ref[12 + 2 * half + head] for head in range(2)]
        first = turn(3, half)
        joined = join_lanes(select_rows(last_ref[half], offsets, 3, first), first)
        for chip in range(4):
            eight_ref[half + 2 * chip] = joined


def share_kernel(tile_ref, wide_ref, c_ref, mine_ref, other_ref):
    core = lax.axis_index("ctx") & 1
    for target_ref, half in ((mine_ref, core), (other_ref, 1 - core)):
        target_ref[0:ROWS, :] = wide_ref[half, 0]
        for level in (1, 2):
            offsets = [tile_ref[pl.ds(4 * level + 2 * half + head, 1), 0:1] for head in range(2)]
            first = turn(level, half)
            chosen = select_rows(wide_ref[half, level], offsets, level, first)
            if level == 1:
                target_ref[ROWS:384, :] = chosen.astype(BF)
            else:
                target_ref[384:SENT, 0:384] = join_lanes(chosen, first)
    cotangent = c_ref[...]
    half_rows = ROWS // 2
    other_ref[SENT:704, :] = cotangent[:, :512]
    other_ref[704:832, 0:256] = cotangent[:half_rows, 512:]
    other_ref[704:832, 256:512] = cotangent[half_rows:, 512:]


def lanes_of(packed):
    return tuple(packed[:, LANES * index : LANES * (index + 1)] for index in (1, 2, 3, 0))


def spread_lanes(narrow):
    blank = jnp.zeros((narrow.shape[0], LANES - PAIR_WIDTH), BF)
    parts = []
    for place in range(4):
        parts += [narrow[:, PAIR_WIDTH * place : PAIR_WIDTH * (place + 1)], blank]
    return jnp.concatenate(parts, axis=1)


def attend(packed, first, queries=ROWS, weights_ref=None, low_ref=None, place=0):
    q, k, v, _ = lanes_of(packed)
    total = None
    for head in range(2):
        scores = mm_nt(q[:queries], own_lanes(k, head, first)) * SCALE
        raw = jnp.exp(scores - jnp.max(scores, axis=1, keepdims=True))
        weights = raw * (1.0 / jnp.sum(raw, axis=1, keepdims=True))
        low = weights.astype(BF)
        if weights_ref is not None:
            weights_ref[place + head] = weights
            low_ref[place + head] = low
        part = mm(low, own_lanes(v, head, first))
        total = part if total is None else total + part
    return total.astype(BF)


def attend_all(units, weights_ref, low_ref, scores_ref):
    done, dots = [], []
    for index, (packed, first) in enumerate(units):
        attended = attend(packed, first, ROWS, weights_ref, low_ref, 2 * index)
        grad = lanes_of(packed)[3]
        done.append(attended)
        for head in range(2):
            product = own_lanes(grad, head, first).astype(F32) * attended.astype(F32)
            dots.append(jnp.sum(product, axis=1, keepdims=True))
    for index, (packed, first) in enumerate(units):
        _, _, v, grad = lanes_of(packed)
        for head in range(2):
            place = 2 * index + head
            grad_weights = mm_nt(grad, own_lanes(v, head, first))
            scores_ref[place] = (weights_ref[place] * (grad_weights - dots[place])).astype(BF)
    grads = []
    for index, (packed, first) in enumerate(units):
        q, k, _, grad = lanes_of(packed)
        dq = dk = dv = None
        for head in range(2):
            place = 2 * index + head
            parts = (
                mm(scores_ref[place], own_lanes(k, head, first)),
                mm_tn(scores_ref[place], own_lanes(q, head, first)),
                mm_tn(low_ref[place], own_lanes(grad, head, first)),
            )
            dq, dk, dv = parts if head == 0 else (dq + parts[0], dk + parts[1], dv + parts[2])
        grads.append(jnp.concatenate([part.astype(BF) for part in (dq * SCALE, dk * SCALE, dv)], axis=1))
    return done, grads


def place_rows(tile_ref, rows, level, half, lane):
    dilation = 1 << level
    count = ROWS // dilation
    offsets = [tile_ref[pl.ds(4 * level + 2 * half + head, 1), :] & (dilation - 1) for head in range(2)]
    if level == 1:
        offset = jnp.concatenate(offsets, axis=1)
    else:
        offset = jnp.where(iota((1, LANES), 1) < count, offsets[0], offsets[1])[:, : 2 * count]
    shape = (ROWS, 2 * count)
    hits = one_hot(iota(shape, 0) - dilation * (iota(shape, 1) & (count - 1)) == offset)
    first = first_head(rows.shape, lane)
    zero = jnp.zeros((), BF)
    stacked = jnp.concatenate([jnp.where(first, rows, zero), jnp.where(first, zero, rows)], axis=0)
    return mm(hits, stacked).astype(BF)


def place_chip(tile_ref, mine, other, level, lane):
    core = lax.axis_index("ctx") & 1
    return jnp.concatenate([place_rows(tile_ref, rows, level, core, lane) for rows in (mine, other)], axis=0)


def fold_lanes(rows, level, first):
    shape = (LANES, LEVELS * PAIR_WIDTH)
    lane = (iota(shape, 0) - first) & (LANES - 1)
    return mm(rows, one_hot(iota(shape, 1) == jnp.where(lane < PAIR_WIDTH, lane + PAIR_WIDTH * level, -1)))


def level_one(mine_ref, other_ref):
    return jnp.concatenate([mine_ref[ROWS:384, :], other_ref[ROWS:384, :]], axis=0)


def first_kernel(tile_ref, mine_ref, other_ref, attended_ref):
    core = lax.axis_index("ctx") & 1
    zero_level = [attend(source[0:ROWS, :], turn(0, core)) for source in (mine_ref, other_ref)]
    done = attend(level_one(mine_ref, other_ref), turn(1, core))
    half = ROWS // 2
    folded = fold_lanes(jnp.concatenate(zero_level, axis=0), 0, turn(0, core))
    folded += fold_lanes(place_chip(tile_ref, done[:half], done[half:], 1, turn(1, core)), 1, turn(1, core))
    attended_ref[...] = folded.astype(BF)


def own_rows_of_eight():
    place = (lax.axis_index("ctx") - NEAR_FIRST) & 7
    return pl.ds(pl.multiple_of(32 * place, 32), 32), pl.ds(pl.multiple_of(32 * (place ^ 1), 32), 32)


def second_kernel(tile_ref, eight_ref, old_ref, attended_ref, done_ref):
    mine, other = own_rows_of_eight()
    done_ref[...] = attend(spread_lanes(eight_ref[...].reshape(ROWS, 4 * PAIR_WIDTH)), 0)
    placed = place_chip(tile_ref, done_ref[mine, :], done_ref[other, :], 3, 0)
    attended_ref[...] = old_ref[...] + fold_lanes(placed, 3, 0).astype(BF)


def weight_kernel(tile_ref, own_ref, other_ref, two_ref, got_two_ref, attended_ref, weight_ref):
    done = attend(spread_lanes(jnp.concatenate([two_ref[...], got_two_ref[...]], axis=0)), 0, ROWS // 2)
    placed = place_chip(tile_ref, done[:64], done[64:], 2, 0)
    folded = attended_ref[...] + fold_lanes(placed, 2, 0).astype(BF)
    narrow = jnp.concatenate([other_ref[704:832, 0:256], other_ref[704:832, 256:512]], axis=0)
    other = jnp.concatenate([other_ref[SENT:704, :], narrow], axis=1)
    cotangent = jnp.concatenate([own_ref[...], other], axis=0)
    part = mm_tn(cotangent, folded).astype(BF)
    for block in range(16):
        rows = part[96 * (block // 2) : 96 * (block // 2 + 1)]
        place = (block - PLANE_FIRST) % 16
        wide, narrow = (256, 192) if block % 2 else (0, 128)
        weight_ref[place, 0:96, :] = rows[:, wide : wide + 128]
        weight_ref[place, 96:144, 0:64] = rows[0:48, narrow : narrow + 64]
        weight_ref[place, 96:144, 64:128] = rows[48:96, narrow : narrow + 64]


def last_kernel(
    mine_ref, other_ref, two_ref, got_two_ref, eight_ref, keep_hbm, send_ref,
    keep_ref, grads_ref, weights_ref, low_ref, scores_ref, sems,
):
    core = lax.axis_index("ctx") & 1
    two = spread_lanes(jnp.concatenate([two_ref[...], got_two_ref[...]], axis=0))
    units = [
        (mine_ref[0:ROWS, :], turn(0, core)),
        (other_ref[0:ROWS, :], turn(0, core)),
        (level_one(mine_ref, other_ref), turn(1, core)),
        (two, 0),
        (spread_lanes(eight_ref[...].reshape(ROWS, 4 * PAIR_WIDTH)), 0),
    ]
    _, grads = attend_all(units, weights_ref, low_ref, scores_ref)
    grads_ref[...] = grads[4]
    for index, (target_ref, rows) in enumerate(zip((keep_ref, send_ref), own_rows_of_eight())):
        target_ref[0:ROWS, :] = grads[index]
        target_ref[ROWS:384, :] = grads[2][128 * index : 128 * (index + 1)]
        target_ref[384:448, :] = grads[3][64 * index : 64 * (index + 1)]
        target_ref[448:480, :] = grads_ref[rows, :]
    wait_all(start_all(((keep_ref, keep_hbm),), sems))


def merge_kernel(
    tile_ref, keep_hbm, got_hbm, dq_hbm, dk_hbm, dv_hbm, keep_ref, got_ref, full_ref, out_ref, sems
):
    core = lax.axis_index("ctx") & 1
    wait_all(start_all(((keep_hbm, keep_ref), (got_hbm.at[1 - core], got_ref)), sems))
    for source, source_ref in enumerate((keep_ref, got_ref)):
        half = 1 - core if source else core
        for level, rows in ((1, source_ref[ROWS:384, :]), (2, source_ref[384:448, :]), (3, source_ref[448:480, :])):
            if level > 1:
                slots = [rows[:, LANES * array : LANES * (array + 1)].astype(F32) for array in range(3)]
                rows = jnp.concatenate([pltpu.roll(slot, turn(level, half), 1) for slot in slots], axis=1).astype(BF)
            full_ref[source, level - 1] = place_rows(tile_ref, rows, level, half, turn(level, half))
    out_moves = []
    lane = iota((ROWS, LANES), 1)
    for array, out_hbm in enumerate((dq_hbm, dk_hbm, dv_hbm)):
        lanes = slice(LANES * array, LANES * (array + 1))
        for own in range(2):

            @pl.when(core == own)
            def _(own=own, array=array, lanes=lanes):
                def piece(index):
                    level, half = index // 2, index % 2
                    if level:
                        return full_ref[int(half != own), level - 1, :, lanes]
                    return (keep_ref if half == own else got_ref)[0:ROWS, lanes]

                for block in range(MODEL // LANES):
                    index = LANES * block // PAIR_WIDTH
                    bound = PAIR_WIDTH * (index + 1) - LANES * block
                    out_ref[array, :, LANES * block : LANES * (block + 1)] = jnp.where(
                        lane < bound, piece(index), piece(index + 1)
                    )

        out_moves.append(pltpu.make_async_copy(out_ref.at[array], out_hbm, sems.at[array]))
        out_moves[-1].start()
    wait_all(out_moves)


def split_kernel(sums_ref, out_ref):
    position = lax.axis_index("ctx")
    core = position & 1
    upper = position >> 5
    shape = (256, LANES)
    row = iota(shape, 0)
    lane = iota(shape, 1)
    inner = row & 15
    source = 24 * (((row >> 4) + FAR_FIRST) & 15) + 12 * core + inner
    second_level = (source >= LEVEL_WIDTH).astype(jnp.int32)
    rest = source - LEVEL_WIDTH * second_level
    second_half = rest >= PAIR_WIDTH
    column = PAIR_WIDTH * second_level + jnp.where(second_half, rest - PAIR_WIDTH, rest)
    wide_first = jnp.where(upper == 0, 0, 64)
    narrow_first = jnp.where(upper == 0, 128, 0)
    in_wide = (lane == column - wide_first) & (inner < 12)
    in_narrow = (lane == column - narrow_first) & (inner < 12)
    out = None
    for half in range(2):
        mine = second_half if half else ~second_half
        wide = one_hot(in_wide & mine)
        narrow = one_hot(in_narrow & mine & (lane < 64))
        sums = sums_ref[half]
        tail = sums[96:144]
        tail_rows = jnp.concatenate([tail, pltpu.roll(tail.astype(F32), 64, 1).astype(BF)], axis=0)
        part = mm_nt(wide, sums[0:96]) + mm_nt(narrow, tail_rows)
        out = part if out is None else out + part
    out_ref[:, 0:96] = out.astype(BF)
    out_ref[:, 96:128] = jnp.zeros((256, 32), BF)


def call(kernel, out_shape, *operands, hbm=0, hbm_out=(), scratch=(), flops=0):
    vmem = pl.BlockSpec(memory_space=pltpu.VMEM)
    far = pl.BlockSpec(memory_space=pltpu.HBM)
    near = len(operands) - hbm
    operands = operands[:near] + tuple(pltpu.with_memory_space_constraint(x, pltpu.HBM) for x in operands[near:])
    out_specs = vmem
    if isinstance(out_shape, tuple):
        out_shape, out_specs = list(out_shape), [vmem] * len(out_shape)
        for index in hbm_out:
            out_shape[index] = pltpu.HBM(out_shape[index].shape, out_shape[index].dtype)
            out_specs[index] = far
    return pl.pallas_call(
        kernel,
        out_shape=out_shape,
        in_specs=[vmem] * near + [far] * hbm,
        out_specs=out_specs,
        scratch_shapes=list(scratch),
        compiler_params=pltpu.CompilerParams(vmem_limit_bytes=VMEM_LIMIT),
        cost_estimate=pl.CostEstimate(flops=flops, bytes_accessed=0, transcendentals=0) if flops else None,
    )(*operands)


def pair_gather(block):
    return lax.all_gather(block, "ctx", axis=0, tiled=False, axis_index_groups=groups_over((0,), 64))


def swap(block, bit):
    return lax.ppermute(block, "ctx", [(index, index ^ (1 << bit)) for index in range(64)])


def local(queries, keys, values, cotangent, out_weight, offsets):
    def bf(*shape):
        return jax.ShapeDtypeStruct(shape, BF)

    def vmem(*shape):
        return pltpu.VMEM(shape, BF)

    def dma(count):
        return pltpu.SemaphoreType.DMA((count,))

    def steps(units):
        shape = (2 * units, ROWS, ROWS)
        return (pltpu.VMEM(shape, F32), vmem(*shape), vmem(*shape))

    wide = 3 * LANES
    rows = vmem(ROWS, MODEL)
    tile, wide_rows, eight = call(
        pack_kernel,
        (jax.ShapeDtypeStruct((HEADS, LANES), jnp.int32), bf(2, 3, ROWS, 512), bf(8, 32, 384)),
        offsets, queries[0], keys[0], values[0], cotangent[0], out_weight,
        hbm=6,
        scratch=(
            vmem(2, ROWS, 512), rows, rows, rows, rows, vmem(MODEL, MODEL), pltpu.SMEM((HEADS,), jnp.int32), dma(6)
        ),
    )
    eight = lax.all_to_all(
        eight, "ctx", 0, 0, tiled=True, axis_index_groups=groups_over((0, 1, 2), 64, NEAR_FIRST)
    )
    mine, other = call(share_kernel, (bf(SENT, 512), bf(832, 512)), tile, wide_rows, cotangent[0], flops=1_000_000)
    other = swap(other, 0)
    own_two = jnp.concatenate([mine[384:SENT, :384], other[384:SENT, :384]], axis=0)
    got_two = swap(own_two, 1)
    attended = call(first_kernel, bf(2 * ROWS, 384), tile, mine, other, flops=1_000_000)
    attended = call(
        second_kernel, bf(2 * ROWS, 384), tile, eight, attended, scratch=(vmem(ROWS, LANES),), flops=1_000_000_000
    )
    weight_parts = call(
        weight_kernel,
        bf(16, 144, 128),
        tile, cotangent[0], other, own_two, got_two, attended,
        flops=2_000_000_000,
    )
    weight_parts, mine, other = lax.optimization_barrier((weight_parts, mine, other))
    members = [(place + PLANE_FIRST) % 16 for place in range(16)]
    plane = [[64 * (member // 2) + 32 * (member % 2) + rest for member in members] for rest in range(32)]
    column_parts = lax.all_to_all(weight_parts, ("batch", "ctx"), 0, 0, tiled=True, axis_index_groups=plane)
    keep, send = call(
        last_kernel,
        (bf(480, wide), bf(480, wide)),
        mine, other, own_two, got_two, eight,
        hbm_out=(0,), scratch=(vmem(480, wide), vmem(ROWS, wide), *steps(5), dma(1)),
        flops=8_000_000_000,
    )
    column_sum = jnp.sum(column_parts.astype(F32), axis=0).astype(BF)
    row_parts = call(split_kernel, bf(256, 128), pair_gather(column_sum))
    row_parts, send = lax.optimization_barrier((row_parts, send))
    row_parts = lax.all_to_all(
        row_parts.reshape(16, 16, 128), "ctx", 0, 0, tiled=True, axis_index_groups=groups_over((1, 2, 3, 4), 64, FAR_FIRST)
    )
    weight_grad = jnp.sum(row_parts.astype(F32), axis=0)[:12, :96]
    dq, dk, dv = call(
        merge_kernel,
        (bf(ROWS, MODEL),) * 3,
        tile, keep, pair_gather(send),
        hbm=2, hbm_out=(0, 1, 2),
        scratch=(vmem(480, wide), vmem(480, wide), vmem(2, 3, ROWS, wide), vmem(3, ROWS, MODEL), dma(3)),
        flops=2_000_000_000,
    )
    return dq[None], dk[None], dv[None], weight_grad


def solution(mesh):
    rows = P("batch", "ctx", None)
    return jax.shard_map(
        local,
        mesh=mesh,
        in_specs=(rows, rows, rows, rows, P(), P()),
        out_specs=(rows, rows, rows, P("ctx", "batch")),
        check_vma=False,
    )
```

time: 74.2 us -> 64.9 us (0.87)
  waiting for transfers between devices: 12.8 us -> 4.77 us
  starting transfers between devices: 31.8 us -> 33.9 us
  blocking collectives: 9.12 us -> 7.14 us
  Pallas kernels: 18.4 us -> 17.1 us
    all_to_all x1, waiting for transfers between devices: 6.3 us -> 0.01 us  [local(): lax.all_to_all(row_parts.reshape(16, 16, 128), 'ctx', 0, 0, tiled=True, a...]
    all_to_all x1, waiting for transfers between devices: 4.99 us -> 1.93 us  [local(): lax.all_to_all(weight_parts, ('batch', 'ctx'), 0, 0, tiled=True, axis_ind...]
    all_to_all x1, starting transfers between devices: 4.19 us -> 6.66 us  [local(): lax.all_to_all(weight_parts, ('batch', 'ctx'), 0, 0, tiled=True, axis_ind...]
    all_gather x3 -> x2, blocking collectives: 9.12 us -> 7.14 us  [pair_gather(): lax.all_gather(block, 'ctx', axis=0, tiled=False, axis_index_groups=group...]
    pallas_call x7 -> x8, Pallas kernels: 18.4 us -> 17.1 us  [call(): pl.pallas_call(kernel, out_shape=out_shape, in_specs=[vmem] * near + [far...]
    ppermute x2, starting transfers between devices: 12 us -> 10.7 us  [swap(): lax.ppermute(block, 'ctx', [(index, index ^ 1 << bit) for index in range(...]
    all_to_all x1, starting transfers between devices: 12.2 us -> 13.2 us  [local(): lax.all_to_all(row_parts.reshape(16, 16, 128), 'ctx', 0, 0, tiled=True, a...]
  transfers between devices with their start and end apart: 5 -> 5, of which waited for: 4 -> 3; matrix products, arithmetic and copies ran while one was open for 0% -> 0% of each run, Pallas kernels for 13% -> 16%
where the time goes in v6:
time: 64.9 us; the launch traced here: 64.4 us
  starting transfers between devices  33.9 us (52%)
  Pallas kernels  17.1 us (26%)
  blocking collectives  7.14 us (11%)
  waiting for transfers between devices  4.77 us (7%)
  between operations  0.76 us (1%)
  other arithmetic  0.72 us (1%)
    pallas_call x8, Pallas kernels, call(): pl.pallas_call(kernel, out_shape=out_shape, in_specs=[vmem] * near + [far...  17.1 us
    all_to_all x1, starting transfers between devices, local(): lax.all_to_all(row_parts.reshape(16, 16, 128), 'ctx', 0, 0, tiled=True, a...  13.2 us
    ppermute x2, starting transfers between devices, swap(): lax.ppermute(block, 'ctx', [(index, index ^ 1 << bit) for index in range(...  10.7 us
    all_gather x2, blocking collectives, pair_gather(): lax.all_gather(block, 'ctx', axis=0, tiled=False, axis_index_groups=group...  7.14 us
    all_to_all x1, starting transfers between devices, local(): lax.all_to_all(weight_parts, ('batch', 'ctx'), 0, 0, tiled=True, axis_ind...  6.66 us
    all_to_all x1, starting transfers between devices, local(): lax.all_to_all(eight, 'ctx', 0, 0, tiled=True, axis_index_groups=groups_o...  3.35 us
    all_to_all x1, waiting for transfers between devices, local(): lax.all_to_all(weight_parts, ('batch', 'ctx'), 0, 0, tiled=True, axis_ind...  1.93 us
    ppermute x2, waiting for transfers between devices, swap(): lax.ppermute(block, 'ctx', [(index, index ^ 1 << bit) for index in range(...  1.79 us
  transfers between devices with their start and end apart: 5, of which 3 were waited for; matrix products, arithmetic and copies ran while one was open for 0% of the time, Pallas kernels for 16%

profile of v6, /device:TPU:1, one launch (start us, length us, event | category | flops | bytes accessed | tf_op | source)
XLA Modules:
  0.0 64.4 jit_solution(11969357059449535159)
XLA Ops:
  0.6 0.0 copy-start
  0.6 3.3 %shard_map.93 = (s32[16,128]{1,0:T(8,128)S(1)}, bf16[2,3,256,512]{3,2,1,0:T(8,128)(2,1)S(1)}, bf16[8,32,384]{2,1,0:T(8,128)(2,1)}) custom-call(s32[16]{0:T(128)} %off_hbm.1, bf16[256,768]{1,0:T(8,128)(2,1)} %bitcast.16, bf16[256,768]{1,0:T(8,128)(2,1)} %bitcast.17, bf16[256,768]{1,0:T(8,128)(2,1)} %bitcast.18, bf16[256,768]{1,0:T(8,128)(2,1)} %bitcast.11, ...), custom_call_target="tpu_custom_call" | custom-call | tf_op jit(solution)/shard_map/pallas_call | solution.py:399
  3.9 0.0 copy-done
  4.0 0.5 shard_map.94
  4.5 8.8 %collective-permute-start = (bf16[832,512]{1,0:T(8,128)(2,1)S(1)}, bf16[832,512]{1,0:T(8,128)(2,1)S(1)}, u32[]{:S(2)}, u32[]{:S(2)}) collective-permute-start(bf16[832,512]{1,0:T(8,128)(2,1)S(1)} %get-tuple-element.21), channel_id=1, source_target_pairs={{0,1},{1,0},{2,3},{3,2},{4,5},{5,4},{6,7},{7,6},{8,9},{9,8},{10,11... | collective-permute-start | bytes 2555912 | tf_op jit(solution)/shard_map/ppermute | solution.py:415
  13.3 3.4 %all-to-all-start = ((bf16[8,32,384]{2,1,0:T(8,128)(2,1)}), bf16[8,32,384]{2,1,0:T(8,128)(2,1)S(1)}, u32[]{:S(2)}, u32[]{:S(2)}) async-start(bf16[8,32,384]{2,1,0:T(8,128)(2,1)} %get-tuple-element.23), calls=%async_computation | async-start | bytes 393216 | tf_op jit(solution)/shard_map/all_to_all | solution.py:443
  16.6 0.0 collective-permute-done.other_ref
  16.7 1.9 %collective-permute-start.1 = (bf16[128,384]{1,0:T(8,128)(2,1)S(1)}, bf16[128,384]{1,0:T(8,128)(2,1)S(1)}, u32[]{:S(2)}, u32[]{:S(2)}) collective-permute-start(bf16[128,384]{1,0:T(8,128)(2,1)S(1)} %pad_maximum_fusion.two_ref), channel_id=1, source_target_pairs={{0,2},{1,3},{2,0},{3,1},{4,6},{5,7},{6,4},{7,5},{8,10},{9,11},{10,... | collective-permute-start | bytes 294920 | tf_op jit(solution)/shard_map/ppermute | solution.py:415
  18.6 2.0 %shard_map.95.old_ref = bf16[512,384]{1,0:T(8,128)(2,1)S(1)} custom-call(s32[16,128]{1,0:T(8,128)S(1)} %get-tuple-element.19.tile_ref, bf16[448,512]{1,0:T(8,128)(2,1)S(1)} %get-tuple-element.24.mine_ref, bf16[832,512]{1,0:T(8,128)(2,1)S(1)} %collective-permute-done.other_ref), custom_call_target="tpu_custom_call" | custom-call | flops 1000000 | tf_op jit(solution)/shard_map/pallas_call | solution.py:399
  20.6 1.0 %all-to-all-done.eight_ref = bf16[8,32,384]{2,1,0:T(8,128)(2,1)S(1)} async-done(((bf16[8,32,384]{2,1,0:T(8,128)(2,1)}), bf16[8,32,384]{2,1,0:T(8,128)(2,1)S(1)}, u32[]{:S(2)}, u32[]{:S(2)}) %all-to-all-start) | async-done | bytes 196640 | tf_op jit(solution)/shard_map/all_to_all | solution.py:443
  21.7 1.0 %shard_map.96.attended_ref = bf16[512,384]{1,0:T(8,128)(2,1)S(1)} custom-call(s32[16,128]{1,0:T(8,128)S(1)} %get-tuple-element.19.tile_ref, bf16[8,32,384]{2,1,0:T(8,128)(2,1)S(1)} %all-to-all-done.eight_ref, bf16[512,384]{1,0:T(8,128)(2,1)S(1)} %shard_map.95.old_ref), custom_call_target="tpu_custom_call" | custom-call | flops 1000000000 | tf_op jit(solution)/shard_map/pallas_call | solution.py:399
  22.6 1.8 %collective-permute-done.1.got_two_ref = bf16[128,384]{1,0:T(8,128)(2,1)S(1)} collective-permute-done((bf16[128,384]{1,0:T(8,128)(2,1)S(1)}, bf16[128,384]{1,0:T(8,128)(2,1)S(1)}, u32[]{:S(2)}, u32[]{:S(2)}) %collective-permute-start.1) | collective-permute-done | bytes 98336 | tf_op jit(solution)/shard_map/ppermute | solution.py:415
  24.4 2.3 %shard_map.97 = bf16[16,144,128]{2,1,0:T(8,128)(2,1)} custom-call(s32[16,128]{1,0:T(8,128)S(1)} %get-tuple-element.19.tile_ref, bf16[256,768]{1,0:T(8,128)(2,1)S(1)} %bitcast.13, bf16[832,512]{1,0:T(8,128)(2,1)S(1)} %collective-permute-done.other_ref, bf16[128,384]{1,0:T(8,128)(2,1)S(1)} %pad_maximum_fusion.two_ref, ...), custom_call_target="tpu_custom_call" | custom-call | flops 2000000000 | tf_op jit(solution)/shard_map/pallas_call | solution.py:399
  26.8 6.7 %all-to-all-start.1 = ((bf16[16,144,128]{2,1,0:T(8,128)(2,1)}), bf16[16,144,128]{2,1,0:T(8,128)(2,1)S(1)}, u32[]{:S(2)}, u32[]{:S(2)}) async-start(bf16[16,144,128]{2,1,0:T(8,128)(2,1)} %shard_map.97), calls=%async_computation.1 | async-start | bytes 1179648 | tf_op jit(solution)/shard_map/all_to_all | solution.py:463
  33.4 4.4 %shard_map.98 = (bf16[480,384]{1,0:T(8,128)(2,1)}, bf16[480,384]{1,0:T(8,128)(2,1)S(1)}) custom-call(bf16[448,512]{1,0:T(8,128)(2,1)S(1)} %get-tuple-element.24.mine_ref, bf16[832,512]{1,0:T(8,128)(2,1)S(1)} %collective-permute-done.other_ref, bf16[128,384]{1,0:T(8,128)(2,1)S(1)} %pad_maximum_fusion.two_ref, ...), custom_call_target="tpu_custom_call" | custom-call | flops 8000000000 | tf_op jit(solution)/shard_map/pallas_call | solution.py:399
  37.8 1.9 %all-to-all-done.1 = bf16[16,144,128]{2,1,0:T(8,128)(2,1)S(1)} async-done(((bf16[16,144,128]{2,1,0:T(8,128)(2,1)}), bf16[16,144,128]{2,1,0:T(8,128)(2,1)S(1)}, u32[]{:S(2)}, u32[]{:S(2)}) %all-to-all-start.1) | async-done | bytes 589856 | tf_op jit(solution)/shard_map/all_to_all | solution.py:463
  39.7 0.1 reduce_sum.21
  39.8 4.2 %all-gather = bf16[288,128]{1,0:T(8,128)(2,1)S(1)} all-gather(bf16[144,128]{1,0:T(8,128)(2,1)S(1)} %reduce_sum.21), channel_id=2, replica_groups={{0,1},{2,3},{4,5},{6,7},{8,9},{10,11},{12,13},{14,15},{16,17},{18,19},{..., dimensions={0}, use_global_device_ids=true | all-gather | bytes 110592 | tf_op jit(solution)/shard_map/all_gather | solution.py:411
  44.0 0.9 %shard_map.99 = bf16[256,128]{1,0:T(8,128)(2,1)} custom-call(bf16[2,144,128]{2,1,0:T(8,128)(2,1)S(1)} %bitcast.14), custom_call_target="tpu_custom_call" | custom-call | tf_op jit(solution)/shard_map/pallas_call | solution.py:399
  44.9 13.2 %all-to-all-start.2 = ((bf16[16,16,128]{2,1,0:T(8,128)(2,1)}), bf16[16,16,128]{2,1,0:T(8,128)(2,1)S(1)}, u32[]{:S(2)}, u32[]{:S(2)}) async-start(bf16[16,16,128]{2,1,0:T(8,128)(2,1)} %bitcast.9), calls=%async_computation.2 | async-start | bytes 131072 | tf_op jit(solution)/shard_map/all_to_all | solution.py:474
  58.1 3.0 %all-gather.1 = bf16[960,384]{1,0:T(8,128)(2,1)} all-gather(bf16[480,384]{1,0:T(8,128)(2,1)S(1)} %get-tuple-element.29), channel_id=3, replica_groups={{0,1},{2,3},{4,5},{6,7},{8,9},{10,11},{12,13},{14,15},{16,17},{18,19},{..., dimensions={0}, use_global_device_ids=true | all-gather | bytes 1105920 | tf_op jit(solution)/shard_map/all_gather | solution.py:411
  61.1 2.7 %shard_map.100 = (bf16[256,768]{1,0:T(8,128)(2,1)}, bf16[256,768]{1,0:T(8,128)(2,1)}, bf16[256,768]{1,0:T(8,128)(2,1)}) custom-call(s32[16,128]{1,0:T(8,128)S(1)} %get-tuple-element.19.tile_ref, bf16[480,384]{1,0:T(8,128)(2,1)} %get-tuple-element.26.keep_hbm, bf16[2,480,384]{2,1,0:T(8,128)(2,1)} %bitcast.15), custom_call_target="tpu_custom_call" | custom-call | flops 2000000000 | tf_op jit(solution)/shard_map/pallas_call | solution.py:399
  63.8 0.0 all-to-all-done.2
  63.8 0.6 convert_reduce_fusion
  (3 shorter events, 0.0 us)
Async XLA Ops:
  0.6 3.3 %copy-start = (bf16[1,256,768]{2,1,0:T(8,128)(2,1)S(1)}, bf16[1,256,768]{2,1,0:T(8,128)(2,1)}, u32[]{:S(2)}) copy-start(bf16[1,256,768]{2,1,0:T(8,128)(2,1)} %param.9) | copy-start | bytes 1179652
  4.5 12.2 %collective-permute-start = (bf16[832,512]{1,0:T(8,128)(2,1)S(1)}, bf16[832,512]{1,0:T(8,128)(2,1)S(1)}, u32[]{:S(2)}, u32[]{:S(2)}) collective-permute-start(bf16[832,512]{1,0:T(8,128)(2,1)S(1)} %get-tuple-element.21), channel_id=1, source_target_pairs={{0,1},{1,0},{2,3},{3,2},{4,5},{5,4},{6,7},{7,6},{8,9},{9,8},{10,11... | collective-permute-start | bytes 2555912 | tf_op jit(solution)/shard_map/ppermute | solution.py:415
  13.3 8.4 %all-to-all-start = ((bf16[8,32,384]{2,1,0:T(8,128)(2,1)}), bf16[8,32,384]{2,1,0:T(8,128)(2,1)S(1)}, u32[]{:S(2)}, u32[]{:S(2)}) async-start(bf16[8,32,384]{2,1,0:T(8,128)(2,1)} %get-tuple-element.23), calls=%async_computation | async-start | bytes 393216 | tf_op jit(solution)/shard_map/all_to_all | solution.py:443
  16.7 7.8 %collective-permute-start.1 = (bf16[128,384]{1,0:T(8,128)(2,1)S(1)}, bf16[128,384]{1,0:T(8,128)(2,1)S(1)}, u32[]{:S(2)}, u32[]{:S(2)}) collective-permute-start(bf16[128,384]{1,0:T(8,128)(2,1)S(1)} %pad_maximum_fusion.two_ref), channel_id=1, source_target_pairs={{0,2},{1,3},{2,0},{3,1},{4,6},{5,7},{6,4},{7,5},{8,10},{9,11},{10,... | collective-permute-start | bytes 294920 | tf_op jit(solution)/shard_map/ppermute | solution.py:415
  26.8 13.0 %all-to-all-start.1 = ((bf16[16,144,128]{2,1,0:T(8,128)(2,1)}), bf16[16,144,128]{2,1,0:T(8,128)(2,1)S(1)}, u32[]{:S(2)}, u32[]{:S(2)}) async-start(bf16[16,144,128]{2,1,0:T(8,128)(2,1)} %shard_map.97), calls=%async_computation.1 | async-start | bytes 1179648 | tf_op jit(solution)/shard_map/all_to_all | solution.py:463
  44.9 18.9 %all-to-all-start.2 = ((bf16[16,16,128]{2,1,0:T(8,128)(2,1)}), bf16[16,16,128]{2,1,0:T(8,128)(2,1)S(1)}, u32[]{:S(2)}, u32[]{:S(2)}) async-start(bf16[16,16,128]{2,1,0:T(8,128)(2,1)} %bitcast.9), calls=%async_computation.2 | async-start | bytes 131072 | tf_op jit(solution)/shard_map/all_to_all | solution.py:474

commit v7 on v6

--- a/solution.py
+++ b/solution.py
@@ -381,8 +381,16 @@
         tail_rows = jnp.concatenate([tail, pltpu.roll(tail.astype(F32), 64, 1).astype(BF)], axis=0)
         part = mm_nt(wide, sums[0:96]) + mm_nt(narrow, tail_rows)
         out = part if out is None else out + part
-    out_ref[:, 0:96] = out.astype(BF)
-    out_ref[:, 96:128] = jnp.zeros((256, 32), BF)
+    out = jnp.concatenate([out, jnp.zeros((256, 32), F32)], axis=1)
+    for chip in range(16):
+        rows = [out[16 * chip + 4 * third : 16 * chip + 4 * (third + 1)] for third in range(3)]
+        out_ref[chip] = jnp.concatenate(rows, axis=1).astype(BF)
+
+
+def total_kernel(parts_ref, out_ref):
+    total = jnp.sum(parts_ref[...].astype(F32), axis=0)
+    for third in range(3):
+        out_ref[4 * third : 4 * (third + 1), :] = total[:, LANES * third : LANES * third + PAIR_WIDTH]
 
 
 def call(kernel, out_shape, *operands, hbm=0, hbm_out=(), scratch=(), flops=0):
@@ -469,12 +477,12 @@
         flops=8_000_000_000,
     )
     column_sum = jnp.sum(column_parts.astype(F32), axis=0).astype(BF)
-    row_parts = call(split_kernel, bf(256, 128), pair_gather(column_sum))
+    row_parts = call(split_kernel, bf(16, 4, 384), pair_gather(column_sum))
     row_parts, send = lax.optimization_barrier((row_parts, send))
     row_parts = lax.all_to_all(
-        row_parts.reshape(16, 16, 128), "ctx", 0, 0, tiled=True, axis_index_groups=groups_over((1, 2, 3, 4), 64, FAR_FIRST)
-    )
-    weight_grad = jnp.sum(row_parts.astype(F32), axis=0)[:12, :96]
+        row_parts, "ctx", 0, 0, tiled=True, axis_index_groups=groups_over((1, 2, 3, 4), 64, FAR_FIRST)
+    )
+    weight_grad = call(total_kernel, jax.ShapeDtypeStruct((12, 96), F32), row_parts)
     dq, dk, dv = call(
         merge_kernel,
         (bf(ROWS, MODEL),) * 3,

time: 64.9 us -> 64.9 us (level)
    pallas_call x8 -> x9, Pallas kernels: 17.1 us -> 17.7 us  [call(): pl.pallas_call(kernel, out_shape=out_shape, in_specs=[vmem] * near + [far...]
where the time goes in v7:
time: 64.9 us; the launch traced here: 64.4 us
  starting transfers between devices  33.9 us (52%)
  Pallas kernels  17.7 us (27%)
  blocking collectives  7.14 us (11%)
  waiting for transfers between devices  4.75 us (7%)
  between operations  0.76 us (1%)
    pallas_call x9, Pallas kernels, call(): pl.pallas_call(kernel, out_shape=out_shape, in_specs=[vmem] * near + [far...  17.7 us
    all_to_all x1, starting transfers between devices, local(): lax.all_to_all(row_parts, 'ctx', 0, 0, tiled=True, axis_index_groups=grou...  13.2 us
    ppermute x2, starting transfers between devices, swap(): lax.ppermute(block, 'ctx', [(index, index ^ 1 << bit) for index in range(...  10.7 us
    all_gather x2, blocking collectives, pair_gather(): lax.all_gather(block, 'ctx', axis=0, tiled=False, axis_index_groups=group...  7.14 us
    all_to_all x1, starting transfers between devices, local(): lax.all_to_all(weight_parts, ('batch', 'ctx'), 0, 0, tiled=True, axis_ind...  6.66 us
    all_to_all x1, starting transfers between devices, local(): lax.all_to_all(eight, 'ctx', 0, 0, tiled=True, axis_index_groups=groups_o...  3.35 us
    all_to_all x1, waiting for transfers between devices, local(): lax.all_to_all(weight_parts, ('batch', 'ctx'), 0, 0, tiled=True, axis_ind...  1.91 us
    ppermute x2, waiting for transfers between devices, swap(): lax.ppermute(block, 'ctx', [(index, index ^ 1 << bit) for index in range(...  1.79 us
  transfers between devices with their start and end apart: 5, of which 3 were waited for; matrix products, arithmetic and copies ran while one was open for 0% of the time, Pallas kernels for 16%

profile of v7, /device:TPU:1, one launch (start us, length us, event | category | flops | bytes accessed | tf_op | source)
XLA Modules:
  0.0 64.4 jit_solution(7406625248409957179)
XLA Ops:
  0.6 0.0 copy-start
  0.6 3.3 %shard_map.93 = (s32[16,128]{1,0:T(8,128)S(1)}, bf16[2,3,256,512]{3,2,1,0:T(8,128)(2,1)S(1)}, bf16[8,32,384]{2,1,0:T(8,128)(2,1)}) custom-call(s32[16]{0:T(128)} %off_hbm.1, bf16[256,768]{1,0:T(8,128)(2,1)} %bitcast.14, bf16[256,768]{1,0:T(8,128)(2,1)} %bitcast.15, bf16[256,768]{1,0:T(8,128)(2,1)} %bitcast.16, bf16[256,768]{1,0:T(8,128)(2,1)} %bitcast.9, ...), custom_call_target="tpu_custom_call" | custom-call | tf_op jit(solution)/shard_map/pallas_call | solution.py:407
  3.9 0.0 copy-done
  4.0 0.5 shard_map.94
  4.5 8.8 %collective-permute-start = (bf16[832,512]{1,0:T(8,128)(2,1)S(1)}, bf16[832,512]{1,0:T(8,128)(2,1)S(1)}, u32[]{:S(2)}, u32[]{:S(2)}) collective-permute-start(bf16[832,512]{1,0:T(8,128)(2,1)S(1)} %get-tuple-element.21), channel_id=1, source_target_pairs={{0,1},{1,0},{2,3},{3,2},{4,5},{5,4},{6,7},{7,6},{8,9},{9,8},{10,11... | collective-permute-start | bytes 2555912 | tf_op jit(solution)/shard_map/ppermute | solution.py:423
  13.3 3.4 %all-to-all-start = ((bf16[8,32,384]{2,1,0:T(8,128)(2,1)}), bf16[8,32,384]{2,1,0:T(8,128)(2,1)S(1)}, u32[]{:S(2)}, u32[]{:S(2)}) async-start(bf16[8,32,384]{2,1,0:T(8,128)(2,1)} %get-tuple-element.23), calls=%async_computation | async-start | bytes 393216 | tf_op jit(solution)/shard_map/all_to_all | solution.py:451
  16.6 0.0 collective-permute-done.other_ref
  16.7 1.9 %collective-permute-start.1 = (bf16[128,384]{1,0:T(8,128)(2,1)S(1)}, bf16[128,384]{1,0:T(8,128)(2,1)S(1)}, u32[]{:S(2)}, u32[]{:S(2)}) collective-permute-start(bf16[128,384]{1,0:T(8,128)(2,1)S(1)} %pad_maximum_fusion.two_ref), channel_id=1, source_target_pairs={{0,2},{1,3},{2,0},{3,1},{4,6},{5,7},{6,4},{7,5},{8,10},{9,11},{10,... | collective-permute-start | bytes 294920 | tf_op jit(solution)/shard_map/ppermute | solution.py:423
  18.6 2.0 %shard_map.95.old_ref = bf16[512,384]{1,0:T(8,128)(2,1)S(1)} custom-call(s32[16,128]{1,0:T(8,128)S(1)} %get-tuple-element.19.tile_ref, bf16[448,512]{1,0:T(8,128)(2,1)S(1)} %get-tuple-element.24.mine_ref, bf16[832,512]{1,0:T(8,128)(2,1)S(1)} %collective-permute-done.other_ref), custom_call_target="tpu_custom_call" | custom-call | flops 1000000 | tf_op jit(solution)/shard_map/pallas_call | solution.py:407
  20.6 1.0 %all-to-all-done.eight_ref = bf16[8,32,384]{2,1,0:T(8,128)(2,1)S(1)} async-done(((bf16[8,32,384]{2,1,0:T(8,128)(2,1)}), bf16[8,32,384]{2,1,0:T(8,128)(2,1)S(1)}, u32[]{:S(2)}, u32[]{:S(2)}) %all-to-all-start) | async-done | bytes 196640 | tf_op jit(solution)/shard_map/all_to_all | solution.py:451
  21.7 1.0 %shard_map.96.attended_ref = bf16[512,384]{1,0:T(8,128)(2,1)S(1)} custom-call(s32[16,128]{1,0:T(8,128)S(1)} %get-tuple-element.19.tile_ref, bf16[8,32,384]{2,1,0:T(8,128)(2,1)S(1)} %all-to-all-done.eight_ref, bf16[512,384]{1,0:T(8,128)(2,1)S(1)} %shard_map.95.old_ref), custom_call_target="tpu_custom_call" | custom-call | flops 1000000000 | tf_op jit(solution)/shard_map/pallas_call | solution.py:407
  22.6 1.8 %collective-permute-done.1.got_two_ref = bf16[128,384]{1,0:T(8,128)(2,1)S(1)} collective-permute-done((bf16[128,384]{1,0:T(8,128)(2,1)S(1)}, bf16[128,384]{1,0:T(8,128)(2,1)S(1)}, u32[]{:S(2)}, u32[]{:S(2)}) %collective-permute-start.1) | collective-permute-done | bytes 98336 | tf_op jit(solution)/shard_map/ppermute | solution.py:423
  24.4 2.3 %shard_map.97 = bf16[16,144,128]{2,1,0:T(8,128)(2,1)} custom-call(s32[16,128]{1,0:T(8,128)S(1)} %get-tuple-element.19.tile_ref, bf16[256,768]{1,0:T(8,128)(2,1)S(1)} %bitcast.11, bf16[832,512]{1,0:T(8,128)(2,1)S(1)} %collective-permute-done.other_ref, bf16[128,384]{1,0:T(8,128)(2,1)S(1)} %pad_maximum_fusion.two_ref, ...), custom_call_target="tpu_custom_call" | custom-call | flops 2000000000 | tf_op jit(solution)/shard_map/pallas_call | solution.py:407
  26.8 6.7 %all-to-all-start.1 = ((bf16[16,144,128]{2,1,0:T(8,128)(2,1)}), bf16[16,144,128]{2,1,0:T(8,128)(2,1)S(1)}, u32[]{:S(2)}, u32[]{:S(2)}) async-start(bf16[16,144,128]{2,1,0:T(8,128)(2,1)} %shard_map.97), calls=%async_computation.1 | async-start | bytes 1179648 | tf_op jit(solution)/shard_map/all_to_all | solution.py:471
  33.4 4.4 %shard_map.98 = (bf16[480,384]{1,0:T(8,128)(2,1)}, bf16[480,384]{1,0:T(8,128)(2,1)S(1)}) custom-call(bf16[448,512]{1,0:T(8,128)(2,1)S(1)} %get-tuple-element.24.mine_ref, bf16[832,512]{1,0:T(8,128)(2,1)S(1)} %collective-permute-done.other_ref, bf16[128,384]{1,0:T(8,128)(2,1)S(1)} %pad_maximum_fusion.two_ref, ...), custom_call_target="tpu_custom_call" | custom-call | flops 8000000000 | tf_op jit(solution)/shard_map/pallas_call | solution.py:407
  37.8 1.9 %all-to-all-done.1 = bf16[16,144,128]{2,1,0:T(8,128)(2,1)S(1)} async-done(((bf16[16,144,128]{2,1,0:T(8,128)(2,1)}), bf16[16,144,128]{2,1,0:T(8,128)(2,1)S(1)}, u32[]{:S(2)}, u32[]{:S(2)}) %all-to-all-start.1) | async-done | bytes 589856 | tf_op jit(solution)/shard_map/all_to_all | solution.py:471
  39.7 0.1 reduce_sum.12
  39.8 4.2 %all-gather = bf16[288,128]{1,0:T(8,128)(2,1)S(1)} all-gather(bf16[144,128]{1,0:T(8,128)(2,1)S(1)} %reduce_sum.12), channel_id=2, replica_groups={{0,1},{2,3},{4,5},{6,7},{8,9},{10,11},{12,13},{14,15},{16,17},{18,19},{..., dimensions={0}, use_global_device_ids=true | all-gather | bytes 110592 | tf_op jit(solution)/shard_map/all_gather | solution.py:419
  44.0 0.9 %shard_map.99 = bf16[16,4,384]{2,1,0:T(4,128)(2,1)} custom-call(bf16[2,144,128]{2,1,0:T(8,128)(2,1)S(1)} %bitcast.12), custom_call_target="tpu_custom_call" | custom-call | tf_op jit(solution)/shard_map/pallas_call | solution.py:407
  44.9 13.2 %all-to-all-start.2 = ((bf16[16,4,384]{2,1,0:T(4,128)(2,1)}), bf16[16,4,384]{2,1,0:T(4,128)(2,1)S(1)}, u32[]{:S(2)}, u32[]{:S(2)}) async-start(bf16[16,4,384]{2,1,0:T(4,128)(2,1)} %shard_map.99), calls=%async_computation.2 | async-start | bytes 98304 | tf_op jit(solution)/shard_map/all_to_all | solution.py:482
  58.1 3.0 %all-gather.1 = bf16[960,384]{1,0:T(8,128)(2,1)} all-gather(bf16[480,384]{1,0:T(8,128)(2,1)S(1)} %get-tuple-element.29), channel_id=3, replica_groups={{0,1},{2,3},{4,5},{6,7},{8,9},{10,11},{12,13},{14,15},{16,17},{18,19},{..., dimensions={0}, use_global_device_ids=true | all-gather | bytes 1105920 | tf_op jit(solution)/shard_map/all_gather | solution.py:419
  61.1 2.7 %shard_map.100 = (bf16[256,768]{1,0:T(8,128)(2,1)}, bf16[256,768]{1,0:T(8,128)(2,1)}, bf16[256,768]{1,0:T(8,128)(2,1)}) custom-call(s32[16,128]{1,0:T(8,128)S(1)} %get-tuple-element.19.tile_ref, bf16[480,384]{1,0:T(8,128)(2,1)} %get-tuple-element.26.keep_hbm, bf16[2,480,384]{2,1,0:T(8,128)(2,1)} %bitcast.13), custom_call_target="tpu_custom_call" | custom-call | flops 2000000000 | tf_op jit(solution)/shard_map/pallas_call | solution.py:407
  63.8 0.0 all-to-all-done.2.parts_ref
  63.8 0.6 shard_map.101
  (3 shorter events, 0.0 us)
Async XLA Ops:
  0.6 3.3 %copy-start = (bf16[1,256,768]{2,1,0:T(8,128)(2,1)S(1)}, bf16[1,256,768]{2,1,0:T(8,128)(2,1)}, u32[]{:S(2)}) copy-start(bf16[1,256,768]{2,1,0:T(8,128)(2,1)} %param.9) | copy-start | bytes 1179652
  4.5 12.2 %collective-permute-start = (bf16[832,512]{1,0:T(8,128)(2,1)S(1)}, bf16[832,512]{1,0:T(8,128)(2,1)S(1)}, u32[]{:S(2)}, u32[]{:S(2)}) collective-permute-start(bf16[832,512]{1,0:T(8,128)(2,1)S(1)} %get-tuple-element.21), channel_id=1, source_target_pairs={{0,1},{1,0},{2,3},{3,2},{4,5},{5,4},{6,7},{7,6},{8,9},{9,8},{10,11... | collective-permute-start | bytes 2555912 | tf_op jit(solution)/shard_map/ppermute | solution.py:423
  13.3 8.4 %all-to-all-start = ((bf16[8,32,384]{2,1,0:T(8,128)(2,1)}), bf16[8,32,384]{2,1,0:T(8,128)(2,1)S(1)}, u32[]{:S(2)}, u32[]{:S(2)}) async-start(bf16[8,32,384]{2,1,0:T(8,128)(2,1)} %get-tuple-element.23), calls=%async_computation | async-start | bytes 393216 | tf_op jit(solution)/shard_map/all_to_all | solution.py:451
  16.7 7.8 %collective-permute-start.1 = (bf16[128,384]{1,0:T(8,128)(2,1)S(1)}, bf16[128,384]{1,0:T(8,128)(2,1)S(1)}, u32[]{:S(2)}, u32[]{:S(2)}) collective-permute-start(bf16[128,384]{1,0:T(8,128)(2,1)S(1)} %pad_maximum_fusion.two_ref), channel_id=1, source_target_pairs={{0,2},{1,3},{2,0},{3,1},{4,6},{5,7},{6,4},{7,5},{8,10},{9,11},{10,... | collective-permute-start | bytes 294920 | tf_op jit(solution)/shard_map/ppermute | solution.py:423
  26.8 13.0 %all-to-all-start.1 = ((bf16[16,144,128]{2,1,0:T(8,128)(2,1)}), bf16[16,144,128]{2,1,0:T(8,128)(2,1)S(1)}, u32[]{:S(2)}, u32[]{:S(2)}) async-start(bf16[16,144,128]{2,1,0:T(8,128)(2,1)} %shard_map.97), calls=%async_computation.1 | async-start | bytes 1179648 | tf_op jit(solution)/shard_map/all_to_all | solution.py:471
  44.9 18.9 %all-to-all-start.2 = ((bf16[16,4,384]{2,1,0:T(4,128)(2,1)}), bf16[16,4,384]{2,1,0:T(4,128)(2,1)S(1)}, u32[]{:S(2)}, u32[]{:S(2)}) async-start(bf16[16,4,384]{2,1,0:T(4,128)(2,1)} %shard_map.99), calls=%async_computation.2 | async-start | bytes 98304 | tf_op jit(solution)/shard_map/all_to_all | solution.py:482
